TPU v7x, 128 devices: a whole 4x4x4 slice. The times are simulated.
128 devices in a mesh: ctx: 32 (over x, y_lo, z), tp: 4 (over y_hi, core).
Axes of the slice: x: 4, y: 4 (y_hi: 2, y_lo: 2; y = y_hi * 2 + y_lo), z: 4, core: 2. Of those that a mesh axis runs over, the one named last changes fastest.
Arguments:
- mixer_input: bfloat16 [8192, 4096], P('ctx', 'tp'), may hold values from -6 to 6
- gate_in: bfloat16 [8192, 4096], P('ctx', 'tp'), may hold values from -6 to 6
- gate_out: bfloat16 [8192, 4096], P('ctx', 'tp'), may hold values from -18 to 18
- residue: float32 [4096, 16], P('tp'), may hold values from -26 to 26
- decay_rate: float32 [4096, 16], P('tp'), may hold values from 3.0517578e-05 to 0.04
- norm_gain: float32 [4096], P('tp'), may hold values from 0.1 to 1.9
- queries: bfloat16 [8192, 4096], P('ctx', 'tp'), may hold values from -10 to 10
- key_vectors: bfloat16 [8192, 4096], P('ctx', 'tp'), may hold values from -10 to 10
- grad_out: bfloat16 [8192, 4096], P('ctx', 'tp'), may hold values from -6 to 6
Outputs:
- attended: bfloat16 [8192, 4096], P('ctx', 'tp')
- grad_queries: bfloat16 [8192, 4096], P('ctx', 'tp')
- grad_keys: bfloat16 [8192, 4096], P('ctx', 'tp')
- grad_input: bfloat16 [8192, 4096], P('ctx', 'tp')
All inputs are finite; a program needn't handle non-finite values.
Results may differ from a plain program's by a relative error of at most 0.025.
Values may be sent and summed in bfloat16 or wider, within the bound.
No kernel may reach another device: no remote copies, remote signals or barrier semaphores. Data moves between devices by JAX's collectives and lax.ppermute only.
A program may use at most 192 MiB of HBM per device.

v0:
```python
from functools import reduce
import math

import jax
import jax.numpy as jnp
from jax import lax
from jax.sharding import PartitionSpec as P

HEAD_DIM = 128
SPAN = 2


EPS = 1e-06
precise = lax.Precision.HIGHEST


def passed_along(value, axis, by):
    devices = lax.axis_size(axis)
    pairs = [(i, i + by) for i in range(devices) if 0 <= i + by < devices]
    return lax.ppermute(value, axis, pairs)


def passed_along_2(block, axis, distance):
    devices = range(lax.axis_size(axis))
    route = [((i - distance) % len(devices), i) for i in devices]
    return lax.ppermute(block, axis, route)


def split_heads(rows):
    return rows.reshape(rows.shape[0], rows.shape[1] // HEAD_DIM, HEAD_DIM)


def channel_total(row_values):
    return lax.psum(row_values, "tp")


def pass_keys(current):
    return passed_along((current[0], current[1]), "ctx", 1)


def modal_tables(decay_rate, residue, window):
    lags = jnp.arange(window, dtype=jnp.float32)
    powers = jnp.exp(-decay_rate[None, :, :] * lags[:, None, None])
    taps = jnp.sum(residue[None, :, :] * powers, axis=2)
    places = jnp.arange(window, dtype=jnp.int32)
    select = (places[:, None, None] - places[None, :, None] == places[None, None, :]).astype(
        jnp.float32
    )
    toeplitz = jnp.einsum("tsk,kc->tsc", select, taps, precision=precise)
    leading = residue[None, :, :] * powers * jnp.exp(-decay_rate)[None, :, :]
    return (toeplitz, powers[::-1], leading)


def carry_in(last_state, decay_rate, length, reverse):
    position = lax.axis_index("ctx")
    piece = lax.all_gather(last_state[None], "ctx", axis=0, tiled=True)
    sources = jnp.arange(piece.shape[0], dtype=jnp.int32)
    if reverse:
        distance = sources - position - 1
    else:
        distance = position - 1 - sources
    factor = jnp.exp(
        -decay_rate[None, :, :]
        * (length * jnp.maximum(distance, 0)).astype(jnp.float32)[:, None, None]
    )
    factor = jnp.where((distance >= 0)[:, None, None], factor, 0.0)
    return jnp.sum(factor * piece, axis=0)


def modal_mix(drive, decay_rate, residue, reverse):
    if reverse:
        drive = drive[::-1]
    length, width = drive.shape
    window = math.gcd(length, 32)
    count = length // window
    toeplitz, trailing, leading = modal_tables(decay_rate, residue, window)
    pieces = drive.reshape(count, window, width)
    inner = jnp.einsum("tsc,bsc->btc", toeplitz, pieces, precision=precise)
    finals = jnp.einsum("bsc,scm->bcm", pieces, trailing, precision=precise)
    stride = jnp.exp(-decay_rate * window)

    def advance(state, final):
        return (stride * state + final, state)

    last_state, before = lax.scan(advance, jnp.zeros_like(decay_rate), finals)
    incoming = carry_in(last_state, decay_rate, length, reverse)
    offsets = window * jnp.arange(count, dtype=jnp.float32)
    states = (
        before + jnp.exp(-decay_rate[None, :, :] * offsets[:, None, None]) * incoming[None, :, :]
    )
    outer = jnp.einsum("tcm,bcm->btc", leading, states, precision=precise)
    mixed = (inner + outer).reshape(length, width)
    if reverse:
        mixed = mixed[::-1]
    return mixed


def block_mask(query_block, key_block, rows, blocks):
    places = jnp.arange(rows, dtype=jnp.int32)
    query_place = query_block * rows + places
    key_place = key_block * rows + places
    valid = (key_block >= 0) & (query_block < blocks) & (query_block - key_block <= SPAN)
    return (key_place[None, :] <= query_place[:, None]) & valid


def block_grads(query_rows, cotangent_rows, log_rows, delta_rows, key_rows, value_rows, allowed):
    scale = 1.0 / math.sqrt(HEAD_DIM)
    query_heads = split_heads(query_rows)
    cotangent_heads = split_heads(cotangent_rows)
    key_heads = split_heads(key_rows)
    value_heads = split_heads(value_rows)
    scores = (
        jnp.einsum("thd,shd->hts", query_heads, key_heads, preferred_element_type=jnp.float32)
        * scale
    )
    probs = jnp.where(allowed[None], jnp.exp(scores - log_rows[:, :, None]), 0.0)
    grad_value_rows = jnp.einsum(
        "hts,thd->shd",
        probs.astype(jnp.bfloat16),
        cotangent_heads,
        preferred_element_type=jnp.float32,
    )
    dprob = jnp.einsum(
        "thd,shd->hts", cotangent_heads, value_heads, preferred_element_type=jnp.float32
    )
    dscore = (probs * (dprob - delta_rows[:, :, None])).astype(jnp.bfloat16)
    grad_query_rows = (
        jnp.einsum("hts,shd->thd", dscore, key_heads, preferred_element_type=jnp.float32) * scale
    )
    grad_key_rows = (
        jnp.einsum("hts,thd->shd", dscore, query_heads, preferred_element_type=jnp.float32) * scale
    )
    rows = query_rows.shape[0]
    return (
        grad_query_rows.reshape(rows, -1),
        grad_key_rows.reshape(rows, -1),
        grad_value_rows.reshape(rows, -1),
    )


def shards(
    mixer_input, gate_in, gate_out, residue, decay_rate, norm_gain, queries, key_vectors, grad_out
):
    length, width = queries.shape
    scale = 1.0 / math.sqrt(HEAD_DIM)
    full_width = width * lax.axis_size("tp")
    position = lax.axis_index("ctx")
    blocks = lax.axis_size("ctx")
    drive = gate_in.astype(jnp.float32) * mixer_input.astype(jnp.float32)
    gate = gate_out.astype(jnp.float32)
    mixed = gate * modal_mix(drive, decay_rate, residue, False)
    inverse = lax.rsqrt(channel_total(jnp.sum(mixed * mixed, axis=1)) / full_width + EPS)
    values = (mixed * inverse[:, None] * norm_gain[None, :]).astype(jnp.bfloat16)
    query_heads = split_heads(queries)
    current = (key_vectors, values)
    received = []
    score_list = []
    value_list = []
    for offset in range(SPAN + 1):
        if offset > 0:
            current = pass_keys(current)
            received.append(current)
        scores = (
            jnp.einsum(
                "thd,shd->hts",
                query_heads,
                split_heads(current[0]),
                preferred_element_type=jnp.float32,
            )
            * scale
        )
        allowed = block_mask(position, position - offset, length, blocks)
        score_list.append(jnp.where(allowed[None], scores, -jnp.inf))
        value_list.append(current[1])
    highest = reduce(jnp.maximum, [jnp.max(block_scores, axis=2) for block_scores in score_list])
    expos = [jnp.exp(block_scores - highest[:, :, None]) for block_scores in score_list]
    total = reduce(jnp.add, [jnp.sum(expo, axis=2) for expo in expos])
    output = reduce(
        jnp.add,
        [
            jnp.einsum(
                "hts,shd->thd",
                (expo / total[:, :, None]).astype(jnp.bfloat16),
                split_heads(value_block),
                preferred_element_type=jnp.float32,
            )
            for expo, value_block in zip(expos, value_list)
        ],
    )
    attended = output.reshape(length, width).astype(jnp.bfloat16)
    log_total = highest + jnp.log(total)
    delta = jnp.transpose(
        jnp.sum(
            split_heads(grad_out).astype(jnp.float32) * split_heads(attended).astype(jnp.float32),
            axis=2,
        )
    )
    own = block_grads(
        queries,
        grad_out,
        log_total,
        delta,
        key_vectors,
        values,
        block_mask(position, position, length, blocks),
    )
    grad_query, key_sum, value_sum = own
    current = (key_vectors, values)
    for offset in range(1, SPAN + 1):
        current = pass_keys(current)
        key_sum, value_sum = (
            passed_along_2(key_sum.astype(jnp.bfloat16), "ctx", 1).astype(key_sum.dtype),
            passed_along_2(value_sum.astype(jnp.bfloat16), "ctx", 1).astype(value_sum.dtype),
        )
        part = block_grads(
            queries,
            grad_out,
            log_total,
            delta,
            current[0],
            current[1],
            block_mask(position, position - offset, length, blocks),
        )
        grad_query = grad_query + part[0]
        key_sum = key_sum + part[1]
        value_sum = value_sum + part[2]
    key_sum, value_sum = (
        passed_along_2(key_sum.astype(jnp.bfloat16), "ctx", -SPAN).astype(key_sum.dtype),
        passed_along_2(value_sum.astype(jnp.bfloat16), "ctx", -SPAN).astype(value_sum.dtype),
    )
    grad_queries = grad_query.astype(jnp.bfloat16)
    grad_keys = key_sum.astype(jnp.bfloat16)
    scaled = norm_gain[None, :] * value_sum
    inner_dot = channel_total(jnp.sum(scaled * mixed, axis=1))
    grad_mixed = inverse[:, None] * scaled - mixed * (inverse**3 * inner_dot / full_width)[:, None]
    grad_drive = modal_mix(gate * grad_mixed, decay_rate, residue, True)
    grad_input = (gate_in.astype(jnp.float32) * grad_drive).astype(jnp.bfloat16)
    return (attended, grad_queries, grad_keys, grad_input)


def solution(mesh):
    in_specs = (
        P("ctx", "tp"),
        P("ctx", "tp"),
        P("ctx", "tp"),
        P("tp", None),
        P("tp", None),
        P("tp"),
        P("ctx", "tp"),
        P("ctx", "tp"),
        P("ctx", "tp"),
    )
    out_specs = (P("ctx", "tp"), P("ctx", "tp"), P("ctx", "tp"), P("ctx", "tp"))
    return jax.shard_map(shards, mesh=mesh, in_specs=in_specs, out_specs=out_specs, check_vma=False)
```

profile of v0, /device:TPU:0, one launch (start us, length us, event | category | flops | bytes accessed | tf_op | source)
XLA Modules:
  0.0 665.0 jit_solution(14674883021272661408)
XLA Ops:
  8.5 3.9 collective-permute-start
  16.8 6.1 multiply_exponential_fusion
  22.9 13.2 %rev.10 = f32[32,1024,16]{0,2,1:T(8,128)} reverse(f32[32,1024,16]{0,2,1:T(8,128)} %multiply_exponential_fusion), dimensions={0} | reverse | bytes 4194304 | tf_op jit(solution)/shard_map/rev | solution.py:51
  36.1 17.6 %convolution_bitcast_fusion.1 = f32[8,1024,16]{2,0,1:T(8,128)} fusion(f32[32,1024,16]{0,2,1:T(8,128)} %rev.10, f32[8,32,1024]{1,0,2:T(8,128)} %copy.131), kind=kOutput, calls=%fused_computation.23 | convolution fusion | flops 50331648 | bytes 3670016 | tf_op jit(solution)/shard_map/bsc,scm->bcm/dot_general | solution.py:79
  63.3 4.0 collective-permute-start.1
  68.5 11.6 %collective-permute-done.1 = bf16[256,1024]{0,1:T(8,128)(2,1)S(1)} collective-permute-done((bf16[256,1024]{0,1:T(8,128)(2,1)S(1)}, bf16[256,1024]{0,1:T(8,128)(2,1)S(1)}, u32[]{:S(2)}, u32[]{:S(2)}) %collective-permute-start.1) | collective-permute-done | bytes 524320 | tf_op jit(solution)/shard_map/ppermute | solution.py:20
  95.7 10.2 %collective-permute-done.7 = bf16[256,1024]{1,0:T(8,128)(2,1)} collective-permute-done((bf16[256,1024]{1,0:T(8,128)(2,1)}, bf16[256,1024]{1,0:T(8,128)(2,1)}, u32[]{:S(2)}, u32[]{:S(2)}) %collective-permute-start.7) | collective-permute-done | bytes 524320 | tf_op jit(solution)/shard_map/ppermute | solution.py:26
  113.6 13.0 %collective-permute-done.8 = bf16[256,1024]{1,0:T(8,128)(2,1)} collective-permute-done((bf16[256,1024]{1,0:T(8,128)(2,1)}, bf16[256,1024]{1,0:T(8,128)(2,1)}, u32[]{:S(2)}, u32[]{:S(2)}) %collective-permute-start.8) | collective-permute-done | bytes 524320 | tf_op jit(solution)/shard_map/ppermute | solution.py:26
  128.9 85.4 %all-gather.5.cloned.1.call-done = f32[32768,16]{0,1:T(8,128)} async-done(((f32[1024,16]{0,1:T(8,128)}), f32[32768,16]{0,1:T(8,128)}) %all-gather.5.cloned.1.call-update) | async-done | bytes 2097168 | tf_op jit(solution)/shard_map/all_gather | solution.py:56
  214.3 4.1 copy.213
  218.5 7.9 %copy.135 = f32[32,1024,16]{0,2,1:T(8,128)} copy(f32[32,1024,16]{1,0,2:T(8,128)} %bitcast.150) | data formatting | bytes 4194304 | tf_op jit(solution)/shard_map/all_gather | solution.py:56
  226.4 35.1 %multiply_reduce_fusion.1 = (f32[1024,16]{1,0:T(8,128)}, f32[32,1024]{0,1:T(8,128)S(1)}) fusion(f32[32,1024,16]{0,2,1:T(8,128)} %copy.135, f32[32]{0:T(128)} %multiply_convert_fusion.2, f32[1024,16]{1,0:T(8,128)S(1)} %copy.129, pred[32]{0:T(512)(128)(4,1)} %fusion.63, f32[1024,16]{1,0:T(8,128)} %copy.128), kind=kLoop, calls=%fused_computation.5 | loop fusion | flops 3620864 | bytes 2424992 | tf_op jit(solution)/shard_map/reduce_sum | solution.py:67
  261.5 3.8 fusion.56
  265.3 14.3 %copy.132 = f32[32,32,1024]{1,0,2:T(8,128)} copy(f32[32,32,1024]{2,1,0:T(8,128)} %fusion.56) | data formatting | bytes 8388608 | tf_op jit(solution)/shard_map/tsk,kc->tsc/dot_general | solution.py:49
  279.6 29.9 %fusion.77 = f32[1024,8,32]{2,1,0:T(8,128)} fusion(f32[8,32,1024]{1,0,2:T(8,128)} %copy.131, f32[32,32,1024]{1,0,2:T(8,128)} %copy.132), kind=kOutput, calls=%fused_computation.141 | convolution fusion | flops 100663296 | bytes 6291456 | tf_op jit(solution)/shard_map/tsc,bsc->btc/dot_general | solution.py:78
  317.0 16.4 %add_bitcast_fusion.1 = f32[8,32,1024]{1,0,2:T(8,128)} fusion(f32[1024,8,32]{2,1,0:T(8,128)} %fusion.77, f32[8,1024,16]{2,0,1:T(8,128)} %copy.138, f32[1024,16]{1,0:T(8,128)} %copy.137, f32[1024,16]{1,0:T(8,128)S(1)} %copy.129, f32[1024,16]{1,0:T(8,128)} %copy.128), kind=kOutput, calls=%fused_computation.15 | convolution fusion | flops 52166656 | bytes 2818048 | tf_op jit(solution)/shard_map/tcm,bcm->btc/dot_general | solution.py:91
  333.4 3.6 copy.139
  339.5 7.8 %all-reduce = (f32[256]{0:T(256)}, f32[256]{0:T(256)}) all-reduce(f32[256]{0:T(256)} %get-tuple-element.143, f32[256]{0:T(256)} %get-tuple-element.142), channel_id=1, replica_groups=mesh['ctx'=32,'tp'=4] {'tp'}, use_global_device_ids=true, to_apply=%region_5.6 | all-reduce | flops 512 | bytes 4096 | tf_op jit(solution)/shard_map/psum | solution.py:34
  351.2 4.2 collective-permute-start.2
  355.4 8.9 %rev.11 = f32[256,1024]{1,0:T(8,128)} reverse(f32[256,1024]{1,0:T(8,128)} %get-tuple-element.173), dimensions={0} | reverse | bytes 2097152 | tf_op jit(solution)/shard_map/rev | solution.py:72
  364.4 3.7 copy.179
  368.0 17.6 %convolution_bitcast_fusion = f32[8,1024,16]{2,0,1:T(8,128)} fusion(f32[32,1024,16]{0,2,1:T(8,128)} %rev.10, f32[8,32,1024]{1,0,2:T(8,128)} %copy.179), kind=kOutput, calls=%fused_computation.22 | convolution fusion | flops 50331648 | bytes 3670016 | tf_op jit(solution)/shard_map/bsc,scm->bcm/dot_general | solution.py:79
  390.1 12.2 %while.27 = (s32[]{:T(128)}, f32[1024,16]{0,1:T(8,128)S(1)}, f32[8,1024,16]{1,2,0:T(8,128)}, f32[1024,16]{0,1:T(8,128)S(1)}, f32[8,1024,16]{1,2,0:T(8,128)}, /*index=5*/s32[]{:T(128)}, s32[]{:T(128)}) while((s32[]{:T(128)}, f32[1024,16]{0,1:T(8,128)S(1)}, f32[8,1024,16]{1,2,0:T(8,128)}, f32[1024,16]{0,1:T(8,128)S(1)}, ...), condition=%wide.region_16.17_spmd.clone, body=%wide.region_15.16_spmd.clone.sunk | while | flops 65539 | bytes 393320 | solution.py:85
  402.3 30.3 %fusion.78 = f32[1024,8,32]{2,1,0:T(8,128)} fusion(f32[8,32,1024]{1,0,2:T(8,128)} %copy.179, f32[32,32,1024]{1,0,2:T(8,128)} %copy.132), kind=kOutput, calls=%fused_computation.142 | convolution fusion | flops 100663296 | bytes 6291456 | tf_op jit(solution)/shard_map/tsc,bsc->btc/dot_general | solution.py:78
  439.5 3.7 convolution_add_fusion.3
  471.8 7.6 %collective-permute-done.4 = bf16[256,1024]{1,0:T(8,128)(2,1)} collective-permute-done((bf16[256,1024]{1,0:T(8,128)(2,1)}, bf16[256,1024]{1,0:T(8,128)(2,1)}, u32[]{:S(2)}, u32[]{:S(2)}) %collective-permute-start.4) | collective-permute-done | bytes 524320 | tf_op jit(solution)/shard_map/ppermute | solution.py:26
  485.2 15.2 %collective-permute-done.5 = bf16[256,1024]{1,0:T(8,128)(2,1)} collective-permute-done((bf16[256,1024]{1,0:T(8,128)(2,1)}, bf16[256,1024]{1,0:T(8,128)(2,1)}, u32[]{:S(2)}, u32[]{:S(2)}) %collective-permute-start.5) | collective-permute-done | bytes 524320 | tf_op jit(solution)/shard_map/ppermute | solution.py:26
  505.1 12.8 %collective-permute-done.6 = bf16[256,1024]{1,0:T(8,128)(2,1)S(1)} collective-permute-done((bf16[256,1024]{1,0:T(8,128)(2,1)}, bf16[256,1024]{1,0:T(8,128)(2,1)S(1)}, u32[]{:S(2)}, u32[]{:S(2)}) %collective-permute-start.6) | collective-permute-done | bytes 524320 | tf_op jit(solution)/shard_map/ppermute | solution.py:26
  517.9 76.3 %all-gather.7.cloned.1.call-done = f32[32768,16]{0,1:T(8,128)} async-done(((f32[1024,16]{0,1:T(8,128)}), f32[32768,16]{0,1:T(8,128)}) %all-gather.7.cloned.1.call-update) | async-done | bytes 2097168 | tf_op jit(solution)/shard_map/all_gather | solution.py:56
  597.1 6.3 copy.183
  603.4 29.7 %multiply_reduce_fusion = f32[1024,16]{1,0:T(8,128)S(1)} fusion(f32[32,1024,16]{0,2,1:T(8,128)} %copy.183, f32[32]{0:T(128)S(1)} %copy-done.33, f32[1024,16]{1,0:T(8,128)S(1)} %copy.129, pred[32]{0:T(512)(128)(4,1)S(1)} %copy-done.34), kind=kLoop, calls=%fused_computation.4 | loop fusion | flops 2080768 | bytes 2228384 | tf_op jit(solution)/shard_map/reduce_sum | solution.py:67
  636.1 16.0 %add_bitcast_fusion = f32[8,32,1024]{1,0,2:T(8,128)} fusion(f32[1024,8,32]{2,1,0:T(8,128)} %fusion.78, f32[8,1024,16]{2,0,1:T(8,128)} %copy.185, f32[1024,16]{1,0:T(8,128)S(1)} %copy-done.24, f32[1024,16]{1,0:T(8,128)S(1)} %copy.129, f32[1024,16]{1,0:T(8,128)S(1)} %copy-done.23), kind=kOutput, calls=%fused_computation.14 | convolution fusion | flops 52166656 | bytes 2818048 | tf_op jit(solution)/shard_map/tcm,bcm->btc/dot_general | solution.py:91
  (190 shorter events, 129.6 us)
Async XLA Ops:
  7.2 207.2 %all-gather.5.cloned.1.call-start = ((), (), s32[]{:S(2)}) async-start(), calls=%async_computation | async-start | bytes 2162688 | tf_op jit(solution)/shard_map/all_gather | solution.py:56
  8.5 58.9 %copy-start.5 = (bf16[256,1024]{0,1:T(8,128)(2,1)}, bf16[256,1024]{0,1:T(8,128)(2,1)S(1)}, u32[]{:S(2)}) copy-start(bf16[256,1024]{0,1:T(8,128)(2,1)S(1)} %copy.211) | copy-start | bytes 1572868
  8.5 54.8 %collective-permute-start = (bf16[256,1024]{0,1:T(8,128)(2,1)S(1)}, bf16[256,1024]{0,1:T(8,128)(2,1)S(1)}, u32[]{:S(2)}, u32[]{:S(2)}) collective-permute-start(bf16[256,1024]{0,1:T(8,128)(2,1)S(1)} %copy.211), channel_id=1, source_target_pairs={{0,4},{4,8},{8,12},{12,16},{16,20},{20,24},{24,28},{28,32},{32,36}... | collective-permute-start | bytes 1572872 | tf_op jit(solution)/shard_map/ppermute | solution.py:20
  56.5 4.6 copy-start.29
  57.7 536.6 %all-gather.7.cloned.1.call-start = ((), (), s32[]{:S(2)}) async-start(), calls=%async_computation.1 | async-start | bytes 2162688 | tf_op jit(solution)/shard_map/all_gather | solution.py:56
  63.3 5.1 copy-start.16
  63.3 16.7 %collective-permute-start.1 = (bf16[256,1024]{0,1:T(8,128)(2,1)S(1)}, bf16[256,1024]{0,1:T(8,128)(2,1)S(1)}, u32[]{:S(2)}, u32[]{:S(2)}) collective-permute-start(bf16[256,1024]{0,1:T(8,128)(2,1)S(1)} %collective-permute-done), channel_id=1, source_target_pairs={{0,4},{4,8},{8,12},{12,16},{16,20},{20,24},{24,28},{28,32},{32,36}... | collective-permute-start | bytes 1572872 | tf_op jit(solution)/shard_map/ppermute | solution.py:20
  67.9 14.9 %copy-start.1 = (f32[8,256,256]{1,2,0:T(8,128)}, f32[8,256,256]{1,2,0:T(8,128)S(1)}, u32[]{:S(2)}) copy-start(f32[8,256,256]{1,2,0:T(8,128)S(1)} %get-tuple-element.186) | copy-start | bytes 6291460
  68.5 13.7 %copy-start = (f32[8,256,256]{1,2,0:T(8,128)}, f32[8,256,256]{1,2,0:T(8,128)S(1)}, u32[]{:S(2)}) copy-start(f32[8,256,256]{1,2,0:T(8,128)S(1)} %get-tuple-element.188) | copy-start | bytes 6291460
  86.2 19.8 %collective-permute-start.7 = (bf16[256,1024]{1,0:T(8,128)(2,1)}, bf16[256,1024]{1,0:T(8,128)(2,1)}, u32[]{:S(2)}, u32[]{:S(2)}) collective-permute-start(bf16[256,1024]{1,0:T(8,128)(2,1)} %copy.174), channel_id=1, source_target_pairs={{124,0},{0,4},{4,8},{8,12},{12,16},{16,20},{20,24},{24,28},{28,32}... | collective-permute-start | bytes 1572872 | tf_op jit(solution)/shard_map/ppermute | solution.py:26
  95.7 13.7 %copy-start.8 = (bf16[256,1024]{0,1:T(8,128)(2,1)S(1)}, bf16[256,1024]{0,1:T(8,128)(2,1)}, u32[]{:S(2)}) copy-start(bf16[256,1024]{0,1:T(8,128)(2,1)} %copy.153) | copy-start | bytes 1572868
  108.3 18.4 %collective-permute-start.8 = (bf16[256,1024]{1,0:T(8,128)(2,1)}, bf16[256,1024]{1,0:T(8,128)(2,1)}, u32[]{:S(2)}, u32[]{:S(2)}) collective-permute-start(bf16[256,1024]{1,0:T(8,128)(2,1)} %add_convert_fusion.1), channel_id=1, source_target_pairs={{124,0},{0,4},{4,8},{8,12},{12,16},{16,20},{20,24},{24,28},{28,32}... | collective-permute-start | bytes 1572872 | tf_op jit(solution)/shard_map/ppermute | solution.py:26
  128.9 208.1 %collective-permute-start.9 = (bf16[256,1024]{1,0:T(8,128)(2,1)}, bf16[256,1024]{1,0:T(8,128)(2,1)}, u32[]{:S(2)}, u32[]{:S(2)}) collective-permute-start(bf16[256,1024]{1,0:T(8,128)(2,1)} %add_convert_fusion), channel_id=1, source_target_pairs={{8,0},{12,4},{16,8},{20,12},{24,16},{28,20},{32,24},{36,28},{40,32... | collective-permute-start | bytes 1572872 | tf_op jit(solution)/shard_map/ppermute | solution.py:26
  226.4 35.1 %copy-start.28 = (s32[32,32]{1,0:T(8,128)S(1)}, s32[32,32]{1,0:T(8,128)}, u32[]{:S(2)}) copy-start(s32[32,32]{1,0:T(8,128)} %iota_subtract_fusion) | copy-start | bytes 12292
  351.2 81.3 %collective-permute-start.2 = (bf16[256,1024]{1,0:T(8,128)(2,1)}, bf16[256,1024]{1,0:T(8,128)(2,1)}, u32[]{:S(2)}, u32[]{:S(2)}) collective-permute-start(bf16[256,1024]{1,0:T(8,128)(2,1)} %get-tuple-element.174), channel_id=1, source_target_pairs={{0,4},{4,8},{8,12},{12,16},{16,20},{20,24},{24,28},{28,32},{32,36}... | collective-permute-start | bytes 1572872 | tf_op jit(solution)/shard_map/ppermute | solution.py:20
  402.3 30.3 %copy-start.3 = (f32[1024,16]{0,1:T(8,128)}, f32[1024,16]{0,1:T(8,128)S(1)}, u32[]{:S(2)}) copy-start(f32[1024,16]{0,1:T(8,128)S(1)} %get-tuple-element.63) | copy-start | bytes 196612
  402.3 32.5 %copy-start.2 = (f32[8,256,256]{1,2,0:T(8,128)S(1)}, f32[8,256,256]{1,2,0:T(8,128)}, u32[]{:S(2)}) copy-start(f32[8,256,256]{1,2,0:T(8,128)} %copy-done.1) | copy-start | bytes 6291460
  402.3 32.4 %copy-start.31 = (f32[8,256]{1,0:T(8,128)S(1)}, f32[8,256]{1,0:T(8,128)}, u32[]{:S(2)}) copy-start(f32[8,256]{1,0:T(8,128)} %get-tuple-element.172) | copy-start | bytes 24580
  432.6 12.8 %collective-permute-start.3 = (bf16[256,1024]{1,0:T(8,128)(2,1)}, bf16[256,1024]{1,0:T(8,128)(2,1)}, u32[]{:S(2)}, u32[]{:S(2)}) collective-permute-start(bf16[256,1024]{1,0:T(8,128)(2,1)} %collective-permute-done.2), channel_id=1, source_target_pairs={{0,4},{4,8},{8,12},{12,16},{16,20},{20,24},{24,28},{28,32},{32,36}... | collective-permute-start | bytes 1572872 | tf_op jit(solution)/shard_map/ppermute | solution.py:20
  459.5 19.9 %collective-permute-start.4 = (bf16[256,1024]{1,0:T(8,128)(2,1)}, bf16[256,1024]{1,0:T(8,128)(2,1)}, u32[]{:S(2)}, u32[]{:S(2)}) collective-permute-start(bf16[256,1024]{1,0:T(8,128)(2,1)} %copy.166), channel_id=1, source_target_pairs={{124,0},{0,4},{4,8},{8,12},{12,16},{16,20},{20,24},{24,28},{28,32}... | collective-permute-start | bytes 1572872 | tf_op jit(solution)/shard_map/ppermute | solution.py:26
  469.7 9.7 %copy-start.14 = (f32[256,1024]{1,0:T(8,128)S(1)}, f32[256,1024]{1,0:T(8,128)}, u32[]{:S(2)}) copy-start(f32[256,1024]{1,0:T(8,128)} %copy.169) | copy-start | bytes 3145732
  471.8 10.4 %copy-start.11 = (bf16[8,256,256]{1,2,0:T(8,128)(2,1)}, bf16[8,256,256]{1,2,0:T(8,128)(2,1)S(1)}, u32[]{:S(2)}) copy-start(bf16[8,256,256]{1,2,0:T(8,128)(2,1)S(1)} %fusion.16) | copy-start | bytes 3145732
  481.4 19.0 %collective-permute-start.5 = (bf16[256,1024]{1,0:T(8,128)(2,1)}, bf16[256,1024]{1,0:T(8,128)(2,1)}, u32[]{:S(2)}, u32[]{:S(2)}) collective-permute-start(bf16[256,1024]{1,0:T(8,128)(2,1)} %add_convert_fusion.3), channel_id=1, source_target_pairs={{124,0},{0,4},{4,8},{8,12},{12,16},{16,20},{20,24},{24,28},{28,32}... | collective-permute-start | bytes 1572872 | tf_op jit(solution)/shard_map/ppermute | solution.py:26
  483.5 16.9 %copy-start.15 = (f32[256,1024]{1,0:T(8,128)S(1)}, f32[256,1024]{1,0:T(8,128)}, u32[]{:S(2)}) copy-start(f32[256,1024]{1,0:T(8,128)} %copy.172) | copy-start | bytes 3145732
  483.5 18.9 %copy-start.10 = (bf16[8,256,256]{1,2,0:T(8,128)(2,1)S(1)}, bf16[8,256,256]{1,2,0:T(8,128)(2,1)}, u32[]{:S(2)}) copy-start(bf16[8,256,256]{1,2,0:T(8,128)(2,1)} %copy-done.9) | copy-start | bytes 3145732
  483.5 18.9 %copy-start.17 = (bf16[256,1024]{0,1:T(8,128)(2,1)S(1)}, bf16[256,1024]{0,1:T(8,128)(2,1)}, u32[]{:S(2)}) copy-start(bf16[256,1024]{0,1:T(8,128)(2,1)} %copy-done.16) | copy-start | bytes 1572868
  502.4 15.5 %collective-permute-start.6 = (bf16[256,1024]{1,0:T(8,128)(2,1)}, bf16[256,1024]{1,0:T(8,128)(2,1)S(1)}, u32[]{:S(2)}, u32[]{:S(2)}) collective-permute-start(bf16[256,1024]{1,0:T(8,128)(2,1)} %add_convert_fusion.2), channel_id=1, source_target_pairs={{8,0},{12,4},{16,8},{20,12},{24,16},{28,20},{32,24},{36,28},{40,32... | collective-permute-start | bytes 1572872 | tf_op jit(solution)/shard_map/ppermute | solution.py:26
  517.9 76.3 %copy-start.26 = (bf16[256,1024]{1,0:T(8,128)(2,1)}, bf16[256,1024]{1,0:T(8,128)(2,1)S(1)}, u32[]{:S(2)}) copy-start(bf16[256,1024]{1,0:T(8,128)(2,1)S(1)} %collective-permute-done.6) | copy-start | bytes 1572868
  597.0 6.3 copy-start.33
  597.1 6.3 copy-start.34
  603.4 29.9 %copy-start.20 = (f32[8,1024,16]{1,2,0:T(8,128)S(1)}, f32[8,1024,16]{1,2,0:T(8,128)}, u32[]{:S(2)}) copy-start(f32[8,1024,16]{1,2,0:T(8,128)} %get-tuple-element.62) | copy-start | bytes 1572868
  603.4 29.9 %copy-start.32 = (f32[8]{0:T(128)S(1)}, f32[8]{0:T(128)}, u32[]{:S(2)}) copy-start(f32[8]{0:T(128)} %iota_multiply_fusion) | copy-start | bytes 100
  (15 other events, 26.3 us)
Sparse Core Ops, SparseCore 0:
  57.8 156.5 all-gather.4
  437.6 156.5 all-gather.6
where the time goes:
time: 675 us; the launch traced here: 665 us
  waiting for transfers between devices  234 us (35%)
  matrix products  162 us (24%)
  local copies, waits for them, and re-layouts  118 us (17%)
  other arithmetic  108 us (16%)
  starting transfers between devices  19.7 us (3%)
  between operations  15 us (2%)
  blocking collectives  7.83 us (1%)
    all_gather x2, waiting for transfers between devices, carry_in(): piece = lax.all_gather(last_state[None], 'ctx', axis=0, tiled=True)  162 us
    reduce_sum x2, other arithmetic, carry_in(): return jnp.sum(factor * piece, axis=0)  64.8 us
    dot_general x2, matrix products, modal_mix(): inner = jnp.einsum('tsc,bsc->btc', toeplitz, pieces, precision=precise)  60.2 us
    ppermute x6, waiting for transfers between devices, passed_along_2(): return lax.ppermute(block, axis, route)  58.9 us
    dot_general x2, matrix products, modal_mix(): finals = jnp.einsum('bsc,scm->bcm', pieces, trailing, precision=precise)  35.2 us
    dot_general x2, matrix products, modal_mix(): outer = jnp.einsum('tcm,bcm->btc', leading, states, precision=precise)  32.4 us
    unnamed x79, local copies, waits for them, and re-layouts  23.6 us
    ppermute x4, starting transfers between devices, passed_along(): return lax.ppermute(value, axis, pairs)  14.3 us
  transfers between devices with their start and end apart: 12, of which 9 were waited for; matrix products, arithmetic and copies ran while one was open for 47% of the time, Pallas kernels for 0%

commit v1 on v0

v1 whole, which is shorter than its diff:
```python
import functools
import math

import jax
import jax.numpy as jnp
from jax import lax
from jax.experimental import pallas as pl
from jax.experimental.pallas import tpu as pltpu
from jax.sharding import PartitionSpec as P

HEAD_DIM = 128
SPAN = 2
EPS = 1e-06
LOG2E = 1.4426950408889634
MASKED = -1e30
LANES = 128
SUBLANES = 8
ROWS_PER_STEP = 8
f32 = jnp.float32
bf16 = jnp.bfloat16


def params(*semantics):
    return pltpu.CompilerParams(dimension_semantics=semantics or None, vmem_limit_bytes=48 << 20)


def shifted(value, by):
    devices = lax.axis_size("ctx")
    return lax.ppermute(value, "ctx", [(i, (i + by) % devices) for i in range(devices)])


def along(value, axis, by):
    def target(i):
        place = [i // 8, (i // 4) % 2, i % 4]
        size = (4, 2, 4)
        place[axis] = (place[axis] + by) % size[axis]
        return (place[0] * 2 + place[1]) * 4 + place[2]

    return lax.ppermute(value, "ctx", [(i, target(i)) for i in range(32)])


def carry_in(final, rate, length, reverse):
    position = lax.axis_index("ctx")
    position = (31 - position) if reverse else position
    sign = -1 if reverse else 1
    x, y, z = position // 8, (position // 4) % 2, position % 4

    def decayed(blocks, keep=True):
        blocks = jnp.asarray(blocks, f32)
        return jnp.where(keep, jnp.exp(-rate * (length * jnp.maximum(blocks, 0.0))), 0.0)

    others = [along(final, 2, sign * d) for d in (1, 2, 3)]
    state = sum(decayed(d - 1, d <= z) * other for d, other in zip((1, 2, 3), others))
    group = decayed(3 - z) * final
    for d, other in zip((1, 2, 3), others):
        group = group + decayed(3 - (z - d) % 4) * other
    partner = along(group, 1, 1)
    state = state + decayed(z, y == 1) * partner
    pair = jnp.where(y == 1, group + decayed(4) * partner, partner + decayed(4) * group)
    planes = [along(pair, 0, sign * d) for d in (1, 2, 3)]
    for d, other in zip((1, 2, 3), planes):
        state = state + decayed(position % 8 + 8 * (d - 1), d <= x) * other
    return state


def to_tokens(scratch, head, rows, block):
    scratch[pl.ds(head, rows, SUBLANES), :] = block


def from_tokens(scratch, head, rows):
    return scratch[pl.ds(head, rows, SUBLANES), :]


def head_slice(head):
    return slice(head * LANES, (head + 1) * LANES)


def tile(ref, m):
    return ref[m * SUBLANES : (m + 1) * SUBLANES, :]


def scan(drive, decay, residue, state, rows, out, reverse):
    modes = len(decay)

    def step(i, state):
        state = list(state)
        for j in range(ROWS_PER_STEP):
            t = i * ROWS_PER_STEP + j
            t = (rows - 1 - t) if reverse else t
            place = pl.ds(pl.multiple_of(t * SUBLANES, SUBLANES), SUBLANES)
            row = drive[place, :]
            state = [decay[m] * state[m] + row for m in range(modes)]
            if out is not None:
                terms = [residue[m] * state[m] for m in range(modes)]
                while len(terms) > 1:
                    terms = [a + b for a, b in zip(terms[::2], terms[1::2])]
                out[place, :] = terms[0]
        return tuple(state)

    return lax.fori_loop(0, rows // ROWS_PER_STEP, step, tuple(state))


def spread(source, target):
    modes, width = source.shape
    for head in range(width // LANES):
        to_tokens(target, head, modes, source[:, head_slice(head)])


def decays(rates, modes):
    return [jnp.exp(-tile(rates, m)) for m in range(modes)]


def forward_state_kernel(mixer, gate_in, rate, final, rates, drive):
    rows, width = mixer.shape
    modes = rate.shape[0]
    spread(rate, rates)
    for head in range(width // LANES):
        cut = head_slice(head)
        to_tokens(drive, head, rows, mixer[:, cut].astype(f32) * gate_in[:, cut].astype(f32))
    zero = jnp.zeros((SUBLANES, LANES), f32)
    state = scan(drive, decays(rates, modes), None, [zero] * modes, rows, None, False)
    for m in range(modes):
        final[m * SUBLANES : (m + 1) * SUBLANES, :] = state[m]


def forward_state(mixer, gate_in, rate):
    rows, width = mixer.shape
    modes = rate.shape[0]
    small = jax.ShapeDtypeStruct((modes * SUBLANES, LANES), f32)
    big = jax.ShapeDtypeStruct((rows * SUBLANES, LANES), f32)
    return pl.pallas_call(
        forward_state_kernel,
        out_shape=(small, small, big),
        compiler_params=params(),
        name="forward_state",
    )(mixer, gate_in, rate)


def row_total(block):
    ones = jnp.ones((SUBLANES, LANES), f32)
    return lax.dot_general(
        ones, block, (((1,), (1,)), ((), ())), precision=lax.Precision.HIGHEST, preferred_element_type=f32
    )


def forward_mix_kernel(drive, rates, residue, start, gate_out, gain, mixed, scaled, squares, residues, out):
    rows, width = mixed.shape
    modes = residue.shape[0]
    spread(residue, residues)
    decay = decays(rates, modes)
    res = [tile(residues, m) for m in range(modes)]
    scan(drive, decay, res, [tile(start, m) for m in range(modes)], rows, out, False)
    total = jnp.zeros((rows, LANES), f32)
    for head in range(width // LANES):
        cut = head_slice(head)
        value = gate_out[:, cut].astype(f32) * from_tokens(out, head, rows)
        mixed[:, cut] = value
        scaled[:, cut] = (value * gain[:, cut]).astype(bf16)
        total = total + value * value
    squares[...] = row_total(total)


def forward_mix(drive, rates, residue, start, gate_out, gain):
    rows, width = gate_out.shape
    modes = residue.shape[0]
    return pl.pallas_call(
        forward_mix_kernel,
        out_shape=(
            jax.ShapeDtypeStruct((rows, width), f32),
            jax.ShapeDtypeStruct((rows, width), bf16),
            jax.ShapeDtypeStruct((SUBLANES, rows), f32),
        ),
        scratch_shapes=[
            pltpu.VMEM((modes * SUBLANES, LANES), f32),
            pltpu.VMEM((rows * SUBLANES, LANES), f32),
        ],
        compiler_params=params(),
        name="forward_mix",
    )(drive, rates, residue, start, gate_out, gain)


def column(rows_ref):
    return jnp.transpose(rows_ref[...])[:, 0:1]


def inverse_of(squares, full_width):
    return lax.rsqrt(squares * (1.0 / full_width) + EPS)


def backward_state_kernel(full_width, scaled, mixed, gate_out, squares, inner, rates, final, drive):
    rows, width = mixed.shape
    modes = rates.shape[0] // SUBLANES
    inverse = inverse_of(column(squares), full_width)
    pull = inverse * inverse * inverse * column(inner) * (1.0 / full_width)
    for head in range(width // LANES):
        cut = head_slice(head)
        grad = inverse * scaled[:, cut] - mixed[:, cut] * pull
        to_tokens(drive, head, rows, gate_out[:, cut].astype(f32) * grad)
    zero = jnp.zeros((SUBLANES, LANES), f32)
    state = scan(drive, decays(rates, modes), None, [zero] * modes, rows, None, True)
    for m in range(modes):
        final[m * SUBLANES : (m + 1) * SUBLANES, :] = state[m]


def backward_state(full_width, scaled, mixed, gate_out, squares, inner, rates):
    rows, width = mixed.shape
    return pl.pallas_call(
        functools.partial(backward_state_kernel, full_width),
        out_shape=(
            jax.ShapeDtypeStruct(rates.shape, f32),
            jax.ShapeDtypeStruct((rows * SUBLANES, LANES), f32),
        ),
        compiler_params=params(),
        name="backward_state",
    )(scaled, mixed, gate_out, squares, inner, rates)


def backward_mix_kernel(drive, rates, residue, start, gate_in, grad, residues, out):
    rows, width = gate_in.shape
    modes = residue.shape[0]
    spread(residue, residues)
    decay = decays(rates, modes)
    res = [tile(residues, m) for m in range(modes)]
    scan(drive, decay, res, [tile(start, m) for m in range(modes)], rows, out, True)
    for head in range(width // LANES):
        cut = head_slice(head)
        grad[:, cut] = (gate_in[:, cut].astype(f32) * from_tokens(out, head, rows)).astype(bf16)


def backward_mix(drive, rates, residue, start, gate_in):
    rows, width = gate_in.shape
    modes = residue.shape[0]
    return pl.pallas_call(
        backward_mix_kernel,
        out_shape=jax.ShapeDtypeStruct((rows, width), bf16),
        scratch_shapes=[
            pltpu.VMEM((modes * SUBLANES, LANES), f32),
            pltpu.VMEM((rows * SUBLANES, LANES), f32),
        ],
        compiler_params=params(),
        name="backward_mix",
    )(drive, rates, residue, start, gate_in)


def rows_by_rows(a, b):
    return lax.dot_general(a, b, (((1,), (1,)), ((), ())), preferred_element_type=f32)


def product(a, b):
    return jnp.dot(a, b, preferred_element_type=f32)


def masked(scores, offset, near, transposed):
    if offset == 0:
        rows = lax.broadcasted_iota(jnp.int32, scores.shape, 0)
        columns = lax.broadcasted_iota(jnp.int32, scores.shape, 1)
        allowed = (rows <= columns) if transposed else (columns <= rows)
        return jnp.where(allowed, scores, MASKED)
    return scores + jnp.where(near, 0.0, MASKED)


SCALE = 1.0 / math.sqrt(HEAD_DIM)


def totals_kernel(place, queries, keys, keys_1, keys_2, totals):
    head = pl.program_id(0)
    position = place[0]
    scores = [
        masked(rows_by_rows(block[...], queries[...]) * (SCALE * LOG2E), offset, position >= offset, True)
        for offset, block in enumerate((keys, keys_1, keys_2))
    ]
    top = functools.reduce(jnp.maximum, [jnp.max(s, axis=0, keepdims=True) for s in scores])
    total = sum(jnp.sum(jnp.exp2(s - top), axis=0, keepdims=True) for s in scores)
    totals[pl.ds(head, 1), :] = top + jnp.log(total) * LOG2E


def head_block(rows, part=0):
    return pl.BlockSpec((rows, HEAD_DIM), lambda head, *_: (part, head))


def whole(shape):
    return pl.BlockSpec(shape, lambda head, *_: (0,) * len(shape))


def per_head(kernel, place, operands, specs, out_shape, out_specs, scratch=(), name=None):
    heads = operands[0].shape[1] // HEAD_DIM
    return pl.pallas_call(
        kernel,
        out_shape=out_shape,
        grid_spec=pltpu.PrefetchScalarGridSpec(
            num_scalar_prefetch=1,
            grid=(heads,),
            in_specs=specs,
            out_specs=out_specs,
            scratch_shapes=scratch,
        ),
        compiler_params=params("arbitrary"),
        name=name,
    )(place, *operands)


def row_totals(place, queries, keys, keys_1, keys_2):
    rows, width = queries.shape
    shape = (width // HEAD_DIM, rows)
    block = head_block(rows)
    return per_head(
        totals_kernel,
        place,
        (queries, keys, keys_1, keys_2),
        [block] * 4,
        jax.ShapeDtypeStruct(shape, f32),
        whole(shape),
        name="row_totals",
    )


def value_grads_kernel(
    blocks, place, keys, q0, q1, q2, d0, d1, d2, t0, t1, t2, gain, mixed, scaled, inner, acc
):
    head = pl.program_id(0)
    position = place[0]
    grad = None
    for offset, (query, cotangent, total) in enumerate(((q0, d0, t0), (q1, d1, t1), (q2, d2, t2))):
        scores = rows_by_rows(keys[...], query[...]) * (SCALE * LOG2E)
        scores = masked(scores, offset, position + offset < blocks, True)
        probs = jnp.exp2(scores - total[pl.ds(head, 1), :])
        part = product(probs.astype(bf16), cotangent[...])
        grad = part if grad is None else grad + part
    value = grad * gain[...]
    scaled[...] = value

    @pl.when(head == 0)
    def _():
        acc[...] = jnp.zeros_like(acc)

    acc[...] += value * mixed[...]

    @pl.when(head == pl.num_programs(0) - 1)
    def _():
        inner[...] = row_total(acc[...])


def value_grads(blocks, place, keys, queries, cotangents, totals, gain, mixed):
    rows, width = keys.shape
    heads = width // HEAD_DIM
    block = head_block(rows)
    stat = whole((heads, rows))
    return per_head(
        functools.partial(value_grads_kernel, blocks),
        place,
        (keys, *queries, *cotangents, *totals, gain, mixed),
        [block] * 7 + [stat] * 3 + [head_block(1), block],
        (jax.ShapeDtypeStruct((rows, width), f32), jax.ShapeDtypeStruct((SUBLANES, rows), f32)),
        (block, whole((SUBLANES, rows))),
        scratch=[pltpu.VMEM((rows, LANES), f32)],
        name="value_grads",
    )


def attend_kernel(
    full_width, place, queries, cotangent, k0, k1, k2, v0, v1, v2, s0, s1, s2, totals, attended, grad, delta, columns
):
    head = pl.program_id(0)
    position = place[0]

    @pl.when(head == 0)
    def _():
        columns[...] = jnp.transpose(totals[...])

    lane = lax.broadcasted_iota(jnp.int32, columns.shape, 1)
    log_total = jnp.sum(jnp.where(lane == head, columns[...], 0.0), axis=1, keepdims=True)
    probs, inverses = [], []
    output = None
    for offset, (key, value, squares) in enumerate(((k0, v0, s0), (k1, v1, s1), (k2, v2, s2))):
        scores = rows_by_rows(queries[...], key[...]) * (SCALE * LOG2E)
        scores = masked(scores, offset, position >= offset, False)
        prob = jnp.exp2(scores - log_total)
        inverse = inverse_of(squares[0:1, :], full_width)
        probs.append(prob)
        inverses.append(inverse)
        part = product((prob * inverse).astype(bf16), value[...])
        output = part if output is None else output + part
    result = output.astype(bf16)
    attended[...] = result
    weighed = cotangent[...].astype(f32) * result.astype(f32)
    delta[pl.ds(head, 1), :] = row_total(weighed)[0:1, :]
    delta_column = jnp.sum(weighed, axis=1, keepdims=True)
    total = None
    for prob, inverse, key, value in zip(probs, inverses, (k0, k1, k2), (v0, v1, v2)):
        dprob = rows_by_rows(cotangent[...], value[...]) * inverse
        dscore = (prob * (dprob - delta_column)).astype(bf16)
        part = product(dscore, key[...])
        total = part if total is None else total + part
    grad[...] = (total * SCALE).astype(bf16)


def attend(full_width, place, queries, cotangent, keys, values, squares, totals):
    rows, width = queries.shape
    heads = width // HEAD_DIM
    block = head_block(rows)
    stat = whole((heads, rows))
    out = jax.ShapeDtypeStruct((rows, width), bf16)
    return per_head(
        functools.partial(attend_kernel, full_width),
        place,
        (queries, cotangent, *keys, *values, *squares, totals),
        [block] * 8 + [whole((SUBLANES, rows))] * 3 + [stat],
        (out, out, jax.ShapeDtypeStruct((heads, rows), f32)),
        (block, block, stat),
        scratch=[pltpu.VMEM((rows, heads), f32)],
        name="attend",
    )


def key_grads_kernel(
    full_width, blocks, place, keys, values, q0, q1, q2, d0, d1, d2, t0, t1, t2, e0, e1, e2, squares, grad
):
    head = pl.program_id(0)
    position = place[0]
    inverse = inverse_of(column(squares), full_width)
    total = None
    groups = ((q0, d0, t0, e0), (q1, d1, t1, e1), (q2, d2, t2, e2))
    for offset, (query, cotangent, log_total, delta) in enumerate(groups):
        scores = rows_by_rows(keys[...], query[...]) * (SCALE * LOG2E)
        scores = masked(scores, offset, position + offset < blocks, True)
        probs = jnp.exp2(scores - log_total[pl.ds(head, 1), :])
        dprob = rows_by_rows(values[...], cotangent[...]) * inverse
        dscore = (probs * (dprob - delta[pl.ds(head, 1), :])).astype(bf16)
        part = product(dscore, query[...])
        total = part if total is None else total + part
    grad[...] = (total * SCALE).astype(bf16)


def key_grads(full_width, blocks, place, keys, values, queries, cotangents, totals, deltas, squares):
    rows, width = keys.shape
    heads = width // HEAD_DIM
    block = head_block(rows)
    stat = whole((heads, rows))
    return per_head(
        functools.partial(key_grads_kernel, full_width, blocks),
        place,
        (keys, values, *queries, *cotangents, *totals, *deltas, squares),
        [block] * 8 + [stat] * 6 + [whole((SUBLANES, rows))],
        jax.ShapeDtypeStruct((rows, width), bf16),
        block,
        name="key_grads",
    )


def shards(
    mixer_input, gate_in, gate_out, residue, decay_rate, norm_gain, queries, key_vectors, grad_out
):
    length, width = queries.shape
    full_width = width * lax.axis_size("tp")
    blocks = lax.axis_size("ctx")
    place = lax.axis_index("ctx").reshape(1).astype(jnp.int32)
    gain = norm_gain[None, :]
    residue = jnp.transpose(residue)

    keys_1 = shifted(key_vectors, 1)
    keys_2 = shifted(keys_1, 1)
    queries_1 = shifted(queries, -1)
    cotangent_1 = shifted(grad_out, -1)
    queries_2 = shifted(queries_1, -1)
    cotangent_2 = shifted(cotangent_1, -1)

    final, rates, drive = forward_state(mixer_input, gate_in, jnp.transpose(decay_rate))
    start = carry_in(final, rates, length, False)
    mixed, scaled_mix, squares = forward_mix(drive, rates, residue, start, gate_out, gain)
    mix_1 = shifted(scaled_mix, 1)
    mix_2 = shifted(mix_1, 1)
    squares = lax.psum(squares, "tp")
    squares_1 = shifted(squares, 1)
    squares_2 = shifted(squares, 2)

    totals = row_totals(place, queries, key_vectors, keys_1, keys_2)
    totals_1 = shifted(totals, -1)
    totals_2 = shifted(totals, -2)
    all_queries = (queries, queries_1, queries_2)
    all_cotangents = (grad_out, cotangent_1, cotangent_2)
    all_totals = (totals, totals_1, totals_2)
    scaled, inner = value_grads(
        blocks, place, key_vectors, all_queries, all_cotangents, all_totals, gain, mixed
    )
    inner = lax.psum(inner, "tp")
    final, drive = backward_state(full_width, scaled, mixed, gate_out, squares, inner, rates)
    start = carry_in(final, rates, length, True)
    grad_input = backward_mix(drive, rates, residue, start, gate_in)

    attended, grad_queries, delta = attend(
        full_width,
        place,
        queries,
        grad_out,
        (key_vectors, keys_1, keys_2),
        (scaled_mix, mix_1, mix_2),
        (squares, squares_1, squares_2),
        totals,
    )
    all_deltas = (delta, shifted(delta, -1), shifted(delta, -2))
    grad_keys = key_grads(
        full_width,
        blocks,
        place,
        key_vectors,
        scaled_mix,
        all_queries,
        all_cotangents,
        all_totals,
        all_deltas,
        squares,
    )
    return (attended, grad_queries, grad_keys, grad_input)


def solution(mesh):
    in_specs = (
        P("ctx", "tp"),
        P("ctx", "tp"),
        P("ctx", "tp"),
        P("tp", None),
        P("tp", None),
        P("tp"),
        P("ctx", "tp"),
        P("ctx", "tp"),
        P("ctx", "tp"),
    )
    out_specs = (P("ctx", "tp"), P("ctx", "tp"), P("ctx", "tp"), P("ctx", "tp"))
    return jax.shard_map(shards, mesh=mesh, in_specs=in_specs, out_specs=out_specs, check_vma=False)
```

time: 675 us -> 181 us (0.27); the launches traced: 665 us -> 179 us
  waiting for transfers between devices: 234 us -> 57.1 us
  matrix products: 162 us -> 0 us
  local copies, waits for them, and re-layouts: 118 us -> 11.8 us
  other arithmetic: 108 us -> 1.94 us
  Pallas kernels: 0 us -> 39.9 us
  starting transfers between devices: 19.7 us -> 53.8 us
  between operations: 15 us -> 0.95 us
    dot_general x25 -> x0, matrix products: 162 us -> none  [the longest x2 60.2 us: modal_mix(): inner = jnp.einsum('tsc,bsc->btc', toeplitz, pieces, precision=precise)]
    all_gather x2 -> x0, waiting for transfers between devices: 162 us -> none  [carry_in(): piece = lax.all_gather(last_state[None], 'ctx', axis=0, tiled=True)]
    reduce_sum x4 -> x0, other arithmetic: 68.6 us -> none  [the longest x2 64.8 us: carry_in(): return jnp.sum(factor * piece, axis=0)]
    pallas_call x0 -> x8, Pallas kernels: none -> 39.9 us  [the longest x4 29.9 us: per_head(): pl.pallas_call(kernel, out_shape=out_shape, grid_spec=pltpu.PrefetchScala...]
    ppermute x10 -> x28, starting transfers between devices: 19.6 us -> 53.8 us  [the longest x14 34.7 us: along(): return lax.ppermute(value, 'ctx', [(i, target(i)) for i in range(32)])]
    rev x3 -> x0, local copies, waits for them, and re-layouts: 22.6 us -> none  [the longest x1 13.2 us: modal_tables(): return (toeplitz, powers[::-1], leading)]
    reshape x8 -> x0, local copies, waits for them, and re-layouts: 17.9 us -> none  [the longest x2 6.39 us: modal_mix(): pieces = drive.reshape(count, window, width)]
    ppermute x10 -> x28, waiting for transfers between devices: 72.6 us -> 57.1 us  [the longest x14 29.2 us: along(): return lax.ppermute(value, 'ctx', [(i, target(i)) for i in range(32)])]
  transfers between devices with their start and end apart: 12 -> 28, of which waited for: 9 -> 11; matrix products, arithmetic and copies ran while one was open for 47% -> 0% of each run, Pallas kernels for 0% -> 19%
where the time goes in v1:
time: 181 us; the launch traced here: 179 us
  waiting for transfers between devices  57.1 us (32%)
  starting transfers between devices  53.8 us (30%)
  Pallas kernels  39.9 us (22%)
  blocking collectives  13.8 us (8%)
  local copies, waits for them, and re-layouts  11.8 us (7%)
  other arithmetic  1.94 us (1%)
    ppermute x14, starting transfers between devices, along(): return lax.ppermute(value, 'ctx', [(i, target(i)) for i in range(32)])  34.7 us
    pallas_call x4, Pallas kernels, per_head(): pl.pallas_call(kernel, out_shape=out_shape, grid_spec=pltpu.PrefetchScala...  29.9 us
    ppermute x14, waiting for transfers between devices, along(): return lax.ppermute(value, 'ctx', [(i, target(i)) for i in range(32)])  29.2 us
    ppermute x14, waiting for transfers between devices, shifted(): lax.ppermute(value, 'ctx', [(i, (i + by) % devices) for i in range(device...  28 us
    ppermute x14, starting transfers between devices, shifted(): lax.ppermute(value, 'ctx', [(i, (i + by) % devices) for i in range(device...  19.2 us
    psum x1, blocking collectives, shards(): squares = lax.psum(squares, 'tp')  13.8 us
    unnamed x54, local copies, waits for them, and re-layouts  11.8 us
  transfers between devices with their start and end apart: 28, of which 11 were waited for; matrix products, arithmetic and copies ran while one was open for 0% of the time, Pallas kernels for 19%

profile of v1, /device:TPU:0, one launch (start us, length us, event | category | flops | bytes accessed | tf_op | source)
XLA Modules:
  0.0 179.3 jit_solution(14757327421005984114)
XLA Ops:
  3.6 1.5 forward_state.1
  6.1 2.0 %collective-permute-start.2 = (f32[128,128]{1,0:T(8,128)S(1)}, f32[128,128]{1,0:T(8,128)S(1)}, u32[]{:S(2)}, u32[]{:S(2)}) collective-permute-start(f32[128,128]{1,0:T(8,128)S(1)} %get-tuple-element.19), channel_id=1, source_target_pairs={{0,4},{4,8},{8,12},{12,0},{16,20},{20,24},{24,28},{28,16},{32,36},... | collective-permute-start | bytes 196616 | tf_op jit(solution)/shard_map/ppermute | solution.py:39
  8.1 3.6 %collective-permute-start.3 = (f32[128,128]{1,0:T(8,128)S(1)}, f32[128,128]{1,0:T(8,128)S(1)}, u32[]{:S(2)}, u32[]{:S(2)}) collective-permute-start(f32[128,128]{1,0:T(8,128)S(1)} %get-tuple-element.19), channel_id=1, source_target_pairs={{0,8},{4,12},{8,0},{12,4},{16,24},{20,28},{24,16},{28,20},{32,40},... | collective-permute-start | bytes 196616 | tf_op jit(solution)/shard_map/ppermute | solution.py:39
  13.8 5.2 %collective-permute-start.13 = (bf16[256,1024]{1,0:T(8,128)(2,1)S(1)}, bf16[256,1024]{1,0:T(8,128)(2,1)}, u32[]{:S(2)}, u32[]{:S(2)}) collective-permute-start(bf16[256,1024]{1,0:T(8,128)(2,1)S(1)} %copy-done), channel_id=1, source_target_pairs={{0,124},{4,0},{8,4},{12,8},{16,12},{20,16},{24,20},{28,24},{32,28}... | collective-permute-start | bytes 1572872 | tf_op jit(solution)/shard_map/ppermute | solution.py:29
  19.3 22.3 %collective-permute-done.5 = f32[128,128]{1,0:T(8,128)S(1)} collective-permute-done((f32[128,128]{1,0:T(8,128)S(1)}, f32[128,128]{1,0:T(8,128)S(1)}, u32[]{:S(2)}, u32[]{:S(2)}) %collective-permute-start.5) | collective-permute-done | bytes 65568 | tf_op jit(solution)/shard_map/ppermute | solution.py:39
  41.6 1.6 collective-permute-start.6
  43.2 2.7 %collective-permute-start.7 = (f32[128,128]{1,0:T(8,128)S(1)}, f32[128,128]{1,0:T(8,128)S(1)}, u32[]{:S(2)}, u32[]{:S(2)}) collective-permute-start(f32[128,128]{1,0:T(8,128)S(1)} %add_select_fusion.1), channel_id=1, source_target_pairs={{0,64},{4,68},{8,72},{12,76},{16,80},{20,84},{24,88},{28,92},{32,9... | collective-permute-start | bytes 196616 | tf_op jit(solution)/shard_map/ppermute | solution.py:39
  45.9 1.5 collective-permute-done.6
  48.8 6.2 %collective-permute-start.14 = (bf16[256,1024]{1,0:T(8,128)(2,1)}, bf16[256,1024]{1,0:T(8,128)(2,1)S(1)}, u32[]{:S(2)}, u32[]{:S(2)}) collective-permute-start(bf16[256,1024]{1,0:T(8,128)(2,1)} %collective-permute-done.13.q1), channel_id=1, source_target_pairs={{0,124},{4,0},{8,4},{12,8},{16,12},{20,16},{24,20},{28,24},{32,28}... | collective-permute-start | bytes 1572872 | tf_op jit(solution)/shard_map/ppermute | solution.py:29
  57.1 3.3 %forward_mix.1 = (f32[256,1024]{1,0:T(8,128)S(1)}, bf16[256,1024]{1,0:T(8,128)(2,1)}, f32[8,256]{1,0:T(8,128)S(1)}) custom-call(f32[2048,128]{1,0:T(8,128)S(1)} %copy-done.14, f32[128,128]{1,0:T(8,128)S(1)} %get-tuple-element.18.rates, f32[16,1024]{1,0:T(8,128)S(1)} %bitcast.4, f32[128,128]{1,0:T(8,128)S(1)} %multiply_add_fusion.2.start, ...), custom_call_target="tpu_custom_call" | custom-call | tf_op jit(solution)/shard_map/forward_mix/pallas_call | solution.py:166
  60.4 2.0 %collective-permute-start.9 = (bf16[256,1024]{1,0:T(8,128)(2,1)}, bf16[256,1024]{1,0:T(8,128)(2,1)}, u32[]{:S(2)}, u32[]{:S(2)}) collective-permute-start(bf16[256,1024]{1,0:T(8,128)(2,1)} %get-tuple-element.20.v0.values), channel_id=1, source_target_pairs={{0,4},{4,8},{8,12},{12,16},{16,20},{20,24},{24,28},{28,32},{32,36}... | collective-permute-start | bytes 1572872 | tf_op jit(solution)/shard_map/ppermute | solution.py:29
  62.4 1.7 collective-permute-done.1.keys_2.k2
  64.1 3.9 %row_totals.1.totals.t0 = f32[8,256]{1,0:T(8,128)S(1)} custom-call(s32[1]{0:T(128)} %bitcast.place, bf16[256,1024]{1,0:T(8,128)(2,1)S(1)} %copy-done, bf16[256,1024]{1,0:T(8,128)(2,1)S(1)} %copy-done.1, bf16[256,1024]{1,0:T(8,128)(2,1)S(1)} %collective-permute-done.keys_1.k1, bf16[256,1024]{1,0:T(8,128)(2,1)S(1)} %collective-permute-done.1.keys_2.k2), custom_call_target="tpu_custom_call" | custom-call | tf_op jit(solution)/shard_map/row_totals/pallas_call | solution.py:287
  68.0 2.7 %collective-permute-start.17 = (f32[8,256]{1,0:T(8,128)S(1)}, f32[8,256]{1,0:T(8,128)S(1)}, u32[]{:S(2)}, u32[]{:S(2)}) collective-permute-start(f32[8,256]{1,0:T(8,128)S(1)} %row_totals.1.totals.t0), channel_id=1, source_target_pairs={{0,124},{4,0},{8,4},{12,8},{16,12},{20,16},{24,20},{28,24},{32,28}... | collective-permute-start | bytes 24584 | tf_op jit(solution)/shard_map/ppermute | solution.py:29
  70.7 4.4 %collective-permute-done.16.d2 = bf16[256,1024]{1,0:T(8,128)(2,1)S(1)} collective-permute-done((bf16[256,1024]{1,0:T(8,128)(2,1)}, bf16[256,1024]{1,0:T(8,128)(2,1)S(1)}, u32[]{:S(2)}, u32[]{:S(2)}) %collective-permute-start.16) | collective-permute-done | bytes 524320 | tf_op jit(solution)/shard_map/ppermute | solution.py:29
  75.8 7.2 %value_grads.1 = (f32[256,1024]{1,0:T(8,128)S(1)}, f32[8,256]{1,0:T(8,128)S(1)}) custom-call(s32[1]{0:T(128)} %bitcast.place, bf16[256,1024]{1,0:T(8,128)(2,1)S(1)} %copy-done.1, bf16[256,1024]{1,0:T(8,128)(2,1)S(1)} %copy-done, bf16[256,1024]{1,0:T(8,128)(2,1)} %collective-permute-done.13.q1, bf16[256,1024]{1,0:T(8,128)(2,1)S(1)} %collective-permute-done.14.q2, ...), custom_call_target="tpu_custom_call" | custom-call | tf_op jit(solution)/shard_map/value_grads/pallas_call | solution.py:287
  84.1 13.8 %all-reduce = (f32[8,256]{1,0:T(8,128)S(1)}, f32[8,256]{1,0:T(8,128)S(1)}) all-reduce(f32[8,256]{1,0:T(8,128)S(1)} %get-tuple-element.21, f32[8,256]{1,0:T(8,128)S(1)} %get-tuple-element.27), channel_id=1, replica_groups=mesh['ctx'=32,'tp'=4] {'tp'}, use_global_device_ids=true, to_apply=%region_0.1 | all-reduce | flops 4096 | bytes 32768 | tf_op jit(solution)/shard_map/psum | solution.py:472
  100.1 1.6 backward_state.1
  102.8 3.8 %collective-permute-start.21 = (f32[128,128]{1,0:T(8,128)S(1)}, f32[128,128]{1,0:T(8,128)S(1)}, u32[]{:S(2)}, u32[]{:S(2)}) collective-permute-start(f32[128,128]{1,0:T(8,128)S(1)} %get-tuple-element.29), channel_id=1, source_target_pairs={{0,12},{4,0},{8,4},{12,8},{16,28},{20,16},{24,20},{28,24},{32,44},... | collective-permute-start | bytes 196616 | tf_op jit(solution)/shard_map/ppermute | solution.py:39
  108.2 1.9 %collective-permute-start.10 = (bf16[256,1024]{1,0:T(8,128)(2,1)}, bf16[256,1024]{1,0:T(8,128)(2,1)}, u32[]{:S(2)}, u32[]{:S(2)}) collective-permute-start(bf16[256,1024]{1,0:T(8,128)(2,1)} %collective-permute-done.9.v1), channel_id=1, source_target_pairs={{0,4},{4,8},{8,12},{12,16},{16,20},{20,24},{24,28},{28,32},{32,36}... | collective-permute-start | bytes 1572872 | tf_op jit(solution)/shard_map/ppermute | solution.py:29
  110.1 3.0 %collective-permute-done.22 = f32[128,128]{1,0:T(8,128)S(1)} collective-permute-done((f32[128,128]{1,0:T(8,128)S(1)}, f32[128,128]{1,0:T(8,128)S(1)}, u32[]{:S(2)}, u32[]{:S(2)}) %collective-permute-start.22) | collective-permute-done | bytes 65568 | tf_op jit(solution)/shard_map/ppermute | solution.py:39
  113.7 10.4 %collective-permute-start.24 = (f32[128,128]{1,0:T(8,128)S(1)}, f32[128,128]{1,0:T(8,128)S(1)}, u32[]{:S(2)}, u32[]{:S(2)}) collective-permute-start(f32[128,128]{1,0:T(8,128)S(1)} %multiply_add_fusion.1), channel_id=1, source_target_pairs={{0,16},{4,20},{8,24},{12,28},{16,0},{20,4},{24,8},{28,12},{32,48},... | collective-permute-start | bytes 196616 | tf_op jit(solution)/shard_map/ppermute | solution.py:39
  124.2 2.2 %collective-permute-done.24 = f32[128,128]{1,0:T(8,128)S(1)} collective-permute-done((f32[128,128]{1,0:T(8,128)S(1)}, f32[128,128]{1,0:T(8,128)S(1)}, u32[]{:S(2)}, u32[]{:S(2)}) %collective-permute-start.24) | collective-permute-done | bytes 65568 | tf_op jit(solution)/shard_map/ppermute | solution.py:39
  127.1 2.9 %collective-permute-start.25 = (f32[128,128]{1,0:T(8,128)}, f32[128,128]{1,0:T(8,128)}, u32[]{:S(2)}, u32[]{:S(2)}) collective-permute-start(f32[128,128]{1,0:T(8,128)} %add_select_fusion), channel_id=1, source_target_pairs={{0,96},{4,100},{8,104},{12,108},{16,112},{20,116},{24,120},{28,124... | collective-permute-start | bytes 196616 | tf_op jit(solution)/shard_map/ppermute | solution.py:39
  130.0 3.7 %collective-permute-start.26 = (f32[128,128]{1,0:T(8,128)}, f32[128,128]{1,0:T(8,128)}, u32[]{:S(2)}, u32[]{:S(2)}) collective-permute-start(f32[128,128]{1,0:T(8,128)} %add_select_fusion), channel_id=1, source_target_pairs={{0,64},{4,68},{8,72},{12,76},{16,80},{20,84},{24,88},{28,92},{32,9... | collective-permute-start | bytes 196616 | tf_op jit(solution)/shard_map/ppermute | solution.py:39
  133.7 7.9 %collective-permute-done.11.s1 = f32[8,256]{1,0:T(8,128)S(1)} collective-permute-done((f32[8,256]{1,0:T(8,128)S(1)}, f32[8,256]{1,0:T(8,128)S(1)}, u32[]{:S(2)}, u32[]{:S(2)}) %collective-permute-start.11) | collective-permute-done | bytes 8224 | tf_op jit(solution)/shard_map/ppermute | solution.py:29
  141.6 8.2 %collective-permute-done.12.s2 = f32[8,256]{1,0:T(8,128)S(1)} collective-permute-done((f32[8,256]{1,0:T(8,128)S(1)}, f32[8,256]{1,0:T(8,128)S(1)}, u32[]{:S(2)}, u32[]{:S(2)}) %collective-permute-start.12) | collective-permute-done | bytes 8224 | tf_op jit(solution)/shard_map/ppermute | solution.py:29
  149.7 10.6 %attend.1 = (bf16[256,1024]{1,0:T(8,128)(2,1)}, bf16[256,1024]{1,0:T(8,128)(2,1)}, f32[8,256]{1,0:T(8,128)S(1)}) custom-call(s32[1]{0:T(128)} %bitcast.place, bf16[256,1024]{1,0:T(8,128)(2,1)S(1)} %copy-done, bf16[256,1024]{1,0:T(8,128)(2,1)S(1)} %copy-done.2, bf16[256,1024]{1,0:T(8,128)(2,1)S(1)} %copy-done.1, ...), custom_call_target="tpu_custom_call" | custom-call | tf_op jit(solution)/shard_map/attend/pallas_call | solution.py:287
  160.4 3.6 %collective-permute-done.19.e1 = f32[8,256]{1,0:T(8,128)S(1)} collective-permute-done((f32[8,256]{1,0:T(8,128)S(1)}, f32[8,256]{1,0:T(8,128)S(1)}, u32[]{:S(2)}, u32[]{:S(2)}) %collective-permute-start.19) | collective-permute-done | bytes 8224 | tf_op jit(solution)/shard_map/ppermute | solution.py:29
  164.0 1.5 collective-permute-done.20.e2
  166.5 8.2 %key_grads.1 = bf16[256,1024]{1,0:T(8,128)(2,1)} custom-call(s32[1]{0:T(128)} %bitcast.place, bf16[256,1024]{1,0:T(8,128)(2,1)S(1)} %copy-done.1, bf16[256,1024]{1,0:T(8,128)(2,1)} %get-tuple-element.20.v0.values, bf16[256,1024]{1,0:T(8,128)(2,1)S(1)} %copy-done, bf16[256,1024]{1,0:T(8,128)(2,1)} %collective-permute-done.13.q1, ...), custom_call_target="tpu_custom_call" | custom-call | tf_op jit(solution)/shard_map/key_grads/pallas_call | solution.py:287
  175.9 3.4 %backward_mix.1 = bf16[256,1024]{1,0:T(8,128)(2,1)} custom-call(f32[2048,128]{1,0:T(8,128)S(1)} %copy-done.16, f32[128,128]{1,0:T(8,128)S(1)} %get-tuple-element.18.rates, f32[16,1024]{1,0:T(8,128)S(1)} %bitcast.5, f32[128,128]{1,0:T(8,128)S(1)} %multiply_add_fusion.start, bf16[256,1024]{1,0:T(8,128)(2,1)S(1)} %copy-done.8), custom_call_target="tpu_custom_call" | custom-call | tf_op jit(solution)/shard_map/backward_mix/pallas_call | solution.py:233
  (93 shorter events, 19.7 us)
Async XLA Ops:
  6.1 12.8 %collective-permute-start.2 = (f32[128,128]{1,0:T(8,128)S(1)}, f32[128,128]{1,0:T(8,128)S(1)}, u32[]{:S(2)}, u32[]{:S(2)}) collective-permute-start(f32[128,128]{1,0:T(8,128)S(1)} %get-tuple-element.19), channel_id=1, source_target_pairs={{0,4},{4,8},{8,12},{12,0},{16,20},{20,24},{24,28},{28,16},{32,36},... | collective-permute-start | bytes 196616 | tf_op jit(solution)/shard_map/ppermute | solution.py:39
  8.1 10.9 %collective-permute-start.3 = (f32[128,128]{1,0:T(8,128)S(1)}, f32[128,128]{1,0:T(8,128)S(1)}, u32[]{:S(2)}, u32[]{:S(2)}) collective-permute-start(f32[128,128]{1,0:T(8,128)S(1)} %get-tuple-element.19), channel_id=1, source_target_pairs={{0,8},{4,12},{8,0},{12,4},{16,24},{20,28},{24,16},{28,20},{32,40},... | collective-permute-start | bytes 196616 | tf_op jit(solution)/shard_map/ppermute | solution.py:39
  11.7 7.3 %collective-permute-start.4 = (f32[128,128]{1,0:T(8,128)S(1)}, f32[128,128]{1,0:T(8,128)S(1)}, u32[]{:S(2)}, u32[]{:S(2)}) collective-permute-start(f32[128,128]{1,0:T(8,128)S(1)} %get-tuple-element.19), channel_id=1, source_target_pairs={{0,12},{4,0},{8,4},{12,8},{16,28},{20,16},{24,20},{28,24},{32,44},... | collective-permute-start | bytes 196616 | tf_op jit(solution)/shard_map/ppermute | solution.py:39
  12.7 36.0 %collective-permute-start = (bf16[256,1024]{1,0:T(8,128)(2,1)S(1)}, bf16[256,1024]{1,0:T(8,128)(2,1)S(1)}, u32[]{:S(2)}, u32[]{:S(2)}) collective-permute-start(bf16[256,1024]{1,0:T(8,128)(2,1)S(1)} %copy-done.1), channel_id=1, source_target_pairs={{0,4},{4,8},{8,12},{12,16},{16,20},{20,24},{24,28},{28,32},{32,36}... | collective-permute-start | bytes 1572872 | tf_op jit(solution)/shard_map/ppermute | solution.py:29
  13.8 35.0 %collective-permute-start.13 = (bf16[256,1024]{1,0:T(8,128)(2,1)S(1)}, bf16[256,1024]{1,0:T(8,128)(2,1)}, u32[]{:S(2)}, u32[]{:S(2)}) collective-permute-start(bf16[256,1024]{1,0:T(8,128)(2,1)S(1)} %copy-done), channel_id=1, source_target_pairs={{0,124},{4,0},{8,4},{12,8},{16,12},{20,16},{24,20},{28,24},{32,28}... | collective-permute-start | bytes 1572872 | tf_op jit(solution)/shard_map/ppermute | solution.py:29
  19.0 36.0 %collective-permute-start.15 = (bf16[256,1024]{1,0:T(8,128)(2,1)}, bf16[256,1024]{1,0:T(8,128)(2,1)}, u32[]{:S(2)}, u32[]{:S(2)}) collective-permute-start(bf16[256,1024]{1,0:T(8,128)(2,1)} %d0.3), channel_id=1, source_target_pairs={{0,124},{4,0},{8,4},{12,8},{16,12},{20,16},{24,20},{28,24},{32,28}... | collective-permute-start | bytes 1572872 | tf_op jit(solution)/shard_map/ppermute | solution.py:29
  19.1 36.1 %copy-start.5 = (bf16[256,1024]{1,0:T(8,128)(2,1)S(1)}, bf16[256,1024]{1,0:T(8,128)(2,1)}, u32[]{:S(2)}) copy-start(bf16[256,1024]{1,0:T(8,128)(2,1)} %gate_out.3) | copy-start | bytes 1572868
  19.1 22.5 %collective-permute-start.5 = (f32[128,128]{1,0:T(8,128)S(1)}, f32[128,128]{1,0:T(8,128)S(1)}, u32[]{:S(2)}, u32[]{:S(2)}) collective-permute-start(f32[128,128]{1,0:T(8,128)S(1)} %multiply_add_fusion.3), channel_id=1, source_target_pairs={{0,16},{4,20},{8,24},{12,28},{16,0},{20,4},{24,8},{28,12},{32,48},... | collective-permute-start | bytes 196616 | tf_op jit(solution)/shard_map/ppermute | solution.py:39
  41.6 5.8 %collective-permute-start.6 = (f32[128,128]{1,0:T(8,128)S(1)}, f32[128,128]{1,0:T(8,128)S(1)}, u32[]{:S(2)}, u32[]{:S(2)}) collective-permute-start(f32[128,128]{1,0:T(8,128)S(1)} %add_select_fusion.1), channel_id=1, source_target_pairs={{0,32},{4,36},{8,40},{12,44},{16,48},{20,52},{24,56},{28,60},{32,6... | collective-permute-start | bytes 196616 | tf_op jit(solution)/shard_map/ppermute | solution.py:39
  43.2 11.9 %collective-permute-start.7 = (f32[128,128]{1,0:T(8,128)S(1)}, f32[128,128]{1,0:T(8,128)S(1)}, u32[]{:S(2)}, u32[]{:S(2)}) collective-permute-start(f32[128,128]{1,0:T(8,128)S(1)} %add_select_fusion.1), channel_id=1, source_target_pairs={{0,64},{4,68},{8,72},{12,76},{16,80},{20,84},{24,88},{28,92},{32,9... | collective-permute-start | bytes 196616 | tf_op jit(solution)/shard_map/ppermute | solution.py:39
  47.4 7.6 %collective-permute-start.8 = (f32[128,128]{1,0:T(8,128)S(1)}, f32[128,128]{1,0:T(8,128)S(1)}, u32[]{:S(2)}, u32[]{:S(2)}) collective-permute-start(f32[128,128]{1,0:T(8,128)S(1)} %add_select_fusion.1), channel_id=1, source_target_pairs={{0,96},{4,100},{8,104},{12,108},{16,112},{20,116},{24,120},{28,124... | collective-permute-start | bytes 196616 | tf_op jit(solution)/shard_map/ppermute | solution.py:39
  48.7 15.4 %collective-permute-start.1 = (bf16[256,1024]{1,0:T(8,128)(2,1)S(1)}, bf16[256,1024]{1,0:T(8,128)(2,1)S(1)}, u32[]{:S(2)}, u32[]{:S(2)}) collective-permute-start(bf16[256,1024]{1,0:T(8,128)(2,1)S(1)} %collective-permute-done.keys_1.k1), channel_id=1, source_target_pairs={{0,4},{4,8},{8,12},{12,16},{16,20},{20,24},{24,28},{28,32},{32,36}... | collective-permute-start | bytes 1572872 | tf_op jit(solution)/shard_map/ppermute | solution.py:29
  48.8 21.9 %collective-permute-start.14 = (bf16[256,1024]{1,0:T(8,128)(2,1)}, bf16[256,1024]{1,0:T(8,128)(2,1)S(1)}, u32[]{:S(2)}, u32[]{:S(2)}) collective-permute-start(bf16[256,1024]{1,0:T(8,128)(2,1)} %collective-permute-done.13.q1), channel_id=1, source_target_pairs={{0,124},{4,0},{8,4},{12,8},{16,12},{20,16},{24,20},{28,24},{32,28}... | collective-permute-start | bytes 1572872 | tf_op jit(solution)/shard_map/ppermute | solution.py:29
  55.0 20.1 %collective-permute-start.16 = (bf16[256,1024]{1,0:T(8,128)(2,1)}, bf16[256,1024]{1,0:T(8,128)(2,1)S(1)}, u32[]{:S(2)}, u32[]{:S(2)}) collective-permute-start(bf16[256,1024]{1,0:T(8,128)(2,1)} %collective-permute-done.15.d1), channel_id=1, source_target_pairs={{0,124},{4,0},{8,4},{12,8},{16,12},{20,16},{24,20},{28,24},{32,28}... | collective-permute-start | bytes 1572872 | tf_op jit(solution)/shard_map/ppermute | solution.py:29
  60.4 47.7 %collective-permute-start.9 = (bf16[256,1024]{1,0:T(8,128)(2,1)}, bf16[256,1024]{1,0:T(8,128)(2,1)}, u32[]{:S(2)}, u32[]{:S(2)}) collective-permute-start(bf16[256,1024]{1,0:T(8,128)(2,1)} %get-tuple-element.20.v0.values), channel_id=1, source_target_pairs={{0,4},{4,8},{8,12},{12,16},{16,20},{20,24},{24,28},{28,32},{32,36}... | collective-permute-start | bytes 1572872 | tf_op jit(solution)/shard_map/ppermute | solution.py:29
  68.0 7.1 %collective-permute-start.17 = (f32[8,256]{1,0:T(8,128)S(1)}, f32[8,256]{1,0:T(8,128)S(1)}, u32[]{:S(2)}, u32[]{:S(2)}) collective-permute-start(f32[8,256]{1,0:T(8,128)S(1)} %row_totals.1.totals.t0), channel_id=1, source_target_pairs={{0,124},{4,0},{8,4},{12,8},{16,12},{20,16},{24,20},{28,24},{32,28}... | collective-permute-start | bytes 24584 | tf_op jit(solution)/shard_map/ppermute | solution.py:29
  70.6 5.2 %collective-permute-start.18 = (f32[8,256]{1,0:T(8,128)S(1)}, f32[8,256]{1,0:T(8,128)S(1)}, u32[]{:S(2)}, u32[]{:S(2)}) collective-permute-start(f32[8,256]{1,0:T(8,128)S(1)} %row_totals.1.totals.t0), channel_id=1, source_target_pairs={{0,120},{4,124},{8,0},{12,4},{16,8},{20,12},{24,16},{28,20},{32,24... | collective-permute-start | bytes 24584 | tf_op jit(solution)/shard_map/ppermute | solution.py:29
  70.7 12.4 %copy-start.9 = (bf16[256,1024]{1,0:T(8,128)(2,1)}, bf16[256,1024]{1,0:T(8,128)(2,1)S(1)}, u32[]{:S(2)}) copy-start(bf16[256,1024]{1,0:T(8,128)(2,1)S(1)} %collective-permute-done.14.q2) | copy-start | bytes 1572868
  102.8 46.9 %copy-start.4 = (bf16[256,1024]{1,0:T(8,128)(2,1)S(1)}, bf16[256,1024]{1,0:T(8,128)(2,1)}, u32[]{:S(2)}) copy-start(bf16[256,1024]{1,0:T(8,128)(2,1)} %copy-done.3) | copy-start | bytes 1572868
  102.8 7.3 %collective-permute-start.21 = (f32[128,128]{1,0:T(8,128)S(1)}, f32[128,128]{1,0:T(8,128)S(1)}, u32[]{:S(2)}, u32[]{:S(2)}) collective-permute-start(f32[128,128]{1,0:T(8,128)S(1)} %get-tuple-element.29), channel_id=1, source_target_pairs={{0,12},{4,0},{8,4},{12,8},{16,28},{20,16},{24,20},{28,24},{32,44},... | collective-permute-start | bytes 196616 | tf_op jit(solution)/shard_map/ppermute | solution.py:39
  106.6 6.5 %collective-permute-start.22 = (f32[128,128]{1,0:T(8,128)S(1)}, f32[128,128]{1,0:T(8,128)S(1)}, u32[]{:S(2)}, u32[]{:S(2)}) collective-permute-start(f32[128,128]{1,0:T(8,128)S(1)} %get-tuple-element.29), channel_id=1, source_target_pairs={{0,8},{4,12},{8,0},{12,4},{16,24},{20,28},{24,16},{28,20},{32,40},... | collective-permute-start | bytes 196616 | tf_op jit(solution)/shard_map/ppermute | solution.py:39
  106.7 6.4 %collective-permute-start.23 = (f32[128,128]{1,0:T(8,128)S(1)}, f32[128,128]{1,0:T(8,128)S(1)}, u32[]{:S(2)}, u32[]{:S(2)}) collective-permute-start(f32[128,128]{1,0:T(8,128)S(1)} %get-tuple-element.29), channel_id=1, source_target_pairs={{0,4},{4,8},{8,12},{12,0},{16,20},{20,24},{24,28},{28,16},{32,36},... | collective-permute-start | bytes 196616 | tf_op jit(solution)/shard_map/ppermute | solution.py:39
  108.2 41.6 %collective-permute-start.10 = (bf16[256,1024]{1,0:T(8,128)(2,1)}, bf16[256,1024]{1,0:T(8,128)(2,1)}, u32[]{:S(2)}, u32[]{:S(2)}) collective-permute-start(bf16[256,1024]{1,0:T(8,128)(2,1)} %collective-permute-done.9.v1), channel_id=1, source_target_pairs={{0,4},{4,8},{8,12},{12,16},{16,20},{20,24},{24,28},{28,32},{32,36}... | collective-permute-start | bytes 1572872 | tf_op jit(solution)/shard_map/ppermute | solution.py:29
  113.7 12.7 %collective-permute-start.24 = (f32[128,128]{1,0:T(8,128)S(1)}, f32[128,128]{1,0:T(8,128)S(1)}, u32[]{:S(2)}, u32[]{:S(2)}) collective-permute-start(f32[128,128]{1,0:T(8,128)S(1)} %multiply_add_fusion.1), channel_id=1, source_target_pairs={{0,16},{4,20},{8,24},{12,28},{16,0},{20,4},{24,8},{28,12},{32,48},... | collective-permute-start | bytes 196616 | tf_op jit(solution)/shard_map/ppermute | solution.py:39
  127.1 38.4 %copy-start.10 = (bf16[256,1024]{1,0:T(8,128)(2,1)S(1)}, bf16[256,1024]{1,0:T(8,128)(2,1)}, u32[]{:S(2)}) copy-start(bf16[256,1024]{1,0:T(8,128)(2,1)} %copy-done.9) | copy-start | bytes 1572868
  127.1 47.7 %collective-permute-start.25 = (f32[128,128]{1,0:T(8,128)}, f32[128,128]{1,0:T(8,128)}, u32[]{:S(2)}, u32[]{:S(2)}) collective-permute-start(f32[128,128]{1,0:T(8,128)} %add_select_fusion), channel_id=1, source_target_pairs={{0,96},{4,100},{8,104},{12,108},{16,112},{20,116},{24,120},{28,124... | collective-permute-start | bytes 196616 | tf_op jit(solution)/shard_map/ppermute | solution.py:39
  130.0 44.8 %collective-permute-start.26 = (f32[128,128]{1,0:T(8,128)}, f32[128,128]{1,0:T(8,128)}, u32[]{:S(2)}, u32[]{:S(2)}) collective-permute-start(f32[128,128]{1,0:T(8,128)} %add_select_fusion), channel_id=1, source_target_pairs={{0,64},{4,68},{8,72},{12,76},{16,80},{20,84},{24,88},{28,92},{32,9... | collective-permute-start | bytes 196616 | tf_op jit(solution)/shard_map/ppermute | solution.py:39
  133.7 41.1 %collective-permute-start.27 = (f32[128,128]{1,0:T(8,128)}, f32[128,128]{1,0:T(8,128)}, u32[]{:S(2)}, u32[]{:S(2)}) collective-permute-start(f32[128,128]{1,0:T(8,128)} %add_select_fusion), channel_id=1, source_target_pairs={{0,32},{4,36},{8,40},{12,44},{16,48},{20,52},{24,56},{28,60},{32,6... | collective-permute-start | bytes 196616 | tf_op jit(solution)/shard_map/ppermute | solution.py:39
  133.7 7.9 %collective-permute-start.11 = (f32[8,256]{1,0:T(8,128)S(1)}, f32[8,256]{1,0:T(8,128)S(1)}, u32[]{:S(2)}, u32[]{:S(2)}) collective-permute-start(f32[8,256]{1,0:T(8,128)S(1)} %get-tuple-element.30.s0.squares), channel_id=1, source_target_pairs={{0,4},{4,8},{8,12},{12,16},{16,20},{20,24},{24,28},{28,32},{32,36}... | collective-permute-start | bytes 24584 | tf_op jit(solution)/shard_map/ppermute | solution.py:29
  141.6 8.2 %collective-permute-start.12 = (f32[8,256]{1,0:T(8,128)S(1)}, f32[8,256]{1,0:T(8,128)S(1)}, u32[]{:S(2)}, u32[]{:S(2)}) collective-permute-start(f32[8,256]{1,0:T(8,128)S(1)} %get-tuple-element.30.s0.squares), channel_id=1, source_target_pairs={{0,8},{4,12},{8,16},{12,20},{16,24},{20,28},{24,32},{28,36},{32,40... | collective-permute-start | bytes 24584 | tf_op jit(solution)/shard_map/ppermute | solution.py:29
  160.3 3.7 %collective-permute-start.19 = (f32[8,256]{1,0:T(8,128)S(1)}, f32[8,256]{1,0:T(8,128)S(1)}, u32[]{:S(2)}, u32[]{:S(2)}) collective-permute-start(f32[8,256]{1,0:T(8,128)S(1)} %get-tuple-element.24.e0), channel_id=1, source_target_pairs={{0,124},{4,0},{8,4},{12,8},{16,12},{20,16},{24,20},{28,24},{32,28}... | collective-permute-start | bytes 24584 | tf_op jit(solution)/shard_map/ppermute | solution.py:29
  160.3 5.2 %collective-permute-start.20 = (f32[8,256]{1,0:T(8,128)S(1)}, f32[8,256]{1,0:T(8,128)S(1)}, u32[]{:S(2)}, u32[]{:S(2)}) collective-permute-start(f32[8,256]{1,0:T(8,128)S(1)} %get-tuple-element.24.e0), channel_id=1, source_target_pairs={{0,120},{4,124},{8,0},{12,4},{16,8},{20,12},{24,16},{28,20},{32,24... | collective-permute-start | bytes 24584 | tf_op jit(solution)/shard_map/ppermute | solution.py:29
  (23 other events, 89.0 us)

commit v2 on v1

--- a/solution.py
+++ b/solution.py
@@ -16,8 +16,20 @@
 LANES = 128
 SUBLANES = 8
 ROWS_PER_STEP = 8
+HEADS_PER_STEP = 4
+GROUP = HEADS_PER_STEP * HEAD_DIM
 f32 = jnp.float32
 bf16 = jnp.bfloat16
+
+
+COST = 0.3
+
+
+def cost(microseconds):
+    microseconds = microseconds * COST
+    return pl.CostEstimate(
+        flops=int(microseconds * 1.0e9), bytes_accessed=int(microseconds * 2.0e6), transcendentals=0
+    )
 
 
 def params(*semantics):
@@ -58,9 +70,17 @@
     state = state + decayed(z, y == 1) * partner
     pair = jnp.where(y == 1, group + decayed(4) * partner, partner + decayed(4) * group)
     planes = [along(pair, 0, sign * d) for d in (1, 2, 3)]
-    for d, other in zip((1, 2, 3), planes):
-        state = state + decayed(position % 8 + 8 * (d - 1), d <= x) * other
-    return state
+    return (state, *planes)
+
+
+def add_planes(place, reverse, length, rates, start, planes, target):
+    position = (31 - place[0]) if reverse else place[0]
+    state = start[...]
+    for d, plane in zip((1, 2, 3), planes):
+        blocks = (position % 8 + 8 * (d - 1)).astype(f32)
+        factor = jnp.exp(-rates[...] * (blocks * length))
+        state = state + plane[...] * jnp.where(position >= 8 * d, factor, 0.0)
+    target[...] = state
 
 
 def to_tokens(scratch, head, rows, block):
@@ -132,24 +152,29 @@
         forward_state_kernel,
         out_shape=(small, small, big),
         compiler_params=params(),
+        cost_estimate=cost(2),
         name="forward_state",
     )(mixer, gate_in, rate)
 
 
 def row_total(block):
     ones = jnp.ones((SUBLANES, LANES), f32)
-    return lax.dot_general(
+    totals = lax.dot_general(
         ones, block, (((1,), (1,)), ((), ())), precision=lax.Precision.HIGHEST, preferred_element_type=f32
     )
-
-
-def forward_mix_kernel(drive, rates, residue, start, gate_out, gain, mixed, scaled, squares, residues, out):
+    return totals[0:1, :]
+
+
+def forward_mix_kernel(
+    place, drive, rates, residue, start, p1, p2, p3, gate_out, gain, mixed, scaled, squares, residues, out, carried
+):
     rows, width = mixed.shape
     modes = residue.shape[0]
     spread(residue, residues)
     decay = decays(rates, modes)
     res = [tile(residues, m) for m in range(modes)]
-    scan(drive, decay, res, [tile(start, m) for m in range(modes)], rows, out, False)
+    add_planes(place, False, rows, rates, start, (p1, p2, p3), carried)
+    scan(drive, decay, res, [tile(carried, m) for m in range(modes)], rows, out, False)
     total = jnp.zeros((rows, LANES), f32)
     for head in range(width // LANES):
         cut = head_slice(head)
@@ -160,7 +185,7 @@
     squares[...] = row_total(total)
 
 
-def forward_mix(drive, rates, residue, start, gate_out, gain):
+def forward_mix(place, drive, rates, residue, carry, gate_out, gain):
     rows, width = gate_out.shape
     modes = residue.shape[0]
     return pl.pallas_call(
@@ -168,30 +193,33 @@
         out_shape=(
             jax.ShapeDtypeStruct((rows, width), f32),
             jax.ShapeDtypeStruct((rows, width), bf16),
-            jax.ShapeDtypeStruct((SUBLANES, rows), f32),
+            jax.ShapeDtypeStruct((1, rows), f32),
         ),
         scratch_shapes=[
             pltpu.VMEM((modes * SUBLANES, LANES), f32),
             pltpu.VMEM((rows * SUBLANES, LANES), f32),
+            pltpu.VMEM((modes * SUBLANES, LANES), f32),
         ],
+        in_specs=[pl.BlockSpec(memory_space=pltpu.SMEM)] + [pl.BlockSpec(memory_space=pltpu.VMEM)] * 9,
         compiler_params=params(),
+        cost_estimate=cost(4),
         name="forward_mix",
-    )(drive, rates, residue, start, gate_out, gain)
-
-
-def column(rows_ref):
-    return jnp.transpose(rows_ref[...])[:, 0:1]
+    )(place, drive, rates, residue, *carry, gate_out, gain)
+
+
+def column(row):
+    return jnp.transpose(jnp.broadcast_to(row, (SUBLANES, row.shape[1])))[:, 0:1]
 
 
 def inverse_of(squares, full_width):
     return lax.rsqrt(squares * (1.0 / full_width) + EPS)
 
 
-def backward_state_kernel(full_width, scaled, mixed, gate_out, squares, inner, rates, final, drive):
+def backward_state_kernel(full_width, scaled, mixed, gate_out, stats, rates, final, drive):
     rows, width = mixed.shape
     modes = rates.shape[0] // SUBLANES
-    inverse = inverse_of(column(squares), full_width)
-    pull = inverse * inverse * inverse * column(inner) * (1.0 / full_width)
+    inverse = inverse_of(column(stats[0:1, :]), full_width)
+    pull = inverse * inverse * inverse * column(stats[1:2, :]) * (1.0 / full_width)
     for head in range(width // LANES):
         cut = head_slice(head)
         grad = inverse * scaled[:, cut] - mixed[:, cut] * pull
@@ -202,7 +230,7 @@
         final[m * SUBLANES : (m + 1) * SUBLANES, :] = state[m]
 
 
-def backward_state(full_width, scaled, mixed, gate_out, squares, inner, rates):
+def backward_state(full_width, scaled, mixed, gate_out, stats, rates):
     rows, width = mixed.shape
     return pl.pallas_call(
         functools.partial(backward_state_kernel, full_width),
@@ -211,23 +239,25 @@
             jax.ShapeDtypeStruct((rows * SUBLANES, LANES), f32),
         ),
         compiler_params=params(),
+        cost_estimate=cost(2),
         name="backward_state",
-    )(scaled, mixed, gate_out, squares, inner, rates)
-
-
-def backward_mix_kernel(drive, rates, residue, start, gate_in, grad, residues, out):
+    )(scaled, mixed, gate_out, stats, rates)
+
+
+def backward_mix_kernel(place, drive, rates, residue, start, p1, p2, p3, gate_in, grad, residues, out, carried):
     rows, width = gate_in.shape
     modes = residue.shape[0]
     spread(residue, residues)
     decay = decays(rates, modes)
     res = [tile(residues, m) for m in range(modes)]
-    scan(drive, decay, res, [tile(start, m) for m in range(modes)], rows, out, True)
+    add_planes(place, True, rows, rates, start, (p1, p2, p3), carried)
+    scan(drive, decay, res, [tile(carried, m) for m in range(modes)], rows, out, True)
     for head in range(width // LANES):
         cut = head_slice(head)
         grad[:, cut] = (gate_in[:, cut].astype(f32) * from_tokens(out, head, rows)).astype(bf16)
 
 
-def backward_mix(drive, rates, residue, start, gate_in):
+def backward_mix(place, drive, rates, residue, carry, gate_in):
     rows, width = gate_in.shape
     modes = residue.shape[0]
     return pl.pallas_call(
@@ -236,10 +266,13 @@
         scratch_shapes=[
             pltpu.VMEM((modes * SUBLANES, LANES), f32),
             pltpu.VMEM((rows * SUBLANES, LANES), f32),
+            pltpu.VMEM((modes * SUBLANES, LANES), f32),
         ],
+        in_specs=[pl.BlockSpec(memory_space=pltpu.SMEM)] + [pl.BlockSpec(memory_space=pltpu.VMEM)] * 8,
         compiler_params=params(),
+        cost_estimate=cost(4),
         name="backward_mix",
-    )(drive, rates, residue, start, gate_in)
+    )(place, drive, rates, residue, *carry, gate_in)
 
 
 def rows_by_rows(a, b):
@@ -262,28 +295,35 @@
 SCALE = 1.0 / math.sqrt(HEAD_DIM)
 
 
+def step_heads():
+    first = pl.program_id(0) * HEADS_PER_STEP
+    return [(first + j, head_slice(j)) for j in range(HEADS_PER_STEP)]
+
+
 def totals_kernel(place, queries, keys, keys_1, keys_2, totals):
-    head = pl.program_id(0)
     position = place[0]
-    scores = [
-        masked(rows_by_rows(block[...], queries[...]) * (SCALE * LOG2E), offset, position >= offset, True)
-        for offset, block in enumerate((keys, keys_1, keys_2))
-    ]
-    top = functools.reduce(jnp.maximum, [jnp.max(s, axis=0, keepdims=True) for s in scores])
-    total = sum(jnp.sum(jnp.exp2(s - top), axis=0, keepdims=True) for s in scores)
-    totals[pl.ds(head, 1), :] = top + jnp.log(total) * LOG2E
-
-
-def head_block(rows, part=0):
-    return pl.BlockSpec((rows, HEAD_DIM), lambda head, *_: (part, head))
+    for head, cut in step_heads():
+        scores = [
+            masked(
+                rows_by_rows(block[:, cut], queries[:, cut]) * (SCALE * LOG2E), offset, position >= offset, True
+            )
+            for offset, block in enumerate((keys, keys_1, keys_2))
+        ]
+        top = functools.reduce(jnp.maximum, [jnp.max(s, axis=0, keepdims=True) for s in scores])
+        total = sum(jnp.sum(jnp.exp2(s - top), axis=0, keepdims=True) for s in scores)
+        totals[pl.ds(head, 1), :] = top + jnp.log(total) * LOG2E
+
+
+def head_block(rows):
+    return pl.BlockSpec((rows, GROUP), lambda step, *_: (0, step))
 
 
 def whole(shape):
     return pl.BlockSpec(shape, lambda head, *_: (0,) * len(shape))
 
 
-def per_head(kernel, place, operands, specs, out_shape, out_specs, scratch=(), name=None):
-    heads = operands[0].shape[1] // HEAD_DIM
+def per_head(kernel, place, operands, specs, out_shape, out_specs, scratch=(), name=None, time=5):
+    heads = operands[0].shape[1] // GROUP
     return pl.pallas_call(
         kernel,
         out_shape=out_shape,
@@ -295,6 +335,7 @@
             scratch_shapes=scratch,
         ),
         compiler_params=params("arbitrary"),
+        cost_estimate=cost(time),
         name=name,
     )(place, *operands)
 
@@ -311,36 +352,39 @@
         jax.ShapeDtypeStruct(shape, f32),
         whole(shape),
         name="row_totals",
+        time=4,
     )
 
 
 def value_grads_kernel(
-    blocks, place, keys, q0, q1, q2, d0, d1, d2, t0, t1, t2, gain, mixed, scaled, inner, acc
+    blocks, place, keys, q0, q1, q2, d0, d1, d2, t0, t1, t2, gain, mixed, squares, scaled, stats, acc
 ):
-    head = pl.program_id(0)
+    step = pl.program_id(0)
     position = place[0]
-    grad = None
-    for offset, (query, cotangent, total) in enumerate(((q0, d0, t0), (q1, d1, t1), (q2, d2, t2))):
-        scores = rows_by_rows(keys[...], query[...]) * (SCALE * LOG2E)
-        scores = masked(scores, offset, position + offset < blocks, True)
-        probs = jnp.exp2(scores - total[pl.ds(head, 1), :])
-        part = product(probs.astype(bf16), cotangent[...])
-        grad = part if grad is None else grad + part
-    value = grad * gain[...]
-    scaled[...] = value
-
-    @pl.when(head == 0)
+
+    @pl.when(step == 0)
     def _():
         acc[...] = jnp.zeros_like(acc)
 
-    acc[...] += value * mixed[...]
-
-    @pl.when(head == pl.num_programs(0) - 1)
+    for head, cut in step_heads():
+        grad = None
+        for offset, (query, cotangent, total) in enumerate(((q0, d0, t0), (q1, d1, t1), (q2, d2, t2))):
+            scores = rows_by_rows(keys[:, cut], query[:, cut]) * (SCALE * LOG2E)
+            scores = masked(scores, offset, position + offset < blocks, True)
+            probs = jnp.exp2(scores - total[pl.ds(head, 1), :])
+            part = product(probs.astype(bf16), cotangent[:, cut])
+            grad = part if grad is None else grad + part
+        value = grad * gain[:, cut]
+        scaled[:, cut] = value
+        acc[...] += value * mixed[:, cut]
+
+    @pl.when(step == pl.num_programs(0) - 1)
     def _():
-        inner[...] = row_total(acc[...])
-
-
-def value_grads(blocks, place, keys, queries, cotangents, totals, gain, mixed):
+        stats[0:1, :] = squares[...]
+        stats[1:2, :] = row_total(acc[...])
+
+
+def value_grads(blocks, place, keys, queries, cotangents, totals, gain, mixed, squares):
     rows, width = keys.shape
     heads = width // HEAD_DIM
     block = head_block(rows)
@@ -348,50 +392,50 @@
     return per_head(
         functools.partial(value_grads_kernel, blocks),
         place,
-        (keys, *queries, *cotangents, *totals, gain, mixed),
-        [block] * 7 + [stat] * 3 + [head_block(1), block],
-        (jax.ShapeDtypeStruct((rows, width), f32), jax.ShapeDtypeStruct((SUBLANES, rows), f32)),
-        (block, whole((SUBLANES, rows))),
+        (keys, *queries, *cotangents, *totals, gain, mixed, squares),
+        [block] * 7 + [stat] * 3 + [head_block(1), block, whole((1, rows))],
+        (jax.ShapeDtypeStruct((rows, width), f32), jax.ShapeDtypeStruct((2, rows), f32)),
+        (block, whole((2, rows))),
         scratch=[pltpu.VMEM((rows, LANES), f32)],
         name="value_grads",
+        time=7,
     )
 
 
 def attend_kernel(
     full_width, place, queries, cotangent, k0, k1, k2, v0, v1, v2, s0, s1, s2, totals, attended, grad, delta, columns
 ):
-    head = pl.program_id(0)
     position = place[0]
 
-    @pl.when(head == 0)
+    @pl.when(pl.program_id(0) == 0)
     def _():
         columns[...] = jnp.transpose(totals[...])
 
     lane = lax.broadcasted_iota(jnp.int32, columns.shape, 1)
-    log_total = jnp.sum(jnp.where(lane == head, columns[...], 0.0), axis=1, keepdims=True)
-    probs, inverses = [], []
-    output = None
-    for offset, (key, value, squares) in enumerate(((k0, v0, s0), (k1, v1, s1), (k2, v2, s2))):
-        scores = rows_by_rows(queries[...], key[...]) * (SCALE * LOG2E)
-        scores = masked(scores, offset, position >= offset, False)
-        prob = jnp.exp2(scores - log_total)
-        inverse = inverse_of(squares[0:1, :], full_width)
-        probs.append(prob)
-        inverses.append(inverse)
-        part = product((prob * inverse).astype(bf16), value[...])
-        output = part if output is None else output + part
-    result = output.astype(bf16)
-    attended[...] = result
-    weighed = cotangent[...].astype(f32) * result.astype(f32)
-    delta[pl.ds(head, 1), :] = row_total(weighed)[0:1, :]
-    delta_column = jnp.sum(weighed, axis=1, keepdims=True)
-    total = None
-    for prob, inverse, key, value in zip(probs, inverses, (k0, k1, k2), (v0, v1, v2)):
-        dprob = rows_by_rows(cotangent[...], value[...]) * inverse
-        dscore = (prob * (dprob - delta_column)).astype(bf16)
-        part = product(dscore, key[...])
-        total = part if total is None else total + part
-    grad[...] = (total * SCALE).astype(bf16)
+    inverses = [inverse_of(squares[0:1, :], full_width) for squares in (s0, s1, s2)]
+    for head, cut in step_heads():
+        log_total = jnp.sum(jnp.where(lane == head, columns[...], 0.0), axis=1, keepdims=True)
+        probs = []
+        output = None
+        for offset, (key, value) in enumerate(((k0, v0), (k1, v1), (k2, v2))):
+            scores = rows_by_rows(queries[:, cut], key[:, cut]) * (SCALE * LOG2E)
+            scores = masked(scores, offset, position >= offset, False)
+            prob = jnp.exp2(scores - log_total)
+            probs.append(prob)
+            part = product((prob * inverses[offset]).astype(bf16), value[:, cut])
+            output = part if output is None else output + part
+        result = output.astype(bf16)
+        attended[:, cut] = result
+        weighed = cotangent[:, cut].astype(f32) * result.astype(f32)
+        delta[pl.ds(head, 1), :] = row_total(weighed)
+        delta_column = jnp.sum(weighed, axis=1, keepdims=True)
+        total = None
+        for prob, inverse, key, value in zip(probs, inverses, (k0, k1, k2), (v0, v1, v2)):
+            dprob = rows_by_rows(cotangent[:, cut], value[:, cut]) * inverse
+            dscore = (prob * (dprob - delta_column)).astype(bf16)
+            part = product(dscore, key[:, cut])
+            total = part if total is None else total + part
+        grad[:, cut] = (total * SCALE).astype(bf16)
 
 
 def attend(full_width, place, queries, cotangent, keys, values, squares, totals):
@@ -404,31 +448,32 @@
         functools.partial(attend_kernel, full_width),
         place,
         (queries, cotangent, *keys, *values, *squares, totals),
-        [block] * 8 + [whole((SUBLANES, rows))] * 3 + [stat],
+        [block] * 8 + [whole((2, rows))] * 3 + [stat],
         (out, out, jax.ShapeDtypeStruct((heads, rows), f32)),
         (block, block, stat),
         scratch=[pltpu.VMEM((rows, heads), f32)],
         name="attend",
+        time=10,
     )
 
 
 def key_grads_kernel(
     full_width, blocks, place, keys, values, q0, q1, q2, d0, d1, d2, t0, t1, t2, e0, e1, e2, squares, grad
 ):
-    head = pl.program_id(0)
     position = place[0]
-    inverse = inverse_of(column(squares), full_width)
-    total = None
+    inverse = inverse_of(column(squares[0:1, :]), full_width)
     groups = ((q0, d0, t0, e0), (q1, d1, t1, e1), (q2, d2, t2, e2))
-    for offset, (query, cotangent, log_total, delta) in enumerate(groups):
-        scores = rows_by_rows(keys[...], query[...]) * (SCALE * LOG2E)
-        scores = masked(scores, offset, position + offset < blocks, True)
-        probs = jnp.exp2(scores - log_total[pl.ds(head, 1), :])
-        dprob = rows_by_rows(values[...], cotangent[...]) * inverse
-        dscore = (probs * (dprob - delta[pl.ds(head, 1), :])).astype(bf16)
-        part = product(dscore, query[...])
-        total = part if total is None else total + part
-    grad[...] = (total * SCALE).astype(bf16)
+    for head, cut in step_heads():
+        total = None
+        for offset, (query, cotangent, log_total, delta) in enumerate(groups):
+            scores = rows_by_rows(keys[:, cut], query[:, cut]) * (SCALE * LOG2E)
+            scores = masked(scores, offset, position + offset < blocks, True)
+            probs = jnp.exp2(scores - log_total[pl.ds(head, 1), :])
+            dprob = rows_by_rows(values[:, cut], cotangent[:, cut]) * inverse
+            dscore = (probs * (dprob - delta[pl.ds(head, 1), :])).astype(bf16)
+            part = product(dscore, query[:, cut])
+            total = part if total is None else total + part
+        grad[:, cut] = (total * SCALE).astype(bf16)
 
 
 def key_grads(full_width, blocks, place, keys, values, queries, cotangents, totals, deltas, squares):
@@ -440,10 +485,11 @@
         functools.partial(key_grads_kernel, full_width, blocks),
         place,
         (keys, values, *queries, *cotangents, *totals, *deltas, squares),
-        [block] * 8 + [stat] * 6 + [whole((SUBLANES, rows))],
+        [block] * 8 + [stat] * 6 + [whole((2, rows))],
         jax.ShapeDtypeStruct((rows, width), bf16),
         block,
         name="key_grads",
+        time=8,
     )
 
 
@@ -465,13 +511,10 @@
     cotangent_2 = shifted(cotangent_1, -1)
 
     final, rates, drive = forward_state(mixer_input, gate_in, jnp.transpose(decay_rate))
-    start = carry_in(final, rates, length, False)
-    mixed, scaled_mix, squares = forward_mix(drive, rates, residue, start, gate_out, gain)
+    carry = carry_in(final, rates, length, False)
+    mixed, scaled_mix, squares = forward_mix(place, drive, rates, residue, carry, gate_out, gain)
     mix_1 = shifted(scaled_mix, 1)
     mix_2 = shifted(mix_1, 1)
-    squares = lax.psum(squares, "tp")
-    squares_1 = shifted(squares, 1)
-    squares_2 = shifted(squares, 2)
 
     totals = row_totals(place, queries, key_vectors, keys_1, keys_2)
     totals_1 = shifted(totals, -1)
@@ -479,13 +522,15 @@
     all_queries = (queries, queries_1, queries_2)
     all_cotangents = (grad_out, cotangent_1, cotangent_2)
     all_totals = (totals, totals_1, totals_2)
-    scaled, inner = value_grads(
-        blocks, place, key_vectors, all_queries, all_cotangents, all_totals, gain, mixed
-    )
-    inner = lax.psum(inner, "tp")
-    final, drive = backward_state(full_width, scaled, mixed, gate_out, squares, inner, rates)
-    start = carry_in(final, rates, length, True)
-    grad_input = backward_mix(drive, rates, residue, start, gate_in)
+    scaled, stats = value_grads(
+        blocks, place, key_vectors, all_queries, all_cotangents, all_totals, gain, mixed, squares
+    )
+    stats = lax.psum(stats, "tp")
+    stats_1 = shifted(stats, 1)
+    stats_2 = shifted(stats, 2)
+    final, drive = backward_state(full_width, scaled, mixed, gate_out, stats, rates)
+    carry = carry_in(final, rates, length, True)
+    grad_input = backward_mix(place, drive, rates, residue, carry, gate_in)
 
     attended, grad_queries, delta = attend(
         full_width,
@@ -494,7 +539,7 @@
         grad_out,
         (key_vectors, keys_1, keys_2),
         (scaled_mix, mix_1, mix_2),
-        (squares, squares_1, squares_2),
+        (stats, stats_1, stats_2),
         totals,
     )
     all_deltas = (delta, shifted(delta, -1), shifted(delta, -2))
@@ -508,7 +553,7 @@
         all_cotangents,
         all_totals,
         all_deltas,
-        squares,
+        stats,
     )
     return (attended, grad_queries, grad_keys, grad_input)
 

time: 181 us -> 137 us (0.76)
  waiting for transfers between devices: 57.1 us -> 43.1 us
  starting transfers between devices: 53.8 us -> 41.6 us
  Pallas kernels: 39.9 us -> 33.2 us
  blocking collectives: 13.8 us -> 7.17 us
    ppermute x14, starting transfers between devices: 34.7 us -> 20.1 us  [along(): return lax.ppermute(value, 'ctx', [(i, target(i)) for i in range(32)])]
    ppermute x14, waiting for transfers between devices: 28 us -> 16.1 us  [shifted(): lax.ppermute(value, 'ctx', [(i, (i + by) % devices) for i in range(device...]
    psum x1, blocking collectives: 13.8 us -> 7.17 us  [shards(): stats = lax.psum(stats, 'tp')]
    pallas_call x4, Pallas kernels: 29.9 us -> 23.8 us  [per_head(): pl.pallas_call(kernel, out_shape=out_shape, grid_spec=pltpu.PrefetchScala...]
    ppermute x14, starting transfers between devices: 19.2 us -> 21.5 us  [shifted(): lax.ppermute(value, 'ctx', [(i, (i + by) % devices) for i in range(device...]
    ppermute x14, waiting for transfers between devices: 29.2 us -> 27 us  [along(): return lax.ppermute(value, 'ctx', [(i, target(i)) for i in range(32)])]
  transfers between devices with their start and end apart: 28 -> 28, of which waited for: 11 -> 16; matrix products, arithmetic and copies ran while one was open for 0% -> 0% of each run, Pallas kernels for 19% -> 21%
where the time goes in v2:
time: 137 us; the launch traced here: 136 us
  waiting for transfers between devices  43.1 us (31%)
  starting transfers between devices  41.6 us (30%)
  Pallas kernels  33.2 us (24%)
  local copies, waits for them, and re-layouts  10.1 us (7%)
  blocking collectives  7.17 us (5%)
    ppermute x14, waiting for transfers between devices, along(): return lax.ppermute(value, 'ctx', [(i, target(i)) for i in range(32)])  27 us
    pallas_call x4, Pallas kernels, per_head(): pl.pallas_call(kernel, out_shape=out_shape, grid_spec=pltpu.PrefetchScala...  23.8 us
    ppermute x14, starting transfers between devices, shifted(): lax.ppermute(value, 'ctx', [(i, (i + by) % devices) for i in range(device...  21.5 us
    ppermute x14, starting transfers between devices, along(): return lax.ppermute(value, 'ctx', [(i, target(i)) for i in range(32)])  20.1 us
    ppermute x14, waiting for transfers between devices, shifted(): lax.ppermute(value, 'ctx', [(i, (i + by) % devices) for i in range(device...  16.1 us
    unnamed x54, local copies, waits for them, and re-layouts  10.1 us
    psum x1, blocking collectives, shards(): stats = lax.psum(stats, 'tp')  7.17 us
    pallas_call x1, Pallas kernels, backward_mix(): pl.pallas_call(backward_mix_kernel, out_shape=jax.ShapeDtypeStruct((rows,...  3.44 us
  transfers between devices with their start and end apart: 28, of which 16 were waited for; matrix products, arithmetic and copies ran while one was open for 0% of the time, Pallas kernels for 21%

profile of v2, /device:TPU:0, one launch (start us, length us, event | category | flops | bytes accessed | tf_op | source)
XLA Modules:
  0.0 136.2 jit_solution(14693797591663432312)
XLA Ops:
  3.6 1.5 %forward_state.1 = (f32[128,128]{1,0:T(8,128)S(1)}, f32[128,128]{1,0:T(8,128)S(1)}, f32[2048,128]{1,0:T(8,128)S(1)}) custom-call(bf16[256,1024]{1,0:T(8,128)(2,1)S(1)} %copy-done.3, bf16[256,1024]{1,0:T(8,128)(2,1)S(1)} %copy-done.11, f32[16,1024]{1,0:T(8,128)S(1)} %bitcast.4), custom_call_target="tpu_custom_call" | custom-call | flops 600000000 | bytes 1200000 | tf_op jit(solution)/shard_map/forward_state/pallas_call | solution.py:151
  6.1 2.0 %collective-permute-start.2 = (f32[128,128]{1,0:T(8,128)S(1)}, f32[128,128]{1,0:T(8,128)S(1)}, u32[]{:S(2)}, u32[]{:S(2)}) collective-permute-start(f32[128,128]{1,0:T(8,128)S(1)} %get-tuple-element.19), channel_id=1, source_target_pairs={{0,4},{4,8},{8,12},{12,0},{16,20},{20,24},{24,28},{28,16},{32,36},... | collective-permute-start | bytes 196616 | tf_op jit(solution)/shard_map/ppermute | solution.py:51
  8.1 3.6 %collective-permute-start.3 = (f32[128,128]{1,0:T(8,128)S(1)}, f32[128,128]{1,0:T(8,128)S(1)}, u32[]{:S(2)}, u32[]{:S(2)}) collective-permute-start(f32[128,128]{1,0:T(8,128)S(1)} %get-tuple-element.19), channel_id=1, source_target_pairs={{0,8},{4,12},{8,0},{12,4},{16,24},{20,28},{24,16},{28,20},{32,40},... | collective-permute-start | bytes 196616 | tf_op jit(solution)/shard_map/ppermute | solution.py:51
  13.8 2.1 %collective-permute-done.3 = f32[128,128]{1,0:T(8,128)S(1)} collective-permute-done((f32[128,128]{1,0:T(8,128)S(1)}, f32[128,128]{1,0:T(8,128)S(1)}, u32[]{:S(2)}, u32[]{:S(2)}) %collective-permute-start.3) | collective-permute-done | bytes 65568 | tf_op jit(solution)/shard_map/ppermute | solution.py:51
  16.0 1.7 %collective-permute-start.5 = (f32[128,128]{1,0:T(8,128)S(1)}, f32[128,128]{1,0:T(8,128)S(1)}, u32[]{:S(2)}, u32[]{:S(2)}) collective-permute-start(f32[128,128]{1,0:T(8,128)S(1)} %multiply_add_fusion.3), channel_id=1, source_target_pairs={{0,16},{4,20},{8,24},{12,28},{16,0},{20,4},{24,8},{28,12},{32,48},... | collective-permute-start | bytes 196616 | tf_op jit(solution)/shard_map/ppermute | solution.py:51
  17.7 4.3 %collective-permute-start.11 = (bf16[256,1024]{1,0:T(8,128)(2,1)S(1)}, bf16[256,1024]{1,0:T(8,128)(2,1)}, u32[]{:S(2)}, u32[]{:S(2)}) collective-permute-start(bf16[256,1024]{1,0:T(8,128)(2,1)S(1)} %copy-done.4), channel_id=1, source_target_pairs={{0,124},{4,0},{8,4},{12,8},{16,12},{20,16},{24,20},{28,24},{32,28}... | collective-permute-start | bytes 1572872 | tf_op jit(solution)/shard_map/ppermute | solution.py:41
  22.5 16.9 %collective-permute-done.5 = f32[128,128]{1,0:T(8,128)S(1)} collective-permute-done((f32[128,128]{1,0:T(8,128)S(1)}, f32[128,128]{1,0:T(8,128)S(1)}, u32[]{:S(2)}, u32[]{:S(2)}) %collective-permute-start.5) | collective-permute-done | bytes 65568 | tf_op jit(solution)/shard_map/ppermute | solution.py:51
  39.5 1.6 %collective-permute-start.6 = (f32[128,128]{1,0:T(8,128)S(1)}, f32[128,128]{1,0:T(8,128)S(1)}, u32[]{:S(2)}, u32[]{:S(2)}) collective-permute-start(f32[128,128]{1,0:T(8,128)S(1)} %get-tuple-element.32), channel_id=1, source_target_pairs={{0,32},{4,36},{8,40},{12,44},{16,48},{20,52},{24,56},{28,60},{32,6... | collective-permute-start | bytes 196616 | tf_op jit(solution)/shard_map/ppermute | solution.py:51
  41.1 1.6 %collective-permute-start.7 = (f32[128,128]{1,0:T(8,128)S(1)}, f32[128,128]{1,0:T(8,128)S(1)}, u32[]{:S(2)}, u32[]{:S(2)}) collective-permute-start(f32[128,128]{1,0:T(8,128)S(1)} %get-tuple-element.32), channel_id=1, source_target_pairs={{0,64},{4,68},{8,72},{12,76},{16,80},{20,84},{24,88},{28,92},{32,9... | collective-permute-start | bytes 196616 | tf_op jit(solution)/shard_map/ppermute | solution.py:51
  42.7 2.4 %collective-permute-done.6.p1 = f32[128,128]{1,0:T(8,128)S(1)} collective-permute-done((f32[128,128]{1,0:T(8,128)S(1)}, f32[128,128]{1,0:T(8,128)S(1)}, u32[]{:S(2)}, u32[]{:S(2)}) %collective-permute-start.6) | collective-permute-done | bytes 65568 | tf_op jit(solution)/shard_map/ppermute | solution.py:51
  45.4 1.4 %collective-permute-done.7.p2 = f32[128,128]{1,0:T(8,128)S(1)} collective-permute-done((f32[128,128]{1,0:T(8,128)S(1)}, f32[128,128]{1,0:T(8,128)S(1)}, u32[]{:S(2)}, u32[]{:S(2)}) %collective-permute-start.7) | collective-permute-done | bytes 65568 | tf_op jit(solution)/shard_map/ppermute | solution.py:51
  46.8 2.5 %collective-permute-done.8.p3 = f32[128,128]{1,0:T(8,128)S(1)} collective-permute-done((f32[128,128]{1,0:T(8,128)S(1)}, f32[128,128]{1,0:T(8,128)S(1)}, u32[]{:S(2)}, u32[]{:S(2)}) %collective-permute-start.8) | collective-permute-done | bytes 65568 | tf_op jit(solution)/shard_map/ppermute | solution.py:51
  51.2 2.7 %forward_mix.1 = (f32[256,1024]{1,0:T(8,128)S(1)}, bf16[256,1024]{1,0:T(8,128)(2,1)S(1)}, f32[1,256]{1,0:T(1,128)S(1)}) custom-call(s32[1]{0:T(128)} %bitcast.place, f32[2048,128]{1,0:T(8,128)S(1)} %copy-done.26, f32[128,128]{1,0:T(8,128)S(1)} %get-tuple-element.18.rates, f32[16,1024]{1,0:T(8,128)S(1)} %bitcast.5, f32[128,128]{1,0:T(8,128)S(1)} %get-tuple-element.33.start, ...), custom_call_target="tpu_custom_call" | custom-call | flops 1200000000 | bytes 2400000 | tf_op jit(solution)/shard_map/forward_mix/pallas_call | solution.py:191
  54.1 6.2 %collective-permute-start.12 = (bf16[256,1024]{1,0:T(8,128)(2,1)}, bf16[256,1024]{1,0:T(8,128)(2,1)S(1)}, u32[]{:S(2)}, u32[]{:S(2)}) collective-permute-start(bf16[256,1024]{1,0:T(8,128)(2,1)} %collective-permute-done.11.q1), channel_id=1, source_target_pairs={{0,124},{4,0},{8,4},{12,8},{16,12},{20,16},{24,20},{28,24},{32,28}... | collective-permute-start | bytes 1572872 | tf_op jit(solution)/shard_map/ppermute | solution.py:41
  60.4 4.0 %collective-permute-done.1.keys_2.k2 = bf16[256,1024]{1,0:T(8,128)(2,1)S(1)} collective-permute-done((bf16[256,1024]{1,0:T(8,128)(2,1)}, bf16[256,1024]{1,0:T(8,128)(2,1)S(1)}, u32[]{:S(2)}, u32[]{:S(2)}) %collective-permute-start.1) | collective-permute-done | bytes 524320 | tf_op jit(solution)/shard_map/ppermute | solution.py:41
  64.5 3.2 %row_totals.1.t0.totals = f32[8,256]{1,0:T(8,128)S(1)} custom-call(s32[1]{0:T(128)} %bitcast.place, bf16[256,1024]{1,0:T(8,128)(2,1)S(1)} %copy-done.4, bf16[256,1024]{1,0:T(8,128)(2,1)S(1)} %copy-done.8, bf16[256,1024]{1,0:T(8,128)(2,1)} %collective-permute-done.keys_1.k1, bf16[256,1024]{1,0:T(8,128)(2,1)S(1)} %collective-permute-done.1.keys_2.k2), custom_call_target="tpu_custom_call" | custom-call | flops 1200000000 | bytes 2400000 | tf_op jit(solution)/shard_map/row_totals/pallas_call | solution.py:327
  68.7 1.8 %collective-permute-done.9.v1 = bf16[256,1024]{1,0:T(8,128)(2,1)} collective-permute-done((bf16[256,1024]{1,0:T(8,128)(2,1)S(1)}, bf16[256,1024]{1,0:T(8,128)(2,1)}, u32[]{:S(2)}, u32[]{:S(2)}) %collective-permute-start.9) | collective-permute-done | bytes 524320 | tf_op jit(solution)/shard_map/ppermute | solution.py:41
  70.5 5.5 %collective-permute-done.14.d2 = bf16[256,1024]{1,0:T(8,128)(2,1)S(1)} collective-permute-done((bf16[256,1024]{1,0:T(8,128)(2,1)}, bf16[256,1024]{1,0:T(8,128)(2,1)S(1)}, u32[]{:S(2)}, u32[]{:S(2)}) %collective-permute-start.14) | collective-permute-done | bytes 524320 | tf_op jit(solution)/shard_map/ppermute | solution.py:41
  76.0 5.2 %value_grads.1 = (f32[256,1024]{1,0:T(8,128)S(1)}, f32[2,256]{1,0:T(2,128)S(1)}) custom-call(s32[1]{0:T(128)} %bitcast.place, bf16[256,1024]{1,0:T(8,128)(2,1)S(1)} %copy-done.9, bf16[256,1024]{1,0:T(8,128)(2,1)S(1)} %copy-done.4, bf16[256,1024]{1,0:T(8,128)(2,1)} %collective-permute-done.11.q1, bf16[256,1024]{1,0:T(8,128)(2,1)S(1)} %collective-permute-done.12.q2, ...), custom_call_target="tpu_custom_call" | custom-call | flops 2100000000 | bytes 4200000 | tf_op jit(solution)/shard_map/value_grads/pallas_call | solution.py:327
  81.2 7.2 %psum.7.s0.squares.stats = f32[2,256]{1,0:T(2,128)S(1)} all-reduce(f32[2,256]{1,0:T(2,128)S(1)} %get-tuple-element.23), channel_id=1, replica_groups=mesh['ctx'=32,'tp'=4] {'tp'}, use_global_device_ids=true, to_apply=%region_0.1 | all-reduce | flops 512 | bytes 4096 | tf_op jit(solution)/shard_map/psum | solution.py:528
  88.4 1.6 %backward_state.1 = (f32[128,128]{1,0:T(8,128)S(1)}, f32[2048,128]{1,0:T(8,128)S(1)}) custom-call(f32[256,1024]{1,0:T(8,128)S(1)} %get-tuple-element.27.scaled, f32[256,1024]{1,0:T(8,128)S(1)} %get-tuple-element.21.mixed, bf16[256,1024]{1,0:T(8,128)(2,1)S(1)} %copy-done, f32[2,256]{1,0:T(2,128)S(1)} %psum.7.s0.squares.stats, ...), custom_call_target="tpu_custom_call" | custom-call | flops 600000000 | bytes 1200000 | tf_op jit(solution)/shard_map/backward_state/pallas_call | solution.py:235
  92.1 1.4 %collective-permute-start.23 = (f32[128,128]{1,0:T(8,128)S(1)}, f32[128,128]{1,0:T(8,128)S(1)}, u32[]{:S(2)}, u32[]{:S(2)}) collective-permute-start(f32[128,128]{1,0:T(8,128)S(1)} %get-tuple-element.29), channel_id=1, source_target_pairs={{0,4},{4,8},{8,12},{12,0},{16,20},{20,24},{24,28},{28,16},{32,36},... | collective-permute-start | bytes 196616 | tf_op jit(solution)/shard_map/ppermute | solution.py:51
  93.5 1.7 %collective-permute-start.17 = (f32[2,256]{1,0:T(2,128)S(1)}, f32[2,256]{1,0:T(2,128)S(1)}, u32[]{:S(2)}, u32[]{:S(2)}) collective-permute-start(f32[2,256]{1,0:T(2,128)S(1)} %psum.7.s0.squares.stats), channel_id=1, source_target_pairs={{0,4},{4,8},{8,12},{12,16},{16,20},{20,24},{24,28},{28,32},{32,36}... | collective-permute-start | bytes 6152 | tf_op jit(solution)/shard_map/ppermute | solution.py:41
  95.7 1.6 %collective-permute-start.18 = (f32[2,256]{1,0:T(2,128)S(1)}, f32[2,256]{1,0:T(2,128)S(1)}, u32[]{:S(2)}, u32[]{:S(2)}) collective-permute-start(f32[2,256]{1,0:T(2,128)S(1)} %psum.7.s0.squares.stats), channel_id=1, source_target_pairs={{0,8},{4,12},{8,16},{12,20},{16,24},{20,28},{24,32},{28,36},{32,40... | collective-permute-start | bytes 6152 | tf_op jit(solution)/shard_map/ppermute | solution.py:41
  98.4 3.8 %collective-permute-start.24 = (f32[128,128]{1,0:T(8,128)S(1)}, f32[128,128]{1,0:T(8,128)S(1)}, u32[]{:S(2)}, u32[]{:S(2)}) collective-permute-start(f32[128,128]{1,0:T(8,128)S(1)} %multiply_add_fusion.1), channel_id=1, source_target_pairs={{0,16},{4,20},{8,24},{12,28},{16,0},{20,4},{24,8},{28,12},{32,48},... | collective-permute-start | bytes 196616 | tf_op jit(solution)/shard_map/ppermute | solution.py:51
  102.8 1.5 %collective-permute-done.18.s2 = f32[2,256]{1,0:T(2,128)S(1)} collective-permute-done((f32[2,256]{1,0:T(2,128)S(1)}, f32[2,256]{1,0:T(2,128)S(1)}, u32[]{:S(2)}, u32[]{:S(2)}) %collective-permute-start.18) | collective-permute-done | bytes 2080 | tf_op jit(solution)/shard_map/ppermute | solution.py:41
  107.5 9.3 %attend.1 = (bf16[256,1024]{1,0:T(8,128)(2,1)}, bf16[256,1024]{1,0:T(8,128)(2,1)}, f32[8,256]{1,0:T(8,128)S(1)}) custom-call(s32[1]{0:T(128)} %bitcast.place, bf16[256,1024]{1,0:T(8,128)(2,1)S(1)} %copy-done.4, bf16[256,1024]{1,0:T(8,128)(2,1)S(1)} %copy-done.7, bf16[256,1024]{1,0:T(8,128)(2,1)S(1)} %copy-done.10, ...), custom_call_target="tpu_custom_call" | custom-call | flops 3000000000 | bytes 6000000 | tf_op jit(solution)/shard_map/attend/pallas_call | solution.py:327
  116.7 4.6 %collective-permute-start.19 = (f32[8,256]{1,0:T(8,128)S(1)}, f32[8,256]{1,0:T(8,128)S(1)}, u32[]{:S(2)}, u32[]{:S(2)}) collective-permute-start(f32[8,256]{1,0:T(8,128)S(1)} %get-tuple-element.26.e0), channel_id=1, source_target_pairs={{0,124},{4,0},{8,4},{12,8},{16,12},{20,16},{24,20},{28,24},{32,28}... | collective-permute-start | bytes 24584 | tf_op jit(solution)/shard_map/ppermute | solution.py:41
  122.7 1.3 collective-permute-start.27
  124.0 2.5 %collective-permute-done.20.e2 = f32[8,256]{1,0:T(8,128)S(1)} collective-permute-done((f32[8,256]{1,0:T(8,128)S(1)}, f32[8,256]{1,0:T(8,128)S(1)}, u32[]{:S(2)}, u32[]{:S(2)}) %collective-permute-start.20) | collective-permute-done | bytes 8224 | tf_op jit(solution)/shard_map/ppermute | solution.py:41
  126.5 6.2 %key_grads.1 = bf16[256,1024]{1,0:T(8,128)(2,1)} custom-call(s32[1]{0:T(128)} %bitcast.place, bf16[256,1024]{1,0:T(8,128)(2,1)S(1)} %copy-done.10, bf16[256,1024]{1,0:T(8,128)(2,1)S(1)} %copy-done.15, bf16[256,1024]{1,0:T(8,128)(2,1)S(1)} %copy-done.4, bf16[256,1024]{1,0:T(8,128)(2,1)} %collective-permute-done.11.q1, bf16[256,1024]{1,0:T(8,128)(2,1)S(1)} %copy-done.17, ...), custom_call_target="tpu_custom_call" | custom-call | flops 2400000000 | bytes 4800000 | tf_op jit(solution)/shard_map/key_grads/pallas_call | solution.py:327
  132.7 3.4 %backward_mix.1 = bf16[256,1024]{1,0:T(8,128)(2,1)} custom-call(s32[1]{0:T(128)} %bitcast.place, f32[2048,128]{1,0:T(8,128)S(1)} %copy-done.2, f32[128,128]{1,0:T(8,128)S(1)} %get-tuple-element.18.rates, f32[16,1024]{1,0:T(8,128)S(1)} %bitcast.6, f32[128,128]{1,0:T(8,128)S(1)} %get-tuple-element.31.start, f32[128,128]{1,0:T(8,128)S(1)} %collective-permute-done.25.p1, ...), custom_call_target="tpu_custom_call" | custom-call | flops 1200000000 | bytes 2400000 | tf_op jit(solution)/shard_map/backward_mix/pallas_call | solution.py:263
  (91 shorter events, 19.1 us)
Async XLA Ops:
  6.1 7.6 %collective-permute-start.2 = (f32[128,128]{1,0:T(8,128)S(1)}, f32[128,128]{1,0:T(8,128)S(1)}, u32[]{:S(2)}, u32[]{:S(2)}) collective-permute-start(f32[128,128]{1,0:T(8,128)S(1)} %get-tuple-element.19), channel_id=1, source_target_pairs={{0,4},{4,8},{8,12},{12,0},{16,20},{20,24},{24,28},{28,16},{32,36},... | collective-permute-start | bytes 196616 | tf_op jit(solution)/shard_map/ppermute | solution.py:51
  8.1 7.7 %collective-permute-start.3 = (f32[128,128]{1,0:T(8,128)S(1)}, f32[128,128]{1,0:T(8,128)S(1)}, u32[]{:S(2)}, u32[]{:S(2)}) collective-permute-start(f32[128,128]{1,0:T(8,128)S(1)} %get-tuple-element.19), channel_id=1, source_target_pairs={{0,8},{4,12},{8,0},{12,4},{16,24},{20,28},{24,16},{28,20},{32,40},... | collective-permute-start | bytes 196616 | tf_op jit(solution)/shard_map/ppermute | solution.py:51
  11.7 4.3 %collective-permute-start.4 = (f32[128,128]{1,0:T(8,128)S(1)}, f32[128,128]{1,0:T(8,128)S(1)}, u32[]{:S(2)}, u32[]{:S(2)}) collective-permute-start(f32[128,128]{1,0:T(8,128)S(1)} %get-tuple-element.19), channel_id=1, source_target_pairs={{0,12},{4,0},{8,4},{12,8},{16,28},{20,16},{24,20},{28,24},{32,44},... | collective-permute-start | bytes 196616 | tf_op jit(solution)/shard_map/ppermute | solution.py:51
  12.7 32.7 %collective-permute-start = (bf16[256,1024]{1,0:T(8,128)(2,1)S(1)}, bf16[256,1024]{1,0:T(8,128)(2,1)}, u32[]{:S(2)}, u32[]{:S(2)}) collective-permute-start(bf16[256,1024]{1,0:T(8,128)(2,1)S(1)} %copy-done.8), channel_id=1, source_target_pairs={{0,4},{4,8},{8,12},{12,16},{16,20},{20,24},{24,28},{28,32},{32,36}... | collective-permute-start | bytes 1572872 | tf_op jit(solution)/shard_map/ppermute | solution.py:41
  13.8 35.6 %copy-start = (bf16[256,1024]{1,0:T(8,128)(2,1)S(1)}, bf16[256,1024]{1,0:T(8,128)(2,1)}, u32[]{:S(2)}) copy-start(bf16[256,1024]{1,0:T(8,128)(2,1)} %gate_out.3) | copy-start | bytes 1572868
  16.0 23.4 %collective-permute-start.5 = (f32[128,128]{1,0:T(8,128)S(1)}, f32[128,128]{1,0:T(8,128)S(1)}, u32[]{:S(2)}, u32[]{:S(2)}) collective-permute-start(f32[128,128]{1,0:T(8,128)S(1)} %multiply_add_fusion.3), channel_id=1, source_target_pairs={{0,16},{4,20},{8,24},{12,28},{16,0},{20,4},{24,8},{28,12},{32,48},... | collective-permute-start | bytes 196616 | tf_op jit(solution)/shard_map/ppermute | solution.py:51
  17.7 36.4 %collective-permute-start.11 = (bf16[256,1024]{1,0:T(8,128)(2,1)S(1)}, bf16[256,1024]{1,0:T(8,128)(2,1)}, u32[]{:S(2)}, u32[]{:S(2)}) collective-permute-start(bf16[256,1024]{1,0:T(8,128)(2,1)S(1)} %copy-done.4), channel_id=1, source_target_pairs={{0,124},{4,0},{8,4},{12,8},{16,12},{20,16},{24,20},{28,24},{32,28}... | collective-permute-start | bytes 1572872 | tf_op jit(solution)/shard_map/ppermute | solution.py:41
  22.0 38.3 %collective-permute-start.13 = (bf16[256,1024]{1,0:T(8,128)(2,1)S(1)}, bf16[256,1024]{1,0:T(8,128)(2,1)}, u32[]{:S(2)}, u32[]{:S(2)}) collective-permute-start(bf16[256,1024]{1,0:T(8,128)(2,1)S(1)} %copy-done.5), channel_id=1, source_target_pairs={{0,124},{4,0},{8,4},{12,8},{16,12},{20,16},{24,20},{28,24},{32,28}... | collective-permute-start | bytes 1572872 | tf_op jit(solution)/shard_map/ppermute | solution.py:41
  22.5 26.8 %copy-start.23 = (f32[1024,16]{0,1:T(8,128)S(1)}, f32[1024,16]{0,1:T(8,128)}, u32[]{:S(2)}) copy-start(f32[1024,16]{0,1:T(8,128)} %param.12) | copy-start | bytes 196612
  39.5 5.5 %collective-permute-start.6 = (f32[128,128]{1,0:T(8,128)S(1)}, f32[128,128]{1,0:T(8,128)S(1)}, u32[]{:S(2)}, u32[]{:S(2)}) collective-permute-start(f32[128,128]{1,0:T(8,128)S(1)} %get-tuple-element.32), channel_id=1, source_target_pairs={{0,32},{4,36},{8,40},{12,44},{16,48},{20,52},{24,56},{28,60},{32,6... | collective-permute-start | bytes 196616 | tf_op jit(solution)/shard_map/ppermute | solution.py:51
  41.1 5.8 %collective-permute-start.7 = (f32[128,128]{1,0:T(8,128)S(1)}, f32[128,128]{1,0:T(8,128)S(1)}, u32[]{:S(2)}, u32[]{:S(2)}) collective-permute-start(f32[128,128]{1,0:T(8,128)S(1)} %get-tuple-element.32), channel_id=1, source_target_pairs={{0,64},{4,68},{8,72},{12,76},{16,80},{20,84},{24,88},{28,92},{32,9... | collective-permute-start | bytes 196616 | tf_op jit(solution)/shard_map/ppermute | solution.py:51
  45.1 4.3 %collective-permute-start.8 = (f32[128,128]{1,0:T(8,128)S(1)}, f32[128,128]{1,0:T(8,128)S(1)}, u32[]{:S(2)}, u32[]{:S(2)}) collective-permute-start(f32[128,128]{1,0:T(8,128)S(1)} %get-tuple-element.32), channel_id=1, source_target_pairs={{0,96},{4,100},{8,104},{12,108},{16,112},{20,116},{24,120},{28,124... | collective-permute-start | bytes 196616 | tf_op jit(solution)/shard_map/ppermute | solution.py:51
  45.4 19.0 %collective-permute-start.1 = (bf16[256,1024]{1,0:T(8,128)(2,1)}, bf16[256,1024]{1,0:T(8,128)(2,1)S(1)}, u32[]{:S(2)}, u32[]{:S(2)}) collective-permute-start(bf16[256,1024]{1,0:T(8,128)(2,1)} %collective-permute-done.keys_1.k1), channel_id=1, source_target_pairs={{0,4},{4,8},{8,12},{12,16},{16,20},{20,24},{24,28},{28,32},{32,36}... | collective-permute-start | bytes 1572872 | tf_op jit(solution)/shard_map/ppermute | solution.py:41
  54.0 22.0 %copy-start.6 = (bf16[256,1024]{1,0:T(8,128)(2,1)S(1)}, bf16[256,1024]{1,0:T(8,128)(2,1)}, u32[]{:S(2)}) copy-start(bf16[256,1024]{1,0:T(8,128)(2,1)} %d0.3) | copy-start | bytes 1572868
  54.0 22.0 %copy-start.9 = (bf16[256,1024]{1,0:T(8,128)(2,1)S(1)}, bf16[256,1024]{1,0:T(8,128)(2,1)}, u32[]{:S(2)}) copy-start(bf16[256,1024]{1,0:T(8,128)(2,1)} %keys.5) | copy-start | bytes 1572868
  54.0 16.4 %collective-permute-start.9 = (bf16[256,1024]{1,0:T(8,128)(2,1)S(1)}, bf16[256,1024]{1,0:T(8,128)(2,1)}, u32[]{:S(2)}, u32[]{:S(2)}) collective-permute-start(bf16[256,1024]{1,0:T(8,128)(2,1)S(1)} %get-tuple-element.20.v0.values), channel_id=1, source_target_pairs={{0,4},{4,8},{8,12},{12,16},{16,20},{20,24},{24,28},{28,32},{32,36}... | collective-permute-start | bytes 1572872 | tf_op jit(solution)/shard_map/ppermute | solution.py:41
  54.1 16.3 %collective-permute-start.12 = (bf16[256,1024]{1,0:T(8,128)(2,1)}, bf16[256,1024]{1,0:T(8,128)(2,1)S(1)}, u32[]{:S(2)}, u32[]{:S(2)}) collective-permute-start(bf16[256,1024]{1,0:T(8,128)(2,1)} %collective-permute-done.11.q1), channel_id=1, source_target_pairs={{0,124},{4,0},{8,4},{12,8},{16,12},{20,16},{24,20},{28,24},{32,28}... | collective-permute-start | bytes 1572872 | tf_op jit(solution)/shard_map/ppermute | solution.py:41
  60.3 15.6 %collective-permute-start.14 = (bf16[256,1024]{1,0:T(8,128)(2,1)}, bf16[256,1024]{1,0:T(8,128)(2,1)S(1)}, u32[]{:S(2)}, u32[]{:S(2)}) collective-permute-start(bf16[256,1024]{1,0:T(8,128)(2,1)} %collective-permute-done.13.d1), channel_id=1, source_target_pairs={{0,124},{4,0},{8,4},{12,8},{16,12},{20,16},{24,20},{28,24},{32,28}... | collective-permute-start | bytes 1572872 | tf_op jit(solution)/shard_map/ppermute | solution.py:41
  67.6 8.3 %collective-permute-start.15 = (f32[8,256]{1,0:T(8,128)S(1)}, f32[8,256]{1,0:T(8,128)S(1)}, u32[]{:S(2)}, u32[]{:S(2)}) collective-permute-start(f32[8,256]{1,0:T(8,128)S(1)} %row_totals.1.t0.totals), channel_id=1, source_target_pairs={{0,124},{4,0},{8,4},{12,8},{16,12},{20,16},{24,20},{28,24},{32,28}... | collective-permute-start | bytes 24584 | tf_op jit(solution)/shard_map/ppermute | solution.py:41
  67.7 8.3 %collective-permute-start.16 = (f32[8,256]{1,0:T(8,128)S(1)}, f32[8,256]{1,0:T(8,128)S(1)}, u32[]{:S(2)}, u32[]{:S(2)}) collective-permute-start(f32[8,256]{1,0:T(8,128)S(1)} %row_totals.1.t0.totals), channel_id=1, source_target_pairs={{0,120},{4,124},{8,0},{12,4},{16,8},{20,12},{24,16},{28,20},{32,24... | collective-permute-start | bytes 24584 | tf_op jit(solution)/shard_map/ppermute | solution.py:41
  70.5 33.9 %collective-permute-start.10 = (bf16[256,1024]{1,0:T(8,128)(2,1)}, bf16[256,1024]{1,0:T(8,128)(2,1)}, u32[]{:S(2)}, u32[]{:S(2)}) collective-permute-start(bf16[256,1024]{1,0:T(8,128)(2,1)} %collective-permute-done.9.v1), channel_id=1, source_target_pairs={{0,4},{4,8},{8,12},{12,16},{16,20},{20,24},{24,28},{28,32},{32,36}... | collective-permute-start | bytes 1572872 | tf_op jit(solution)/shard_map/ppermute | solution.py:41
  91.1 4.6 %collective-permute-start.21 = (f32[128,128]{1,0:T(8,128)S(1)}, f32[128,128]{1,0:T(8,128)S(1)}, u32[]{:S(2)}, u32[]{:S(2)}) collective-permute-start(f32[128,128]{1,0:T(8,128)S(1)} %get-tuple-element.29), channel_id=1, source_target_pairs={{0,12},{4,0},{8,4},{12,8},{16,28},{20,16},{24,20},{28,24},{32,44},... | collective-permute-start | bytes 196616 | tf_op jit(solution)/shard_map/ppermute | solution.py:51
  91.7 6.2 %collective-permute-start.22 = (f32[128,128]{1,0:T(8,128)S(1)}, f32[128,128]{1,0:T(8,128)S(1)}, u32[]{:S(2)}, u32[]{:S(2)}) collective-permute-start(f32[128,128]{1,0:T(8,128)S(1)} %get-tuple-element.29), channel_id=1, source_target_pairs={{0,8},{4,12},{8,0},{12,4},{16,24},{20,28},{24,16},{28,20},{32,40},... | collective-permute-start | bytes 196616 | tf_op jit(solution)/shard_map/ppermute | solution.py:51
  92.1 6.2 %collective-permute-start.23 = (f32[128,128]{1,0:T(8,128)S(1)}, f32[128,128]{1,0:T(8,128)S(1)}, u32[]{:S(2)}, u32[]{:S(2)}) collective-permute-start(f32[128,128]{1,0:T(8,128)S(1)} %get-tuple-element.29), channel_id=1, source_target_pairs={{0,4},{4,8},{8,12},{12,0},{16,20},{20,24},{24,28},{28,16},{32,36},... | collective-permute-start | bytes 196616 | tf_op jit(solution)/shard_map/ppermute | solution.py:51
  93.5 9.3 %collective-permute-start.17 = (f32[2,256]{1,0:T(2,128)S(1)}, f32[2,256]{1,0:T(2,128)S(1)}, u32[]{:S(2)}, u32[]{:S(2)}) collective-permute-start(f32[2,256]{1,0:T(2,128)S(1)} %psum.7.s0.squares.stats), channel_id=1, source_target_pairs={{0,4},{4,8},{8,12},{12,16},{16,20},{20,24},{24,28},{28,32},{32,36}... | collective-permute-start | bytes 6152 | tf_op jit(solution)/shard_map/ppermute | solution.py:41
  95.7 8.6 %collective-permute-start.18 = (f32[2,256]{1,0:T(2,128)S(1)}, f32[2,256]{1,0:T(2,128)S(1)}, u32[]{:S(2)}, u32[]{:S(2)}) collective-permute-start(f32[2,256]{1,0:T(2,128)S(1)} %psum.7.s0.squares.stats), channel_id=1, source_target_pairs={{0,8},{4,12},{8,16},{12,20},{16,24},{20,28},{24,32},{28,36},{32,40... | collective-permute-start | bytes 6152 | tf_op jit(solution)/shard_map/ppermute | solution.py:41
  98.4 23.4 %collective-permute-start.24 = (f32[128,128]{1,0:T(8,128)S(1)}, f32[128,128]{1,0:T(8,128)S(1)}, u32[]{:S(2)}, u32[]{:S(2)}) collective-permute-start(f32[128,128]{1,0:T(8,128)S(1)} %multiply_add_fusion.1), channel_id=1, source_target_pairs={{0,16},{4,20},{8,24},{12,28},{16,0},{20,4},{24,8},{28,12},{32,48},... | collective-permute-start | bytes 196616 | tf_op jit(solution)/shard_map/ppermute | solution.py:51
  116.7 7.2 %collective-permute-start.19 = (f32[8,256]{1,0:T(8,128)S(1)}, f32[8,256]{1,0:T(8,128)S(1)}, u32[]{:S(2)}, u32[]{:S(2)}) collective-permute-start(f32[8,256]{1,0:T(8,128)S(1)} %get-tuple-element.26.e0), channel_id=1, source_target_pairs={{0,124},{4,0},{8,4},{12,8},{16,12},{20,16},{24,20},{28,24},{32,28}... | collective-permute-start | bytes 24584 | tf_op jit(solution)/shard_map/ppermute | solution.py:41
  121.4 5.2 %collective-permute-start.20 = (f32[8,256]{1,0:T(8,128)S(1)}, f32[8,256]{1,0:T(8,128)S(1)}, u32[]{:S(2)}, u32[]{:S(2)}) collective-permute-start(f32[8,256]{1,0:T(8,128)S(1)} %get-tuple-element.26.e0), channel_id=1, source_target_pairs={{0,120},{4,124},{8,0},{12,4},{16,8},{20,12},{24,16},{28,20},{32,24... | collective-permute-start | bytes 24584 | tf_op jit(solution)/shard_map/ppermute | solution.py:41
  121.9 10.8 %collective-permute-start.25 = (f32[128,128]{1,0:T(8,128)S(1)}, f32[128,128]{1,0:T(8,128)S(1)}, u32[]{:S(2)}, u32[]{:S(2)}) collective-permute-start(f32[128,128]{1,0:T(8,128)S(1)} %get-tuple-element.30), channel_id=1, source_target_pairs={{0,96},{4,100},{8,104},{12,108},{16,112},{20,116},{24,120},{28,124... | collective-permute-start | bytes 196616 | tf_op jit(solution)/shard_map/ppermute | solution.py:51
  122.7 10.0 %collective-permute-start.26 = (f32[128,128]{1,0:T(8,128)S(1)}, f32[128,128]{1,0:T(8,128)S(1)}, u32[]{:S(2)}, u32[]{:S(2)}) collective-permute-start(f32[128,128]{1,0:T(8,128)S(1)} %get-tuple-element.30), channel_id=1, source_target_pairs={{0,64},{4,68},{8,72},{12,76},{16,80},{20,84},{24,88},{28,92},{32,9... | collective-permute-start | bytes 196616 | tf_op jit(solution)/shard_map/ppermute | solution.py:51
  122.7 10.0 %collective-permute-start.27 = (f32[128,128]{1,0:T(8,128)S(1)}, f32[128,128]{1,0:T(8,128)S(1)}, u32[]{:S(2)}, u32[]{:S(2)}) collective-permute-start(f32[128,128]{1,0:T(8,128)S(1)} %get-tuple-element.30), channel_id=1, source_target_pairs={{0,32},{4,36},{8,40},{12,44},{16,48},{20,52},{24,56},{28,60},{32,6... | collective-permute-start | bytes 196616 | tf_op jit(solution)/shard_map/ppermute | solution.py:51
  (23 other events, 164.9 us)

commit v3 on v2

--- a/solution.py
+++ b/solution.py
@@ -32,8 +32,8 @@
     )
 
 
-def params(*semantics):
-    return pltpu.CompilerParams(dimension_semantics=semantics or None, vmem_limit_bytes=48 << 20)
+def params(*semantics, vmem=48):
+    return pltpu.CompilerParams(dimension_semantics=semantics or None, vmem_limit_bytes=vmem << 20)
 
 
 def shifted(value, by):
@@ -130,13 +130,18 @@
     return [jnp.exp(-tile(rates, m)) for m in range(modes)]
 
 
+def form_drive(mixer, gate_in, drive):
+    rows, width = mixer.shape
+    for head in range(width // LANES):
+        cut = head_slice(head)
+        to_tokens(drive, head, rows, mixer[:, cut].astype(f32) * gate_in[:, cut].astype(f32))
+
+
 def forward_state_kernel(mixer, gate_in, rate, final, rates, drive):
     rows, width = mixer.shape
     modes = rate.shape[0]
     spread(rate, rates)
-    for head in range(width // LANES):
-        cut = head_slice(head)
-        to_tokens(drive, head, rows, mixer[:, cut].astype(f32) * gate_in[:, cut].astype(f32))
+    form_drive(mixer, gate_in, drive)
     zero = jnp.zeros((SUBLANES, LANES), f32)
     state = scan(drive, decays(rates, modes), None, [zero] * modes, rows, None, False)
     for m in range(modes):
@@ -147,10 +152,10 @@
     rows, width = mixer.shape
     modes = rate.shape[0]
     small = jax.ShapeDtypeStruct((modes * SUBLANES, LANES), f32)
-    big = jax.ShapeDtypeStruct((rows * SUBLANES, LANES), f32)
     return pl.pallas_call(
         forward_state_kernel,
-        out_shape=(small, small, big),
+        out_shape=(small, small),
+        scratch_shapes=[pltpu.VMEM((rows * SUBLANES, LANES), f32)],
         compiler_params=params(),
         cost_estimate=cost(2),
         name="forward_state",
@@ -166,13 +171,31 @@
 
 
 def forward_mix_kernel(
-    place, drive, rates, residue, start, p1, p2, p3, gate_out, gain, mixed, scaled, squares, residues, out, carried
+    place,
+    mixer,
+    gate_in,
+    rates,
+    residue,
+    start,
+    p1,
+    p2,
+    p3,
+    gate_out,
+    gain,
+    mixed,
+    scaled,
+    squares,
+    residues,
+    out,
+    carried,
+    drive,
 ):
     rows, width = mixed.shape
     modes = residue.shape[0]
     spread(residue, residues)
     decay = decays(rates, modes)
     res = [tile(residues, m) for m in range(modes)]
+    form_drive(mixer, gate_in, drive)
     add_planes(place, False, rows, rates, start, (p1, p2, p3), carried)
     scan(drive, decay, res, [tile(carried, m) for m in range(modes)], rows, out, False)
     total = jnp.zeros((rows, LANES), f32)
@@ -185,7 +208,7 @@
     squares[...] = row_total(total)
 
 
-def forward_mix(place, drive, rates, residue, carry, gate_out, gain):
+def forward_mix(place, mixer, gate_in, rates, residue, carry, gate_out, gain):
     rows, width = gate_out.shape
     modes = residue.shape[0]
     return pl.pallas_call(
@@ -199,12 +222,13 @@
             pltpu.VMEM((modes * SUBLANES, LANES), f32),
             pltpu.VMEM((rows * SUBLANES, LANES), f32),
             pltpu.VMEM((modes * SUBLANES, LANES), f32),
+            pltpu.VMEM((rows * SUBLANES, LANES), f32),
         ],
-        in_specs=[pl.BlockSpec(memory_space=pltpu.SMEM)] + [pl.BlockSpec(memory_space=pltpu.VMEM)] * 9,
+        in_specs=[pl.BlockSpec(memory_space=pltpu.SMEM)] + [pl.BlockSpec(memory_space=pltpu.VMEM)] * 10,
         compiler_params=params(),
         cost_estimate=cost(4),
         name="forward_mix",
-    )(place, drive, rates, residue, *carry, gate_out, gain)
+    )(place, mixer, gate_in, rates, residue, *carry, gate_out, gain)
 
 
 def column(row):
@@ -219,7 +243,7 @@
     rows, width = mixed.shape
     modes = rates.shape[0] // SUBLANES
     inverse = inverse_of(column(stats[0:1, :]), full_width)
-    pull = inverse * inverse * inverse * column(stats[1:2, :]) * (1.0 / full_width)
+    pull = inverse * inverse * inverse * column(stats[SPAN + 1 : SPAN + 2, :]) * (1.0 / full_width)
     for head in range(width // LANES):
         cut = head_slice(head)
         grad = inverse * scaled[:, cut] - mixed[:, cut] * pull
@@ -322,7 +346,7 @@
     return pl.BlockSpec(shape, lambda head, *_: (0,) * len(shape))
 
 
-def per_head(kernel, place, operands, specs, out_shape, out_specs, scratch=(), name=None, time=5):
+def per_head(kernel, place, operands, specs, out_shape, out_specs, scratch=(), name=None, time=5, vmem=48):
     heads = operands[0].shape[1] // GROUP
     return pl.pallas_call(
         kernel,
@@ -334,7 +358,7 @@
             out_specs=out_specs,
             scratch_shapes=scratch,
         ),
-        compiler_params=params("arbitrary"),
+        compiler_params=params("arbitrary", vmem=vmem),
         cost_estimate=cost(time),
         name=name,
     )(place, *operands)
@@ -357,7 +381,7 @@
 
 
 def value_grads_kernel(
-    blocks, place, keys, q0, q1, q2, d0, d1, d2, t0, t1, t2, gain, mixed, squares, scaled, stats, acc
+    blocks, place, keys, q0, q1, q2, d0, d1, d2, t0, t1, t2, gain, mixed, s0, s1, s2, scaled, stats, acc
 ):
     step = pl.program_id(0)
     position = place[0]
@@ -380,8 +404,9 @@
 
     @pl.when(step == pl.num_programs(0) - 1)
     def _():
-        stats[0:1, :] = squares[...]
-        stats[1:2, :] = row_total(acc[...])
+        for i, squares in enumerate((s0, s1, s2)):
+            stats[i : i + 1, :] = squares[...]
+        stats[SPAN + 1 : SPAN + 2, :] = row_total(acc[...])
 
 
 def value_grads(blocks, place, keys, queries, cotangents, totals, gain, mixed, squares):
@@ -392,10 +417,10 @@
     return per_head(
         functools.partial(value_grads_kernel, blocks),
         place,
-        (keys, *queries, *cotangents, *totals, gain, mixed, squares),
-        [block] * 7 + [stat] * 3 + [head_block(1), block, whole((1, rows))],
-        (jax.ShapeDtypeStruct((rows, width), f32), jax.ShapeDtypeStruct((2, rows), f32)),
-        (block, whole((2, rows))),
+        (keys, *queries, *cotangents, *totals, gain, mixed, *squares),
+        [block] * 7 + [stat] * 3 + [head_block(1), block] + [whole((1, rows))] * 3,
+        (jax.ShapeDtypeStruct((rows, width), f32), jax.ShapeDtypeStruct((SPAN + 2, rows), f32)),
+        (block, whole((SPAN + 2, rows))),
         scratch=[pltpu.VMEM((rows, LANES), f32)],
         name="value_grads",
         time=7,
@@ -403,7 +428,7 @@
 
 
 def attend_kernel(
-    full_width, place, queries, cotangent, k0, k1, k2, v0, v1, v2, s0, s1, s2, totals, attended, grad, delta, columns
+    full_width, place, queries, cotangent, k0, k1, k2, v0, v1, v2, stats, totals, attended, grad, delta, columns
 ):
     position = place[0]
 
@@ -412,7 +437,7 @@
         columns[...] = jnp.transpose(totals[...])
 
     lane = lax.broadcasted_iota(jnp.int32, columns.shape, 1)
-    inverses = [inverse_of(squares[0:1, :], full_width) for squares in (s0, s1, s2)]
+    inverses = [inverse_of(stats[i : i + 1, :], full_width) for i in range(SPAN + 1)]
     for head, cut in step_heads():
         log_total = jnp.sum(jnp.where(lane == head, columns[...], 0.0), axis=1, keepdims=True)
         probs = []
@@ -438,7 +463,7 @@
         grad[:, cut] = (total * SCALE).astype(bf16)
 
 
-def attend(full_width, place, queries, cotangent, keys, values, squares, totals):
+def attend(full_width, place, queries, cotangent, keys, values, stats, totals):
     rows, width = queries.shape
     heads = width // HEAD_DIM
     block = head_block(rows)
@@ -447,12 +472,13 @@
     return per_head(
         functools.partial(attend_kernel, full_width),
         place,
-        (queries, cotangent, *keys, *values, *squares, totals),
-        [block] * 8 + [whole((2, rows))] * 3 + [stat],
+        (queries, cotangent, *keys, *values, stats, totals),
+        [block] * 8 + [whole((SPAN + 2, rows)), stat],
         (out, out, jax.ShapeDtypeStruct((heads, rows), f32)),
         (block, block, stat),
         scratch=[pltpu.VMEM((rows, heads), f32)],
         name="attend",
+        vmem=61,
         time=10,
     )
 
@@ -485,7 +511,7 @@
         functools.partial(key_grads_kernel, full_width, blocks),
         place,
         (keys, values, *queries, *cotangents, *totals, *deltas, squares),
-        [block] * 8 + [stat] * 6 + [whole((2, rows))],
+        [block] * 8 + [stat] * 6 + [whole((SPAN + 2, rows))],
         jax.ShapeDtypeStruct((rows, width), bf16),
         block,
         name="key_grads",
@@ -510,12 +536,15 @@
     queries_2 = shifted(queries_1, -1)
     cotangent_2 = shifted(cotangent_1, -1)
 
-    final, rates, drive = forward_state(mixer_input, gate_in, jnp.transpose(decay_rate))
+    final, rates = forward_state(mixer_input, gate_in, jnp.transpose(decay_rate))
     carry = carry_in(final, rates, length, False)
-    mixed, scaled_mix, squares = forward_mix(place, drive, rates, residue, carry, gate_out, gain)
+    mixed, scaled_mix, squares = forward_mix(
+        place, mixer_input, gate_in, rates, residue, carry, gate_out, gain
+    )
     mix_1 = shifted(scaled_mix, 1)
     mix_2 = shifted(mix_1, 1)
 
+    all_squares = (squares, shifted(squares, 1), shifted(squares, 2))
     totals = row_totals(place, queries, key_vectors, keys_1, keys_2)
     totals_1 = shifted(totals, -1)
     totals_2 = shifted(totals, -2)
@@ -523,11 +552,9 @@
     all_cotangents = (grad_out, cotangent_1, cotangent_2)
     all_totals = (totals, totals_1, totals_2)
     scaled, stats = value_grads(
-        blocks, place, key_vectors, all_queries, all_cotangents, all_totals, gain, mixed, squares
+        blocks, place, key_vectors, all_queries, all_cotangents, all_totals, gain, mixed, all_squares
     )
     stats = lax.psum(stats, "tp")
-    stats_1 = shifted(stats, 1)
-    stats_2 = shifted(stats, 2)
     final, drive = backward_state(full_width, scaled, mixed, gate_out, stats, rates)
     carry = carry_in(final, rates, length, True)
     grad_input = backward_mix(place, drive, rates, residue, carry, gate_in)
@@ -539,7 +566,7 @@
         grad_out,
         (key_vectors, keys_1, keys_2),
         (scaled_mix, mix_1, mix_2),
-        (stats, stats_1, stats_2),
+        stats,
         totals,
     )
     all_deltas = (delta, shifted(delta, -1), shifted(delta, -2))

time: 137 us -> 133 us (0.971)
  local copies, waits for them, and re-layouts: 10.1 us -> 5.76 us
    unnamed x54 -> x58, local copies, waits for them, and re-layouts: 10.1 us -> 5.76 us
    ppermute x14, waiting for transfers between devices: 27 us -> 31 us  [along(): return lax.ppermute(value, 'ctx', [(i, target(i)) for i in range(32)])]
    ppermute x14, waiting for transfers between devices: 16.1 us -> 12.2 us  [shifted(): lax.ppermute(value, 'ctx', [(i, (i + by) % devices) for i in range(device...]
    ppermute x14, starting transfers between devices: 20.1 us -> 17.9 us  [along(): return lax.ppermute(value, 'ctx', [(i, target(i)) for i in range(32)])]
    ppermute x14, starting transfers between devices: 21.5 us -> 22.9 us  [shifted(): lax.ppermute(value, 'ctx', [(i, (i + by) % devices) for i in range(device...]
  transfers between devices with their start and end apart: 28 -> 28, of which waited for: 16 -> 14; matrix products, arithmetic and copies ran while one was open for 0% -> 0% of each run, Pallas kernels for 21% -> 22%
where the time goes in v3:
time: 133 us; the launch traced here: 132 us
  waiting for transfers between devices  43.2 us (32%)
  starting transfers between devices  40.8 us (31%)
  Pallas kernels  34.1 us (26%)
  blocking collectives  7.17 us (5%)
  local copies, waits for them, and re-layouts  5.76 us (4%)
    ppermute x14, waiting for transfers between devices, along(): return lax.ppermute(value, 'ctx', [(i, target(i)) for i in range(32)])  31 us
    pallas_call x4, Pallas kernels, per_head(): pl.pallas_call(kernel, out_shape=out_shape, grid_spec=pltpu.PrefetchScala...  24.3 us
    ppermute x14, starting transfers between devices, shifted(): lax.ppermute(value, 'ctx', [(i, (i + by) % devices) for i in range(device...  22.9 us
    ppermute x14, starting transfers between devices, along(): return lax.ppermute(value, 'ctx', [(i, target(i)) for i in range(32)])  17.9 us
    ppermute x14, waiting for transfers between devices, shifted(): lax.ppermute(value, 'ctx', [(i, (i + by) % devices) for i in range(device...  12.2 us
    psum x1, blocking collectives, shards(): stats = lax.psum(stats, 'tp')  7.17 us
    unnamed x58, local copies, waits for them, and re-layouts  5.76 us
    pallas_call x1, Pallas kernels, backward_mix(): pl.pallas_call(backward_mix_kernel, out_shape=jax.ShapeDtypeStruct((rows,...  3.45 us
  transfers between devices with their start and end apart: 28, of which 14 were waited for; matrix products, arithmetic and copies ran while one was open for 0% of the time, Pallas kernels for 22%

profile of v3, /device:TPU:0, one launch (start us, length us, event | category | flops | bytes accessed | tf_op | source)
XLA Modules:
  0.0 132.2 jit_solution(3493825314827490455)
XLA Ops:
  3.6 1.5 %forward_state.1 = (f32[128,128]{1,0:T(8,128)S(1)}, f32[128,128]{1,0:T(8,128)S(1)}) custom-call(bf16[256,1024]{1,0:T(8,128)(2,1)S(1)} %copy-done.5, bf16[256,1024]{1,0:T(8,128)(2,1)S(1)} %copy-done.13, f32[16,1024]{1,0:T(8,128)S(1)} %bitcast.4), custom_call_target="tpu_custom_call" | custom-call | flops 600000000 | bytes 1200000 | tf_op jit(solution)/shard_map/forward_state/pallas_call | solution.py:155
  5.1 2.1 %collective-permute-start.2 = (f32[128,128]{1,0:T(8,128)S(1)}, f32[128,128]{1,0:T(8,128)S(1)}, u32[]{:S(2)}, u32[]{:S(2)}) collective-permute-start(f32[128,128]{1,0:T(8,128)S(1)} %get-tuple-element.17), channel_id=1, source_target_pairs={{0,4},{4,8},{8,12},{12,0},{16,20},{20,24},{24,28},{28,16},{32,36},... | collective-permute-start | bytes 196616 | tf_op jit(solution)/shard_map/ppermute | solution.py:51
  7.2 3.6 %collective-permute-start.3 = (f32[128,128]{1,0:T(8,128)S(1)}, f32[128,128]{1,0:T(8,128)S(1)}, u32[]{:S(2)}, u32[]{:S(2)}) collective-permute-start(f32[128,128]{1,0:T(8,128)S(1)} %get-tuple-element.17), channel_id=1, source_target_pairs={{0,8},{4,12},{8,0},{12,4},{16,24},{20,28},{24,16},{28,20},{32,40},... | collective-permute-start | bytes 196616 | tf_op jit(solution)/shard_map/ppermute | solution.py:51
  12.8 2.1 %collective-permute-done.3 = f32[128,128]{1,0:T(8,128)S(1)} collective-permute-done((f32[128,128]{1,0:T(8,128)S(1)}, f32[128,128]{1,0:T(8,128)S(1)}, u32[]{:S(2)}, u32[]{:S(2)}) %collective-permute-start.3) | collective-permute-done | bytes 65568 | tf_op jit(solution)/shard_map/ppermute | solution.py:51
  15.1 1.7 %collective-permute-start.5 = (f32[128,128]{1,0:T(8,128)S(1)}, f32[128,128]{1,0:T(8,128)S(1)}, u32[]{:S(2)}, u32[]{:S(2)}) collective-permute-start(f32[128,128]{1,0:T(8,128)S(1)} %multiply_add_fusion.3), channel_id=1, source_target_pairs={{0,16},{4,20},{8,24},{12,28},{16,0},{20,4},{24,8},{28,12},{32,48},... | collective-permute-start | bytes 196616 | tf_op jit(solution)/shard_map/ppermute | solution.py:51
  16.8 4.3 %collective-permute-start.11 = (bf16[256,1024]{1,0:T(8,128)(2,1)S(1)}, bf16[256,1024]{1,0:T(8,128)(2,1)}, u32[]{:S(2)}, u32[]{:S(2)}) collective-permute-start(bf16[256,1024]{1,0:T(8,128)(2,1)S(1)} %copy-done.7), channel_id=1, source_target_pairs={{0,124},{4,0},{8,4},{12,8},{16,12},{20,16},{24,20},{28,24},{32,28}... | collective-permute-start | bytes 1572872 | tf_op jit(solution)/shard_map/ppermute | solution.py:41
  21.6 16.9 %collective-permute-done.5 = f32[128,128]{1,0:T(8,128)S(1)} collective-permute-done((f32[128,128]{1,0:T(8,128)S(1)}, f32[128,128]{1,0:T(8,128)S(1)}, u32[]{:S(2)}, u32[]{:S(2)}) %collective-permute-start.5) | collective-permute-done | bytes 65568 | tf_op jit(solution)/shard_map/ppermute | solution.py:51
  38.6 1.6 %collective-permute-start.6 = (f32[128,128]{1,0:T(8,128)S(1)}, f32[128,128]{1,0:T(8,128)S(1)}, u32[]{:S(2)}, u32[]{:S(2)}) collective-permute-start(f32[128,128]{1,0:T(8,128)S(1)} %get-tuple-element.30), channel_id=1, source_target_pairs={{0,32},{4,36},{8,40},{12,44},{16,48},{20,52},{24,56},{28,60},{32,6... | collective-permute-start | bytes 196616 | tf_op jit(solution)/shard_map/ppermute | solution.py:51
  40.1 1.6 %collective-permute-start.7 = (f32[128,128]{1,0:T(8,128)S(1)}, f32[128,128]{1,0:T(8,128)S(1)}, u32[]{:S(2)}, u32[]{:S(2)}) collective-permute-start(f32[128,128]{1,0:T(8,128)S(1)} %get-tuple-element.30), channel_id=1, source_target_pairs={{0,64},{4,68},{8,72},{12,76},{16,80},{20,84},{24,88},{28,92},{32,9... | collective-permute-start | bytes 196616 | tf_op jit(solution)/shard_map/ppermute | solution.py:51
  41.8 2.4 %collective-permute-done.6.p1 = f32[128,128]{1,0:T(8,128)S(1)} collective-permute-done((f32[128,128]{1,0:T(8,128)S(1)}, f32[128,128]{1,0:T(8,128)S(1)}, u32[]{:S(2)}, u32[]{:S(2)}) %collective-permute-start.6) | collective-permute-done | bytes 65568 | tf_op jit(solution)/shard_map/ppermute | solution.py:51
  44.5 1.4 %collective-permute-done.7.p2 = f32[128,128]{1,0:T(8,128)S(1)} collective-permute-done((f32[128,128]{1,0:T(8,128)S(1)}, f32[128,128]{1,0:T(8,128)S(1)}, u32[]{:S(2)}, u32[]{:S(2)}) %collective-permute-start.7) | collective-permute-done | bytes 65568 | tf_op jit(solution)/shard_map/ppermute | solution.py:51
  45.9 2.5 %collective-permute-done.8.p3 = f32[128,128]{1,0:T(8,128)S(1)} collective-permute-done((f32[128,128]{1,0:T(8,128)S(1)}, f32[128,128]{1,0:T(8,128)S(1)}, u32[]{:S(2)}, u32[]{:S(2)}) %collective-permute-start.8) | collective-permute-done | bytes 65568 | tf_op jit(solution)/shard_map/ppermute | solution.py:51
  49.4 3.1 %forward_mix.1 = (f32[256,1024]{1,0:T(8,128)S(1)}, bf16[256,1024]{1,0:T(8,128)(2,1)S(1)}, f32[1,256]{1,0:T(1,128)S(1)}) custom-call(s32[1]{0:T(128)} %bitcast.place, bf16[256,1024]{1,0:T(8,128)(2,1)S(1)} %copy-done.6, bf16[256,1024]{1,0:T(8,128)(2,1)S(1)} %copy-done.14, f32[128,128]{1,0:T(8,128)S(1)} %get-tuple-element.16.rates, f32[16,1024]{1,0:T(8,128)S(1)} %bitcast.5, ...), custom_call_target="tpu_custom_call" | custom-call | flops 1200000000 | bytes 2400000 | tf_op jit(solution)/shard_map/forward_mix/pallas_call | solution.py:214
  52.6 6.2 %collective-permute-start.12 = (bf16[256,1024]{1,0:T(8,128)(2,1)}, bf16[256,1024]{1,0:T(8,128)(2,1)S(1)}, u32[]{:S(2)}, u32[]{:S(2)}) collective-permute-start(bf16[256,1024]{1,0:T(8,128)(2,1)} %collective-permute-done.11.q1), channel_id=1, source_target_pairs={{0,124},{4,0},{8,4},{12,8},{16,12},{20,16},{24,20},{28,24},{32,28}... | collective-permute-start | bytes 1572872 | tf_op jit(solution)/shard_map/ppermute | solution.py:41
  58.9 2.0 %collective-permute-start.17 = (f32[1,256]{1,0:T(1,128)S(1)}, f32[1,256]{1,0:T(1,128)S(1)}, u32[]{:S(2)}, u32[]{:S(2)}) collective-permute-start(f32[1,256]{1,0:T(1,128)S(1)} %get-tuple-element.20.s0), channel_id=1, source_target_pairs={{0,4},{4,8},{8,12},{12,16},{16,20},{20,24},{24,28},{28,32},{32,36}... | collective-permute-start | bytes 3080 | tf_op jit(solution)/shard_map/ppermute | solution.py:41
  60.9 2.8 %collective-permute-done.1.keys_2.k2 = bf16[256,1024]{1,0:T(8,128)(2,1)S(1)} collective-permute-done((bf16[256,1024]{1,0:T(8,128)(2,1)}, bf16[256,1024]{1,0:T(8,128)(2,1)S(1)}, u32[]{:S(2)}, u32[]{:S(2)}) %collective-permute-start.1) | collective-permute-done | bytes 524320 | tf_op jit(solution)/shard_map/ppermute | solution.py:41
  63.7 3.1 %row_totals.1.t0.totals = f32[8,256]{1,0:T(8,128)S(1)} custom-call(s32[1]{0:T(128)} %bitcast.place, bf16[256,1024]{1,0:T(8,128)(2,1)S(1)} %copy-done.7, bf16[256,1024]{1,0:T(8,128)(2,1)S(1)} %copy-done.11, bf16[256,1024]{1,0:T(8,128)(2,1)} %collective-permute-done.keys_1.k1, bf16[256,1024]{1,0:T(8,128)(2,1)S(1)} %collective-permute-done.1.keys_2.k2), custom_call_target="tpu_custom_call" | custom-call | flops 1200000000 | bytes 2400000 | tf_op jit(solution)/shard_map/row_totals/pallas_call | solution.py:351
  66.8 2.6 %collective-permute-done.17.s1 = f32[1,256]{1,0:T(1,128)S(1)} collective-permute-done((f32[1,256]{1,0:T(1,128)S(1)}, f32[1,256]{1,0:T(1,128)S(1)}, u32[]{:S(2)}, u32[]{:S(2)}) %collective-permute-start.17) | collective-permute-done | bytes 1056 | tf_op jit(solution)/shard_map/ppermute | solution.py:41
  69.8 2.0 %collective-permute-done.18.s2 = f32[1,256]{1,0:T(1,128)S(1)} collective-permute-done((f32[1,256]{1,0:T(1,128)S(1)}, f32[1,256]{1,0:T(1,128)S(1)}, u32[]{:S(2)}, u32[]{:S(2)}) %collective-permute-start.18) | collective-permute-done | bytes 1056 | tf_op jit(solution)/shard_map/ppermute | solution.py:41
  71.8 1.6 %collective-permute-start.16 = (f32[8,256]{1,0:T(8,128)S(1)}, f32[8,256]{1,0:T(8,128)S(1)}, u32[]{:S(2)}, u32[]{:S(2)}) collective-permute-start(f32[8,256]{1,0:T(8,128)S(1)} %row_totals.1.t0.totals), channel_id=1, source_target_pairs={{0,120},{4,124},{8,0},{12,4},{16,8},{20,12},{24,16},{28,20},{32,24... | collective-permute-start | bytes 24584 | tf_op jit(solution)/shard_map/ppermute | solution.py:41
  74.8 2.1 %collective-permute-done.16.t2 = f32[8,256]{1,0:T(8,128)S(1)} collective-permute-done((f32[8,256]{1,0:T(8,128)S(1)}, f32[8,256]{1,0:T(8,128)S(1)}, u32[]{:S(2)}, u32[]{:S(2)}) %collective-permute-start.16) | collective-permute-done | bytes 8224 | tf_op jit(solution)/shard_map/ppermute | solution.py:41
  76.9 5.2 %value_grads.1 = (f32[256,1024]{1,0:T(8,128)S(1)}, f32[4,256]{1,0:T(4,128)S(1)}) custom-call(s32[1]{0:T(128)} %bitcast.place, bf16[256,1024]{1,0:T(8,128)(2,1)S(1)} %copy-done.11, bf16[256,1024]{1,0:T(8,128)(2,1)S(1)} %copy-done.8, bf16[256,1024]{1,0:T(8,128)(2,1)} %collective-permute-done.11.q1, bf16[256,1024]{1,0:T(8,128)(2,1)S(1)} %collective-permute-done.12.q2, ...), custom_call_target="tpu_custom_call" | custom-call | flops 2100000000 | bytes 4200000 | tf_op jit(solution)/shard_map/value_grads/pallas_call | solution.py:351
  82.1 7.2 %psum.7.stats.squares = f32[4,256]{1,0:T(4,128)S(1)} all-reduce(f32[4,256]{1,0:T(4,128)S(1)} %get-tuple-element.21), channel_id=1, replica_groups=mesh['ctx'=32,'tp'=4] {'tp'}, use_global_device_ids=true, to_apply=%region_0.1 | all-reduce | flops 1024 | bytes 8192 | tf_op jit(solution)/shard_map/psum | solution.py:557
  89.3 1.6 %backward_state.1 = (f32[128,128]{1,0:T(8,128)S(1)}, f32[2048,128]{1,0:T(8,128)S(1)}) custom-call(f32[256,1024]{1,0:T(8,128)S(1)} %get-tuple-element.25.scaled, f32[256,1024]{1,0:T(8,128)S(1)} %get-tuple-element.19.mixed, bf16[256,1024]{1,0:T(8,128)(2,1)S(1)} %copy-done, f32[4,256]{1,0:T(4,128)S(1)} %psum.7.stats.squares, f32[128,128]{1,0:T(8,128)S(1)} %get-tuple-element.16.rates), custom_call_target="tpu_custom_call" | custom-call | flops 600000000 | bytes 1200000 | tf_op jit(solution)/shard_map/backward_state/pallas_call | solution.py:259
  92.0 3.0 %collective-permute-start.21 = (f32[128,128]{1,0:T(8,128)S(1)}, f32[128,128]{1,0:T(8,128)S(1)}, u32[]{:S(2)}, u32[]{:S(2)}) collective-permute-start(f32[128,128]{1,0:T(8,128)S(1)} %get-tuple-element.27), channel_id=1, source_target_pairs={{0,12},{4,0},{8,4},{12,8},{16,28},{20,16},{24,20},{28,24},{32,44},... | collective-permute-start | bytes 196616 | tf_op jit(solution)/shard_map/ppermute | solution.py:51
  95.9 2.2 %collective-permute-done.21 = f32[128,128]{1,0:T(8,128)S(1)} collective-permute-done((f32[128,128]{1,0:T(8,128)S(1)}, f32[128,128]{1,0:T(8,128)S(1)}, u32[]{:S(2)}, u32[]{:S(2)}) %collective-permute-start.21) | collective-permute-done | bytes 65568 | tf_op jit(solution)/shard_map/ppermute | solution.py:51
  98.0 3.0 %collective-permute-done.22 = f32[128,128]{1,0:T(8,128)S(1)} collective-permute-done((f32[128,128]{1,0:T(8,128)S(1)}, f32[128,128]{1,0:T(8,128)S(1)}, u32[]{:S(2)}, u32[]{:S(2)}) %collective-permute-start.22) | collective-permute-done | bytes 65568 | tf_op jit(solution)/shard_map/ppermute | solution.py:51
  101.6 9.8 %attend.1 = (bf16[256,1024]{1,0:T(8,128)(2,1)}, bf16[256,1024]{1,0:T(8,128)(2,1)}, f32[8,256]{1,0:T(8,128)}) custom-call(s32[1]{0:T(128)} %bitcast.place, bf16[256,1024]{1,0:T(8,128)(2,1)} %q0.3, bf16[256,1024]{1,0:T(8,128)(2,1)} %d0.3, bf16[256,1024]{1,0:T(8,128)(2,1)} %keys.5, bf16[256,1024]{1,0:T(8,128)(2,1)} %collective-permute-done.keys_1.k1, ...), custom_call_target="tpu_custom_call" | custom-call | flops 3000000000 | bytes 6000000 | tf_op jit(solution)/shard_map/attend/pallas_call | solution.py:351
  111.4 4.9 %collective-permute-start.19 = (f32[8,256]{1,0:T(8,128)}, f32[8,256]{1,0:T(8,128)S(1)}, u32[]{:S(2)}, u32[]{:S(2)}) collective-permute-start(f32[8,256]{1,0:T(8,128)} %get-tuple-element.24.e0), channel_id=1, source_target_pairs={{0,124},{4,0},{8,4},{12,8},{16,12},{20,16},{24,20},{28,24},{32,28}... | collective-permute-start | bytes 24584 | tf_op jit(solution)/shard_map/ppermute | solution.py:41
  119.1 2.6 %collective-permute-done.20.e2 = f32[8,256]{1,0:T(8,128)S(1)} collective-permute-done((f32[8,256]{1,0:T(8,128)}, f32[8,256]{1,0:T(8,128)S(1)}, u32[]{:S(2)}, u32[]{:S(2)}) %collective-permute-start.20) | collective-permute-done | bytes 8224 | tf_op jit(solution)/shard_map/ppermute | solution.py:41
  122.5 6.2 %key_grads.1 = bf16[256,1024]{1,0:T(8,128)(2,1)} custom-call(s32[1]{0:T(128)} %bitcast.place, bf16[256,1024]{1,0:T(8,128)(2,1)S(1)} %copy-done.12, bf16[256,1024]{1,0:T(8,128)(2,1)S(1)} %copy-done.17, bf16[256,1024]{1,0:T(8,128)(2,1)S(1)} %copy-done.9, bf16[256,1024]{1,0:T(8,128)(2,1)} %collective-permute-done.11.q1, bf16[256,1024]{1,0:T(8,128)(2,1)S(1)} %copy-done.19, ...), custom_call_target="tpu_custom_call" | custom-call | flops 2400000000 | bytes 4800000 | tf_op jit(solution)/shard_map/key_grads/pallas_call | solution.py:351
  128.8 3.5 %backward_mix.1 = bf16[256,1024]{1,0:T(8,128)(2,1)} custom-call(s32[1]{0:T(128)} %bitcast.place, f32[2048,128]{1,0:T(8,128)S(1)} %copy-done.4, f32[128,128]{1,0:T(8,128)S(1)} %get-tuple-element.16.rates, f32[16,1024]{1,0:T(8,128)S(1)} %bitcast.6, f32[128,128]{1,0:T(8,128)S(1)} %get-tuple-element.29.start, f32[128,128]{1,0:T(8,128)S(1)} %collective-permute-done.25.p1, ...), custom_call_target="tpu_custom_call" | custom-call | flops 1200000000 | bytes 2400000 | tf_op jit(solution)/shard_map/backward_mix/pallas_call | solution.py:287
  (95 shorter events, 14.8 us)
Async XLA Ops:
  3.6 44.8 %copy-start.24 = (f32[1024,16]{0,1:T(8,128)S(1)}, f32[1024,16]{0,1:T(8,128)}, u32[]{:S(2)}) copy-start(f32[1024,16]{0,1:T(8,128)} %param.12) | copy-start | bytes 196612
  5.1 7.7 %collective-permute-start.2 = (f32[128,128]{1,0:T(8,128)S(1)}, f32[128,128]{1,0:T(8,128)S(1)}, u32[]{:S(2)}, u32[]{:S(2)}) collective-permute-start(f32[128,128]{1,0:T(8,128)S(1)} %get-tuple-element.17), channel_id=1, source_target_pairs={{0,4},{4,8},{8,12},{12,0},{16,20},{20,24},{24,28},{28,16},{32,36},... | collective-permute-start | bytes 196616 | tf_op jit(solution)/shard_map/ppermute | solution.py:51
  7.2 7.7 %collective-permute-start.3 = (f32[128,128]{1,0:T(8,128)S(1)}, f32[128,128]{1,0:T(8,128)S(1)}, u32[]{:S(2)}, u32[]{:S(2)}) collective-permute-start(f32[128,128]{1,0:T(8,128)S(1)} %get-tuple-element.17), channel_id=1, source_target_pairs={{0,8},{4,12},{8,0},{12,4},{16,24},{20,28},{24,16},{28,20},{32,40},... | collective-permute-start | bytes 196616 | tf_op jit(solution)/shard_map/ppermute | solution.py:51
  10.8 4.3 %collective-permute-start.4 = (f32[128,128]{1,0:T(8,128)S(1)}, f32[128,128]{1,0:T(8,128)S(1)}, u32[]{:S(2)}, u32[]{:S(2)}) collective-permute-start(f32[128,128]{1,0:T(8,128)S(1)} %get-tuple-element.17), channel_id=1, source_target_pairs={{0,12},{4,0},{8,4},{12,8},{16,28},{20,16},{24,20},{28,24},{32,44},... | collective-permute-start | bytes 196616 | tf_op jit(solution)/shard_map/ppermute | solution.py:51
  11.8 32.7 %collective-permute-start = (bf16[256,1024]{1,0:T(8,128)(2,1)S(1)}, bf16[256,1024]{1,0:T(8,128)(2,1)}, u32[]{:S(2)}, u32[]{:S(2)}) collective-permute-start(bf16[256,1024]{1,0:T(8,128)(2,1)S(1)} %copy-done.10), channel_id=1, source_target_pairs={{0,4},{4,8},{8,12},{12,16},{16,20},{20,24},{24,28},{28,32},{32,36}... | collective-permute-start | bytes 1572872 | tf_op jit(solution)/shard_map/ppermute | solution.py:41
  12.8 35.6 %copy-start.28 = (f32[1024]{0:T(1024)S(1)}, f32[1024]{0:T(1024)}, u32[]{:S(2)}) copy-start(f32[1024]{0:T(1024)} %param.14) | copy-start | bytes 12292
  12.8 35.6 %copy-start = (bf16[256,1024]{1,0:T(8,128)(2,1)S(1)}, bf16[256,1024]{1,0:T(8,128)(2,1)}, u32[]{:S(2)}) copy-start(bf16[256,1024]{1,0:T(8,128)(2,1)} %gate_out.3) | copy-start | bytes 1572868
  12.8 35.6 %copy-start.6 = (bf16[256,1024]{1,0:T(8,128)(2,1)S(1)}, bf16[256,1024]{1,0:T(8,128)(2,1)}, u32[]{:S(2)}) copy-start(bf16[256,1024]{1,0:T(8,128)(2,1)} %mixer.3) | copy-start | bytes 1572868
  15.1 23.4 %collective-permute-start.5 = (f32[128,128]{1,0:T(8,128)S(1)}, f32[128,128]{1,0:T(8,128)S(1)}, u32[]{:S(2)}, u32[]{:S(2)}) collective-permute-start(f32[128,128]{1,0:T(8,128)S(1)} %multiply_add_fusion.3), channel_id=1, source_target_pairs={{0,16},{4,20},{8,24},{12,28},{16,0},{20,4},{24,8},{28,12},{32,48},... | collective-permute-start | bytes 196616 | tf_op jit(solution)/shard_map/ppermute | solution.py:51
  16.8 35.9 %collective-permute-start.11 = (bf16[256,1024]{1,0:T(8,128)(2,1)S(1)}, bf16[256,1024]{1,0:T(8,128)(2,1)}, u32[]{:S(2)}, u32[]{:S(2)}) collective-permute-start(bf16[256,1024]{1,0:T(8,128)(2,1)S(1)} %copy-done.7), channel_id=1, source_target_pairs={{0,124},{4,0},{8,4},{12,8},{16,12},{20,16},{24,20},{28,24},{32,28}... | collective-permute-start | bytes 1572872 | tf_op jit(solution)/shard_map/ppermute | solution.py:41
  21.1 37.8 %collective-permute-start.13 = (bf16[256,1024]{1,0:T(8,128)(2,1)}, bf16[256,1024]{1,0:T(8,128)(2,1)}, u32[]{:S(2)}, u32[]{:S(2)}) collective-permute-start(bf16[256,1024]{1,0:T(8,128)(2,1)} %d0.3), channel_id=1, source_target_pairs={{0,124},{4,0},{8,4},{12,8},{16,12},{20,16},{24,20},{28,24},{32,28}... | collective-permute-start | bytes 1572872 | tf_op jit(solution)/shard_map/ppermute | solution.py:41
  38.6 5.5 %collective-permute-start.6 = (f32[128,128]{1,0:T(8,128)S(1)}, f32[128,128]{1,0:T(8,128)S(1)}, u32[]{:S(2)}, u32[]{:S(2)}) collective-permute-start(f32[128,128]{1,0:T(8,128)S(1)} %get-tuple-element.30), channel_id=1, source_target_pairs={{0,32},{4,36},{8,40},{12,44},{16,48},{20,52},{24,56},{28,60},{32,6... | collective-permute-start | bytes 196616 | tf_op jit(solution)/shard_map/ppermute | solution.py:51
  40.1 5.8 %collective-permute-start.7 = (f32[128,128]{1,0:T(8,128)S(1)}, f32[128,128]{1,0:T(8,128)S(1)}, u32[]{:S(2)}, u32[]{:S(2)}) collective-permute-start(f32[128,128]{1,0:T(8,128)S(1)} %get-tuple-element.30), channel_id=1, source_target_pairs={{0,64},{4,68},{8,72},{12,76},{16,80},{20,84},{24,88},{28,92},{32,9... | collective-permute-start | bytes 196616 | tf_op jit(solution)/shard_map/ppermute | solution.py:51
  44.1 4.3 %collective-permute-start.8 = (f32[128,128]{1,0:T(8,128)S(1)}, f32[128,128]{1,0:T(8,128)S(1)}, u32[]{:S(2)}, u32[]{:S(2)}) collective-permute-start(f32[128,128]{1,0:T(8,128)S(1)} %get-tuple-element.30), channel_id=1, source_target_pairs={{0,96},{4,100},{8,104},{12,108},{16,112},{20,116},{24,120},{28,124... | collective-permute-start | bytes 196616 | tf_op jit(solution)/shard_map/ppermute | solution.py:51
  44.5 19.2 %collective-permute-start.1 = (bf16[256,1024]{1,0:T(8,128)(2,1)}, bf16[256,1024]{1,0:T(8,128)(2,1)S(1)}, u32[]{:S(2)}, u32[]{:S(2)}) collective-permute-start(bf16[256,1024]{1,0:T(8,128)(2,1)} %collective-permute-done.keys_1.k1), channel_id=1, source_target_pairs={{0,4},{4,8},{8,12},{12,16},{16,20},{20,24},{24,28},{28,32},{32,36}... | collective-permute-start | bytes 1572872 | tf_op jit(solution)/shard_map/ppermute | solution.py:41
  52.6 20.8 %collective-permute-start.9 = (bf16[256,1024]{1,0:T(8,128)(2,1)S(1)}, bf16[256,1024]{1,0:T(8,128)(2,1)}, u32[]{:S(2)}, u32[]{:S(2)}) collective-permute-start(bf16[256,1024]{1,0:T(8,128)(2,1)S(1)} %get-tuple-element.18.v0.values), channel_id=1, source_target_pairs={{0,4},{4,8},{8,12},{12,16},{16,20},{20,24},{24,28},{28,32},{32,36}... | collective-permute-start | bytes 1572872 | tf_op jit(solution)/shard_map/ppermute | solution.py:41
  52.6 22.1 %collective-permute-start.12 = (bf16[256,1024]{1,0:T(8,128)(2,1)}, bf16[256,1024]{1,0:T(8,128)(2,1)S(1)}, u32[]{:S(2)}, u32[]{:S(2)}) collective-permute-start(bf16[256,1024]{1,0:T(8,128)(2,1)} %collective-permute-done.11.q1), channel_id=1, source_target_pairs={{0,124},{4,0},{8,4},{12,8},{16,12},{20,16},{24,20},{28,24},{32,28}... | collective-permute-start | bytes 1572872 | tf_op jit(solution)/shard_map/ppermute | solution.py:41
  58.9 15.9 %collective-permute-start.14 = (bf16[256,1024]{1,0:T(8,128)(2,1)}, bf16[256,1024]{1,0:T(8,128)(2,1)S(1)}, u32[]{:S(2)}, u32[]{:S(2)}) collective-permute-start(bf16[256,1024]{1,0:T(8,128)(2,1)} %collective-permute-done.13.d1), channel_id=1, source_target_pairs={{0,124},{4,0},{8,4},{12,8},{16,12},{20,16},{24,20},{28,24},{32,28}... | collective-permute-start | bytes 1572872 | tf_op jit(solution)/shard_map/ppermute | solution.py:41
  58.9 10.5 %collective-permute-start.17 = (f32[1,256]{1,0:T(1,128)S(1)}, f32[1,256]{1,0:T(1,128)S(1)}, u32[]{:S(2)}, u32[]{:S(2)}) collective-permute-start(f32[1,256]{1,0:T(1,128)S(1)} %get-tuple-element.20.s0), channel_id=1, source_target_pairs={{0,4},{4,8},{8,12},{12,16},{16,20},{20,24},{24,28},{28,32},{32,36}... | collective-permute-start | bytes 3080 | tf_op jit(solution)/shard_map/ppermute | solution.py:41
  63.7 8.1 %collective-permute-start.18 = (f32[1,256]{1,0:T(1,128)S(1)}, f32[1,256]{1,0:T(1,128)S(1)}, u32[]{:S(2)}, u32[]{:S(2)}) collective-permute-start(f32[1,256]{1,0:T(1,128)S(1)} %get-tuple-element.20.s0), channel_id=1, source_target_pairs={{0,8},{4,12},{8,16},{12,20},{16,24},{20,28},{24,32},{28,36},{32,40... | collective-permute-start | bytes 3080 | tf_op jit(solution)/shard_map/ppermute | solution.py:41
  69.5 5.3 %collective-permute-start.15 = (f32[8,256]{1,0:T(8,128)S(1)}, f32[8,256]{1,0:T(8,128)S(1)}, u32[]{:S(2)}, u32[]{:S(2)}) collective-permute-start(f32[8,256]{1,0:T(8,128)S(1)} %row_totals.1.t0.totals), channel_id=1, source_target_pairs={{0,124},{4,0},{8,4},{12,8},{16,12},{20,16},{24,20},{28,24},{32,28}... | collective-permute-start | bytes 24584 | tf_op jit(solution)/shard_map/ppermute | solution.py:41
  71.8 5.2 %collective-permute-start.16 = (f32[8,256]{1,0:T(8,128)S(1)}, f32[8,256]{1,0:T(8,128)S(1)}, u32[]{:S(2)}, u32[]{:S(2)}) collective-permute-start(f32[8,256]{1,0:T(8,128)S(1)} %row_totals.1.t0.totals), channel_id=1, source_target_pairs={{0,120},{4,124},{8,0},{12,4},{16,8},{20,12},{24,16},{28,20},{32,24... | collective-permute-start | bytes 24584 | tf_op jit(solution)/shard_map/ppermute | solution.py:41
  73.4 28.2 %collective-permute-start.10 = (bf16[256,1024]{1,0:T(8,128)(2,1)}, bf16[256,1024]{1,0:T(8,128)(2,1)}, u32[]{:S(2)}, u32[]{:S(2)}) collective-permute-start(bf16[256,1024]{1,0:T(8,128)(2,1)} %collective-permute-done.9.v1), channel_id=1, source_target_pairs={{0,4},{4,8},{8,12},{12,16},{16,20},{20,24},{24,28},{28,32},{32,36}... | collective-permute-start | bytes 1572872 | tf_op jit(solution)/shard_map/ppermute | solution.py:41
  92.0 6.1 %collective-permute-start.21 = (f32[128,128]{1,0:T(8,128)S(1)}, f32[128,128]{1,0:T(8,128)S(1)}, u32[]{:S(2)}, u32[]{:S(2)}) collective-permute-start(f32[128,128]{1,0:T(8,128)S(1)} %get-tuple-element.27), channel_id=1, source_target_pairs={{0,12},{4,0},{8,4},{12,8},{16,28},{20,16},{24,20},{28,24},{32,44},... | collective-permute-start | bytes 196616 | tf_op jit(solution)/shard_map/ppermute | solution.py:51
  95.0 6.1 %collective-permute-start.22 = (f32[128,128]{1,0:T(8,128)S(1)}, f32[128,128]{1,0:T(8,128)S(1)}, u32[]{:S(2)}, u32[]{:S(2)}) collective-permute-start(f32[128,128]{1,0:T(8,128)S(1)} %get-tuple-element.27), channel_id=1, source_target_pairs={{0,8},{4,12},{8,0},{12,4},{16,24},{20,28},{24,16},{28,20},{32,40},... | collective-permute-start | bytes 196616 | tf_op jit(solution)/shard_map/ppermute | solution.py:51
  95.0 6.4 %collective-permute-start.23 = (f32[128,128]{1,0:T(8,128)S(1)}, f32[128,128]{1,0:T(8,128)S(1)}, u32[]{:S(2)}, u32[]{:S(2)}) collective-permute-start(f32[128,128]{1,0:T(8,128)S(1)} %get-tuple-element.27), channel_id=1, source_target_pairs={{0,4},{4,8},{8,12},{12,0},{16,20},{20,24},{24,28},{28,16},{32,36},... | collective-permute-start | bytes 196616 | tf_op jit(solution)/shard_map/ppermute | solution.py:51
  101.5 15.5 %collective-permute-start.24 = (f32[128,128]{1,0:T(8,128)S(1)}, f32[128,128]{1,0:T(8,128)S(1)}, u32[]{:S(2)}, u32[]{:S(2)}) collective-permute-start(f32[128,128]{1,0:T(8,128)S(1)} %multiply_add_fusion.1), channel_id=1, source_target_pairs={{0,16},{4,20},{8,24},{12,28},{16,0},{20,4},{24,8},{28,12},{32,48},... | collective-permute-start | bytes 196616 | tf_op jit(solution)/shard_map/ppermute | solution.py:51
  111.4 7.7 %collective-permute-start.19 = (f32[8,256]{1,0:T(8,128)}, f32[8,256]{1,0:T(8,128)S(1)}, u32[]{:S(2)}, u32[]{:S(2)}) collective-permute-start(f32[8,256]{1,0:T(8,128)} %get-tuple-element.24.e0), channel_id=1, source_target_pairs={{0,124},{4,0},{8,4},{12,8},{16,12},{20,16},{24,20},{28,24},{32,28}... | collective-permute-start | bytes 24584 | tf_op jit(solution)/shard_map/ppermute | solution.py:41
  116.4 5.4 %collective-permute-start.20 = (f32[8,256]{1,0:T(8,128)}, f32[8,256]{1,0:T(8,128)S(1)}, u32[]{:S(2)}, u32[]{:S(2)}) collective-permute-start(f32[8,256]{1,0:T(8,128)} %get-tuple-element.24.e0), channel_id=1, source_target_pairs={{0,120},{4,124},{8,0},{12,4},{16,8},{20,12},{24,16},{28,20},{32,24... | collective-permute-start | bytes 24584 | tf_op jit(solution)/shard_map/ppermute | solution.py:41
  117.0 11.7 %collective-permute-start.25 = (f32[128,128]{1,0:T(8,128)S(1)}, f32[128,128]{1,0:T(8,128)S(1)}, u32[]{:S(2)}, u32[]{:S(2)}) collective-permute-start(f32[128,128]{1,0:T(8,128)S(1)} %get-tuple-element.28), channel_id=1, source_target_pairs={{0,96},{4,100},{8,104},{12,108},{16,112},{20,116},{24,120},{28,124... | collective-permute-start | bytes 196616 | tf_op jit(solution)/shard_map/ppermute | solution.py:51
  117.6 11.1 %collective-permute-start.26 = (f32[128,128]{1,0:T(8,128)S(1)}, f32[128,128]{1,0:T(8,128)S(1)}, u32[]{:S(2)}, u32[]{:S(2)}) collective-permute-start(f32[128,128]{1,0:T(8,128)S(1)} %get-tuple-element.28), channel_id=1, source_target_pairs={{0,64},{4,68},{8,72},{12,76},{16,80},{20,84},{24,88},{28,92},{32,9... | collective-permute-start | bytes 196616 | tf_op jit(solution)/shard_map/ppermute | solution.py:51
  118.1 10.6 %collective-permute-start.27 = (f32[128,128]{1,0:T(8,128)S(1)}, f32[128,128]{1,0:T(8,128)S(1)}, u32[]{:S(2)}, u32[]{:S(2)}) collective-permute-start(f32[128,128]{1,0:T(8,128)S(1)} %get-tuple-element.28), channel_id=1, source_target_pairs={{0,32},{4,36},{8,40},{12,44},{16,48},{20,52},{24,56},{28,60},{32,6... | collective-permute-start | bytes 196616 | tf_op jit(solution)/shard_map/ppermute | solution.py:51
  (25 other events, 253.3 us)

commit v4 on v3

--- a/solution.py
+++ b/solution.py
@@ -49,6 +49,10 @@
         return (place[0] * 2 + place[1]) * 4 + place[2]
 
     return lax.ppermute(value, "ctx", [(i, target(i)) for i in range(32)])
+
+
+def after(value, *others):
+    return lax.optimization_barrier((value, *others))[0]
 
 
 def carry_in(final, rate, length, reverse):
@@ -544,10 +548,11 @@
     mix_1 = shifted(scaled_mix, 1)
     mix_2 = shifted(mix_1, 1)
 
-    all_squares = (squares, shifted(squares, 1), shifted(squares, 2))
     totals = row_totals(place, queries, key_vectors, keys_1, keys_2)
     totals_1 = shifted(totals, -1)
     totals_2 = shifted(totals, -2)
+    late = after(squares, totals)
+    all_squares = (squares, shifted(late, 1), shifted(late, 2))
     all_queries = (queries, queries_1, queries_2)
     all_cotangents = (grad_out, cotangent_1, cotangent_2)
     all_totals = (totals, totals_1, totals_2)

time: 133 us -> 131 us (0.985)
  starting transfers between devices: 40.8 us -> 37.6 us
    ppermute x14, starting transfers between devices: 22.9 us -> 20.1 us  [shifted(): lax.ppermute(value, 'ctx', [(i, (i + by) % devices) for i in range(device...]
  transfers between devices with their start and end apart: 28 -> 28, of which waited for: 14 -> 15; matrix products, arithmetic and copies ran while one was open for 0% -> 0% of each run, Pallas kernels for 22% -> 22%
where the time goes in v4:
time: 131 us; the launch traced here: 130 us
  waiting for transfers between devices  44 us (34%)
  starting transfers between devices  37.6 us (29%)
  Pallas kernels  34.1 us (26%)
  blocking collectives  7.57 us (6%)
  local copies, waits for them, and re-layouts  5.75 us (4%)
    ppermute x14, waiting for transfers between devices, along(): return lax.ppermute(value, 'ctx', [(i, target(i)) for i in range(32)])  30.9 us
    pallas_call x4, Pallas kernels, per_head(): pl.pallas_call(kernel, out_shape=out_shape, grid_spec=pltpu.PrefetchScala...  24.4 us
    ppermute x14, starting transfers between devices, shifted(): lax.ppermute(value, 'ctx', [(i, (i + by) % devices) for i in range(device...  20.1 us
    ppermute x14, starting transfers between devices, along(): return lax.ppermute(value, 'ctx', [(i, target(i)) for i in range(32)])  17.5 us
    ppermute x14, waiting for transfers between devices, shifted(): lax.ppermute(value, 'ctx', [(i, (i + by) % devices) for i in range(device...  13.1 us
    psum x1, blocking collectives, shards(): stats = lax.psum(stats, 'tp')  7.57 us
    unnamed x58, local copies, waits for them, and re-layouts  5.75 us
    pallas_call x1, Pallas kernels, backward_mix(): pl.pallas_call(backward_mix_kernel, out_shape=jax.ShapeDtypeStruct((rows,...  3.45 us
  transfers between devices with their start and end apart: 28, of which 15 were waited for; matrix products, arithmetic and copies ran while one was open for 0% of the time, Pallas kernels for 22%

profile of v4, /device:TPU:0, one launch (start us, length us, event | category | flops | bytes accessed | tf_op | source)
XLA Modules:
  0.0 130.2 jit_solution(4083534696057815180)
XLA Ops:
  3.6 1.5 %forward_state.1 = (f32[128,128]{1,0:T(8,128)S(1)}, f32[128,128]{1,0:T(8,128)S(1)}) custom-call(bf16[256,1024]{1,0:T(8,128)(2,1)S(1)} %copy-done.5, bf16[256,1024]{1,0:T(8,128)(2,1)S(1)} %copy-done.13, f32[16,1024]{1,0:T(8,128)S(1)} %bitcast.4), custom_call_target="tpu_custom_call" | custom-call | flops 600000000 | bytes 1200000 | tf_op jit(solution)/shard_map/forward_state/pallas_call | solution.py:159
  5.1 2.1 %collective-permute-start.2 = (f32[128,128]{1,0:T(8,128)S(1)}, f32[128,128]{1,0:T(8,128)S(1)}, u32[]{:S(2)}, u32[]{:S(2)}) collective-permute-start(f32[128,128]{1,0:T(8,128)S(1)} %get-tuple-element.18), channel_id=1, source_target_pairs={{0,4},{4,8},{8,12},{12,0},{16,20},{20,24},{24,28},{28,16},{32,36},... | collective-permute-start | bytes 196616 | tf_op jit(solution)/shard_map/ppermute | solution.py:51
  7.2 3.6 %collective-permute-start.3 = (f32[128,128]{1,0:T(8,128)S(1)}, f32[128,128]{1,0:T(8,128)S(1)}, u32[]{:S(2)}, u32[]{:S(2)}) collective-permute-start(f32[128,128]{1,0:T(8,128)S(1)} %get-tuple-element.18), channel_id=1, source_target_pairs={{0,8},{4,12},{8,0},{12,4},{16,24},{20,28},{24,16},{28,20},{32,40},... | collective-permute-start | bytes 196616 | tf_op jit(solution)/shard_map/ppermute | solution.py:51
  12.8 2.1 %collective-permute-done.3 = f32[128,128]{1,0:T(8,128)S(1)} collective-permute-done((f32[128,128]{1,0:T(8,128)S(1)}, f32[128,128]{1,0:T(8,128)S(1)}, u32[]{:S(2)}, u32[]{:S(2)}) %collective-permute-start.3) | collective-permute-done | bytes 65568 | tf_op jit(solution)/shard_map/ppermute | solution.py:51
  15.1 1.7 %collective-permute-start.5 = (f32[128,128]{1,0:T(8,128)S(1)}, f32[128,128]{1,0:T(8,128)S(1)}, u32[]{:S(2)}, u32[]{:S(2)}) collective-permute-start(f32[128,128]{1,0:T(8,128)S(1)} %multiply_add_fusion.3), channel_id=1, source_target_pairs={{0,16},{4,20},{8,24},{12,28},{16,0},{20,4},{24,8},{28,12},{32,48},... | collective-permute-start | bytes 196616 | tf_op jit(solution)/shard_map/ppermute | solution.py:51
  16.8 4.3 %collective-permute-start.11 = (bf16[256,1024]{1,0:T(8,128)(2,1)S(1)}, bf16[256,1024]{1,0:T(8,128)(2,1)}, u32[]{:S(2)}, u32[]{:S(2)}) collective-permute-start(bf16[256,1024]{1,0:T(8,128)(2,1)S(1)} %copy-done.7), channel_id=1, source_target_pairs={{0,124},{4,0},{8,4},{12,8},{16,12},{20,16},{24,20},{28,24},{32,28}... | collective-permute-start | bytes 1572872 | tf_op jit(solution)/shard_map/ppermute | solution.py:41
  21.6 16.9 %collective-permute-done.5 = f32[128,128]{1,0:T(8,128)S(1)} collective-permute-done((f32[128,128]{1,0:T(8,128)S(1)}, f32[128,128]{1,0:T(8,128)S(1)}, u32[]{:S(2)}, u32[]{:S(2)}) %collective-permute-start.5) | collective-permute-done | bytes 65568 | tf_op jit(solution)/shard_map/ppermute | solution.py:51
  38.6 1.6 %collective-permute-start.6 = (f32[128,128]{1,0:T(8,128)S(1)}, f32[128,128]{1,0:T(8,128)S(1)}, u32[]{:S(2)}, u32[]{:S(2)}) collective-permute-start(f32[128,128]{1,0:T(8,128)S(1)} %get-tuple-element.32), channel_id=1, source_target_pairs={{0,32},{4,36},{8,40},{12,44},{16,48},{20,52},{24,56},{28,60},{32,6... | collective-permute-start | bytes 196616 | tf_op jit(solution)/shard_map/ppermute | solution.py:51
  40.1 1.6 %collective-permute-start.7 = (f32[128,128]{1,0:T(8,128)S(1)}, f32[128,128]{1,0:T(8,128)S(1)}, u32[]{:S(2)}, u32[]{:S(2)}) collective-permute-start(f32[128,128]{1,0:T(8,128)S(1)} %get-tuple-element.32), channel_id=1, source_target_pairs={{0,64},{4,68},{8,72},{12,76},{16,80},{20,84},{24,88},{28,92},{32,9... | collective-permute-start | bytes 196616 | tf_op jit(solution)/shard_map/ppermute | solution.py:51
  41.8 2.4 %collective-permute-done.6.p1 = f32[128,128]{1,0:T(8,128)S(1)} collective-permute-done((f32[128,128]{1,0:T(8,128)S(1)}, f32[128,128]{1,0:T(8,128)S(1)}, u32[]{:S(2)}, u32[]{:S(2)}) %collective-permute-start.6) | collective-permute-done | bytes 65568 | tf_op jit(solution)/shard_map/ppermute | solution.py:51
  45.9 2.5 %collective-permute-done.8.p3 = f32[128,128]{1,0:T(8,128)S(1)} collective-permute-done((f32[128,128]{1,0:T(8,128)S(1)}, f32[128,128]{1,0:T(8,128)S(1)}, u32[]{:S(2)}, u32[]{:S(2)}) %collective-permute-start.8) | collective-permute-done | bytes 65568 | tf_op jit(solution)/shard_map/ppermute | solution.py:51
  49.4 3.1 %forward_mix.1 = (f32[256,1024]{1,0:T(8,128)S(1)}, bf16[256,1024]{1,0:T(8,128)(2,1)S(1)}, f32[1,256]{1,0:T(1,128)S(1)}) custom-call(s32[1]{0:T(128)} %bitcast.place, bf16[256,1024]{1,0:T(8,128)(2,1)S(1)} %copy-done.6, bf16[256,1024]{1,0:T(8,128)(2,1)S(1)} %copy-done.14, f32[128,128]{1,0:T(8,128)S(1)} %get-tuple-element.17.rates, f32[16,1024]{1,0:T(8,128)S(1)} %bitcast.5, ...), custom_call_target="tpu_custom_call" | custom-call | flops 1200000000 | bytes 2400000 | tf_op jit(solution)/shard_map/forward_mix/pallas_call | solution.py:218
  52.6 6.2 %collective-permute-start.12 = (bf16[256,1024]{1,0:T(8,128)(2,1)}, bf16[256,1024]{1,0:T(8,128)(2,1)S(1)}, u32[]{:S(2)}, u32[]{:S(2)}) collective-permute-start(bf16[256,1024]{1,0:T(8,128)(2,1)} %collective-permute-done.11.q1), channel_id=1, source_target_pairs={{0,124},{4,0},{8,4},{12,8},{16,12},{20,16},{24,20},{28,24},{32,28}... | collective-permute-start | bytes 1572872 | tf_op jit(solution)/shard_map/ppermute | solution.py:41
  58.9 4.8 %collective-permute-done.1.keys_2.k2 = bf16[256,1024]{1,0:T(8,128)(2,1)S(1)} collective-permute-done((bf16[256,1024]{1,0:T(8,128)(2,1)}, bf16[256,1024]{1,0:T(8,128)(2,1)S(1)}, u32[]{:S(2)}, u32[]{:S(2)}) %collective-permute-start.1) | collective-permute-done | bytes 524320 | tf_op jit(solution)/shard_map/ppermute | solution.py:41
  63.7 3.2 %row_totals.1.t0.totals = f32[8,256]{1,0:T(8,128)S(1)} custom-call(s32[1]{0:T(128)} %bitcast.place, bf16[256,1024]{1,0:T(8,128)(2,1)S(1)} %copy-done.7, bf16[256,1024]{1,0:T(8,128)(2,1)S(1)} %copy-done.11, bf16[256,1024]{1,0:T(8,128)(2,1)} %collective-permute-done.keys_1.k1, bf16[256,1024]{1,0:T(8,128)(2,1)S(1)} %collective-permute-done.1.keys_2.k2), custom_call_target="tpu_custom_call" | custom-call | flops 1200000000 | bytes 2400000 | tf_op jit(solution)/shard_map/row_totals/pallas_call | solution.py:355
  67.2 2.3 %collective-permute-done.9.v1 = bf16[256,1024]{1,0:T(8,128)(2,1)} collective-permute-done((bf16[256,1024]{1,0:T(8,128)(2,1)S(1)}, bf16[256,1024]{1,0:T(8,128)(2,1)}, u32[]{:S(2)}, u32[]{:S(2)}) %collective-permute-start.9) | collective-permute-done | bytes 524320 | tf_op jit(solution)/shard_map/ppermute | solution.py:41
  69.5 3.7 %collective-permute-start.18 = (f32[1,256]{1,0:T(1,128)S(1)}, f32[1,256]{1,0:T(1,128)S(1)}, u32[]{:S(2)}, u32[]{:S(2)}) collective-permute-start(f32[1,256]{1,0:T(1,128)S(1)} %get-tuple-element.22.s0), channel_id=1, source_target_pairs={{0,8},{4,12},{8,16},{12,20},{16,24},{20,28},{24,32},{28,36},{32,40... | collective-permute-start | bytes 3080 | tf_op jit(solution)/shard_map/ppermute | solution.py:41
  73.2 1.5 %collective-permute-done.14.d2 = bf16[256,1024]{1,0:T(8,128)(2,1)S(1)} collective-permute-done((bf16[256,1024]{1,0:T(8,128)(2,1)}, bf16[256,1024]{1,0:T(8,128)(2,1)S(1)}, u32[]{:S(2)}, u32[]{:S(2)}) %collective-permute-start.14) | collective-permute-done | bytes 524320 | tf_op jit(solution)/shard_map/ppermute | solution.py:41
  74.7 2.7 %collective-permute-done.17.s1 = f32[1,256]{1,0:T(1,128)S(1)} collective-permute-done((f32[1,256]{1,0:T(1,128)S(1)}, f32[1,256]{1,0:T(1,128)S(1)}, u32[]{:S(2)}, u32[]{:S(2)}) %collective-permute-start.17) | collective-permute-done | bytes 1056 | tf_op jit(solution)/shard_map/ppermute | solution.py:41
  77.6 5.2 %value_grads.1 = (f32[256,1024]{1,0:T(8,128)S(1)}, f32[4,256]{1,0:T(4,128)S(1)}) custom-call(s32[1]{0:T(128)} %bitcast.place, bf16[256,1024]{1,0:T(8,128)(2,1)S(1)} %copy-done.11, bf16[256,1024]{1,0:T(8,128)(2,1)S(1)} %copy-done.8, bf16[256,1024]{1,0:T(8,128)(2,1)} %collective-permute-done.11.q1, bf16[256,1024]{1,0:T(8,128)(2,1)S(1)} %collective-permute-done.12.q2, ...), custom_call_target="tpu_custom_call" | custom-call | flops 2100000000 | bytes 4200000 | tf_op jit(solution)/shard_map/value_grads/pallas_call | solution.py:355
  82.9 7.6 %psum.7.stats.squares = f32[4,256]{1,0:T(4,128)S(1)} all-reduce(f32[4,256]{1,0:T(4,128)S(1)} %get-tuple-element.23), channel_id=1, replica_groups=mesh['ctx'=32,'tp'=4] {'tp'}, use_global_device_ids=true, to_apply=%region_0.1 | all-reduce | flops 1024 | bytes 8192 | tf_op jit(solution)/shard_map/psum | solution.py:562
  90.4 1.6 %backward_state.1 = (f32[128,128]{1,0:T(8,128)S(1)}, f32[2048,128]{1,0:T(8,128)S(1)}) custom-call(f32[256,1024]{1,0:T(8,128)S(1)} %get-tuple-element.27.scaled, f32[256,1024]{1,0:T(8,128)S(1)} %get-tuple-element.20.mixed, bf16[256,1024]{1,0:T(8,128)(2,1)S(1)} %copy-done, f32[4,256]{1,0:T(4,128)S(1)} %psum.7.stats.squares, f32[128,128]{1,0:T(8,128)S(1)} %get-tuple-element.17.rates), custom_call_target="tpu_custom_call" | custom-call | flops 600000000 | bytes 1200000 | tf_op jit(solution)/shard_map/backward_state/pallas_call | solution.py:263
  93.1 2.8 %collective-permute-start.22 = (f32[128,128]{1,0:T(8,128)S(1)}, f32[128,128]{1,0:T(8,128)S(1)}, u32[]{:S(2)}, u32[]{:S(2)}) collective-permute-start(f32[128,128]{1,0:T(8,128)S(1)} %get-tuple-element.29), channel_id=1, source_target_pairs={{0,8},{4,12},{8,0},{12,4},{16,24},{20,28},{24,16},{28,20},{32,40},... | collective-permute-start | bytes 196616 | tf_op jit(solution)/shard_map/ppermute | solution.py:51
  95.9 1.5 %collective-permute-done.21 = f32[128,128]{1,0:T(8,128)S(1)} collective-permute-done((f32[128,128]{1,0:T(8,128)S(1)}, f32[128,128]{1,0:T(8,128)S(1)}, u32[]{:S(2)}, u32[]{:S(2)}) %collective-permute-start.21) | collective-permute-done | bytes 65568 | tf_op jit(solution)/shard_map/ppermute | solution.py:51
  97.4 1.7 %collective-permute-done.22 = f32[128,128]{1,0:T(8,128)S(1)} collective-permute-done((f32[128,128]{1,0:T(8,128)S(1)}, f32[128,128]{1,0:T(8,128)S(1)}, u32[]{:S(2)}, u32[]{:S(2)}) %collective-permute-start.22) | collective-permute-done | bytes 65568 | tf_op jit(solution)/shard_map/ppermute | solution.py:51
  99.1 2.3 %collective-permute-done.23 = f32[128,128]{1,0:T(8,128)S(1)} collective-permute-done((f32[128,128]{1,0:T(8,128)S(1)}, f32[128,128]{1,0:T(8,128)S(1)}, u32[]{:S(2)}, u32[]{:S(2)}) %collective-permute-start.23) | collective-permute-done | bytes 65568 | tf_op jit(solution)/shard_map/ppermute | solution.py:51
  102.0 9.8 %attend.1 = (bf16[256,1024]{1,0:T(8,128)(2,1)}, bf16[256,1024]{1,0:T(8,128)(2,1)}, f32[8,256]{1,0:T(8,128)}) custom-call(s32[1]{0:T(128)} %bitcast.place, bf16[256,1024]{1,0:T(8,128)(2,1)} %q0.3, bf16[256,1024]{1,0:T(8,128)(2,1)} %d0.3, bf16[256,1024]{1,0:T(8,128)(2,1)} %keys.5, bf16[256,1024]{1,0:T(8,128)(2,1)} %collective-permute-done.keys_1.k1, ...), custom_call_target="tpu_custom_call" | custom-call | flops 3000000000 | bytes 6000000 | tf_op jit(solution)/shard_map/attend/pallas_call | solution.py:355
  111.8 2.6 %collective-permute-start.19 = (f32[8,256]{1,0:T(8,128)}, f32[8,256]{1,0:T(8,128)S(1)}, u32[]{:S(2)}, u32[]{:S(2)}) collective-permute-start(f32[8,256]{1,0:T(8,128)} %get-tuple-element.26.e0), channel_id=1, source_target_pairs={{0,124},{4,0},{8,4},{12,8},{16,12},{20,16},{24,20},{28,24},{32,28}... | collective-permute-start | bytes 24584 | tf_op jit(solution)/shard_map/ppermute | solution.py:41
  116.7 1.5 %collective-permute-start.26 = (f32[128,128]{1,0:T(8,128)S(1)}, f32[128,128]{1,0:T(8,128)S(1)}, u32[]{:S(2)}, u32[]{:S(2)}) collective-permute-start(f32[128,128]{1,0:T(8,128)S(1)} %get-tuple-element.30), channel_id=1, source_target_pairs={{0,64},{4,68},{8,72},{12,76},{16,80},{20,84},{24,88},{28,92},{32,9... | collective-permute-start | bytes 196616 | tf_op jit(solution)/shard_map/ppermute | solution.py:51
  118.2 1.5 %collective-permute-done.20.e2 = f32[8,256]{1,0:T(8,128)S(1)} collective-permute-done((f32[8,256]{1,0:T(8,128)}, f32[8,256]{1,0:T(8,128)S(1)}, u32[]{:S(2)}, u32[]{:S(2)}) %collective-permute-start.20) | collective-permute-done | bytes 8224 | tf_op jit(solution)/shard_map/ppermute | solution.py:41
  120.5 6.2 %key_grads.1 = bf16[256,1024]{1,0:T(8,128)(2,1)} custom-call(s32[1]{0:T(128)} %bitcast.place, bf16[256,1024]{1,0:T(8,128)(2,1)S(1)} %copy-done.12, bf16[256,1024]{1,0:T(8,128)(2,1)S(1)} %copy-done.17, bf16[256,1024]{1,0:T(8,128)(2,1)S(1)} %copy-done.9, bf16[256,1024]{1,0:T(8,128)(2,1)} %collective-permute-done.11.q1, bf16[256,1024]{1,0:T(8,128)(2,1)S(1)} %copy-done.19, ...), custom_call_target="tpu_custom_call" | custom-call | flops 2400000000 | bytes 4800000 | tf_op jit(solution)/shard_map/key_grads/pallas_call | solution.py:355
  126.8 3.5 %backward_mix.1 = bf16[256,1024]{1,0:T(8,128)(2,1)} custom-call(s32[1]{0:T(128)} %bitcast.place, f32[2048,128]{1,0:T(8,128)S(1)} %copy-done.4, f32[128,128]{1,0:T(8,128)S(1)} %get-tuple-element.17.rates, f32[16,1024]{1,0:T(8,128)S(1)} %bitcast.6, f32[128,128]{1,0:T(8,128)S(1)} %get-tuple-element.31.start, f32[128,128]{1,0:T(8,128)S(1)} %collective-permute-done.25.p1, ...), custom_call_target="tpu_custom_call" | custom-call | flops 1200000000 | bytes 2400000 | tf_op jit(solution)/shard_map/backward_mix/pallas_call | solution.py:291
  (95 shorter events, 13.9 us)
Async XLA Ops:
  3.6 44.8 %copy-start.24 = (f32[1024,16]{0,1:T(8,128)S(1)}, f32[1024,16]{0,1:T(8,128)}, u32[]{:S(2)}) copy-start(f32[1024,16]{0,1:T(8,128)} %param.12) | copy-start | bytes 196612
  5.1 7.7 %collective-permute-start.2 = (f32[128,128]{1,0:T(8,128)S(1)}, f32[128,128]{1,0:T(8,128)S(1)}, u32[]{:S(2)}, u32[]{:S(2)}) collective-permute-start(f32[128,128]{1,0:T(8,128)S(1)} %get-tuple-element.18), channel_id=1, source_target_pairs={{0,4},{4,8},{8,12},{12,0},{16,20},{20,24},{24,28},{28,16},{32,36},... | collective-permute-start | bytes 196616 | tf_op jit(solution)/shard_map/ppermute | solution.py:51
  7.2 7.7 %collective-permute-start.3 = (f32[128,128]{1,0:T(8,128)S(1)}, f32[128,128]{1,0:T(8,128)S(1)}, u32[]{:S(2)}, u32[]{:S(2)}) collective-permute-start(f32[128,128]{1,0:T(8,128)S(1)} %get-tuple-element.18), channel_id=1, source_target_pairs={{0,8},{4,12},{8,0},{12,4},{16,24},{20,28},{24,16},{28,20},{32,40},... | collective-permute-start | bytes 196616 | tf_op jit(solution)/shard_map/ppermute | solution.py:51
  10.8 4.3 %collective-permute-start.4 = (f32[128,128]{1,0:T(8,128)S(1)}, f32[128,128]{1,0:T(8,128)S(1)}, u32[]{:S(2)}, u32[]{:S(2)}) collective-permute-start(f32[128,128]{1,0:T(8,128)S(1)} %get-tuple-element.18), channel_id=1, source_target_pairs={{0,12},{4,0},{8,4},{12,8},{16,28},{20,16},{24,20},{28,24},{32,44},... | collective-permute-start | bytes 196616 | tf_op jit(solution)/shard_map/ppermute | solution.py:51
  11.8 32.7 %collective-permute-start = (bf16[256,1024]{1,0:T(8,128)(2,1)S(1)}, bf16[256,1024]{1,0:T(8,128)(2,1)}, u32[]{:S(2)}, u32[]{:S(2)}) collective-permute-start(bf16[256,1024]{1,0:T(8,128)(2,1)S(1)} %copy-done.10), channel_id=1, source_target_pairs={{0,4},{4,8},{8,12},{12,16},{16,20},{20,24},{24,28},{28,32},{32,36}... | collective-permute-start | bytes 1572872 | tf_op jit(solution)/shard_map/ppermute | solution.py:41
  12.8 35.6 %copy-start.28 = (f32[1024]{0:T(1024)S(1)}, f32[1024]{0:T(1024)}, u32[]{:S(2)}) copy-start(f32[1024]{0:T(1024)} %param.14) | copy-start | bytes 12292
  12.8 35.6 %copy-start = (bf16[256,1024]{1,0:T(8,128)(2,1)S(1)}, bf16[256,1024]{1,0:T(8,128)(2,1)}, u32[]{:S(2)}) copy-start(bf16[256,1024]{1,0:T(8,128)(2,1)} %gate_out.3) | copy-start | bytes 1572868
  12.8 35.6 %copy-start.6 = (bf16[256,1024]{1,0:T(8,128)(2,1)S(1)}, bf16[256,1024]{1,0:T(8,128)(2,1)}, u32[]{:S(2)}) copy-start(bf16[256,1024]{1,0:T(8,128)(2,1)} %mixer.3) | copy-start | bytes 1572868
  15.1 23.4 %collective-permute-start.5 = (f32[128,128]{1,0:T(8,128)S(1)}, f32[128,128]{1,0:T(8,128)S(1)}, u32[]{:S(2)}, u32[]{:S(2)}) collective-permute-start(f32[128,128]{1,0:T(8,128)S(1)} %multiply_add_fusion.3), channel_id=1, source_target_pairs={{0,16},{4,20},{8,24},{12,28},{16,0},{20,4},{24,8},{28,12},{32,48},... | collective-permute-start | bytes 196616 | tf_op jit(solution)/shard_map/ppermute | solution.py:51
  16.8 35.9 %collective-permute-start.11 = (bf16[256,1024]{1,0:T(8,128)(2,1)S(1)}, bf16[256,1024]{1,0:T(8,128)(2,1)}, u32[]{:S(2)}, u32[]{:S(2)}) collective-permute-start(bf16[256,1024]{1,0:T(8,128)(2,1)S(1)} %copy-done.7), channel_id=1, source_target_pairs={{0,124},{4,0},{8,4},{12,8},{16,12},{20,16},{24,20},{28,24},{32,28}... | collective-permute-start | bytes 1572872 | tf_op jit(solution)/shard_map/ppermute | solution.py:41
  21.1 37.8 %collective-permute-start.13 = (bf16[256,1024]{1,0:T(8,128)(2,1)}, bf16[256,1024]{1,0:T(8,128)(2,1)}, u32[]{:S(2)}, u32[]{:S(2)}) collective-permute-start(bf16[256,1024]{1,0:T(8,128)(2,1)} %d0.3), channel_id=1, source_target_pairs={{0,124},{4,0},{8,4},{12,8},{16,12},{20,16},{24,20},{28,24},{32,28}... | collective-permute-start | bytes 1572872 | tf_op jit(solution)/shard_map/ppermute | solution.py:41
  38.6 5.5 %collective-permute-start.6 = (f32[128,128]{1,0:T(8,128)S(1)}, f32[128,128]{1,0:T(8,128)S(1)}, u32[]{:S(2)}, u32[]{:S(2)}) collective-permute-start(f32[128,128]{1,0:T(8,128)S(1)} %get-tuple-element.32), channel_id=1, source_target_pairs={{0,32},{4,36},{8,40},{12,44},{16,48},{20,52},{24,56},{28,60},{32,6... | collective-permute-start | bytes 196616 | tf_op jit(solution)/shard_map/ppermute | solution.py:51
  40.1 5.8 %collective-permute-start.7 = (f32[128,128]{1,0:T(8,128)S(1)}, f32[128,128]{1,0:T(8,128)S(1)}, u32[]{:S(2)}, u32[]{:S(2)}) collective-permute-start(f32[128,128]{1,0:T(8,128)S(1)} %get-tuple-element.32), channel_id=1, source_target_pairs={{0,64},{4,68},{8,72},{12,76},{16,80},{20,84},{24,88},{28,92},{32,9... | collective-permute-start | bytes 196616 | tf_op jit(solution)/shard_map/ppermute | solution.py:51
  44.1 4.3 %collective-permute-start.8 = (f32[128,128]{1,0:T(8,128)S(1)}, f32[128,128]{1,0:T(8,128)S(1)}, u32[]{:S(2)}, u32[]{:S(2)}) collective-permute-start(f32[128,128]{1,0:T(8,128)S(1)} %get-tuple-element.32), channel_id=1, source_target_pairs={{0,96},{4,100},{8,104},{12,108},{16,112},{20,116},{24,120},{28,124... | collective-permute-start | bytes 196616 | tf_op jit(solution)/shard_map/ppermute | solution.py:51
  44.5 19.3 %collective-permute-start.1 = (bf16[256,1024]{1,0:T(8,128)(2,1)}, bf16[256,1024]{1,0:T(8,128)(2,1)S(1)}, u32[]{:S(2)}, u32[]{:S(2)}) collective-permute-start(bf16[256,1024]{1,0:T(8,128)(2,1)} %collective-permute-done.keys_1.k1), channel_id=1, source_target_pairs={{0,4},{4,8},{8,12},{12,16},{16,20},{20,24},{24,28},{28,32},{32,36}... | collective-permute-start | bytes 1572872 | tf_op jit(solution)/shard_map/ppermute | solution.py:41
  52.6 16.9 %collective-permute-start.9 = (bf16[256,1024]{1,0:T(8,128)(2,1)S(1)}, bf16[256,1024]{1,0:T(8,128)(2,1)}, u32[]{:S(2)}, u32[]{:S(2)}) collective-permute-start(bf16[256,1024]{1,0:T(8,128)(2,1)S(1)} %get-tuple-element.19.v0.values), channel_id=1, source_target_pairs={{0,4},{4,8},{8,12},{12,16},{16,20},{20,24},{24,28},{28,32},{32,36}... | collective-permute-start | bytes 1572872 | tf_op jit(solution)/shard_map/ppermute | solution.py:41
  52.6 16.8 %collective-permute-start.12 = (bf16[256,1024]{1,0:T(8,128)(2,1)}, bf16[256,1024]{1,0:T(8,128)(2,1)S(1)}, u32[]{:S(2)}, u32[]{:S(2)}) collective-permute-start(bf16[256,1024]{1,0:T(8,128)(2,1)} %collective-permute-done.11.q1), channel_id=1, source_target_pairs={{0,124},{4,0},{8,4},{12,8},{16,12},{20,16},{24,20},{28,24},{32,28}... | collective-permute-start | bytes 1572872 | tf_op jit(solution)/shard_map/ppermute | solution.py:41
  58.9 15.8 %collective-permute-start.14 = (bf16[256,1024]{1,0:T(8,128)(2,1)}, bf16[256,1024]{1,0:T(8,128)(2,1)S(1)}, u32[]{:S(2)}, u32[]{:S(2)}) collective-permute-start(bf16[256,1024]{1,0:T(8,128)(2,1)} %collective-permute-done.13.d1), channel_id=1, source_target_pairs={{0,124},{4,0},{8,4},{12,8},{16,12},{20,16},{24,20},{28,24},{32,28}... | collective-permute-start | bytes 1572872 | tf_op jit(solution)/shard_map/ppermute | solution.py:41
  66.9 10.7 %collective-permute-start.15 = (f32[8,256]{1,0:T(8,128)S(1)}, f32[8,256]{1,0:T(8,128)S(1)}, u32[]{:S(2)}, u32[]{:S(2)}) collective-permute-start(f32[8,256]{1,0:T(8,128)S(1)} %row_totals.1.t0.totals), channel_id=1, source_target_pairs={{0,124},{4,0},{8,4},{12,8},{16,12},{20,16},{24,20},{28,24},{32,28}... | collective-permute-start | bytes 24584 | tf_op jit(solution)/shard_map/ppermute | solution.py:41
  67.0 10.6 %collective-permute-start.16 = (f32[8,256]{1,0:T(8,128)S(1)}, f32[8,256]{1,0:T(8,128)S(1)}, u32[]{:S(2)}, u32[]{:S(2)}) collective-permute-start(f32[8,256]{1,0:T(8,128)S(1)} %row_totals.1.t0.totals), channel_id=1, source_target_pairs={{0,120},{4,124},{8,0},{12,4},{16,8},{20,12},{24,16},{28,20},{32,24... | collective-permute-start | bytes 24584 | tf_op jit(solution)/shard_map/ppermute | solution.py:41
  69.5 7.9 %collective-permute-start.17 = (f32[1,256]{1,0:T(1,128)S(1)}, f32[1,256]{1,0:T(1,128)S(1)}, u32[]{:S(2)}, u32[]{:S(2)}) collective-permute-start(f32[1,256]{1,0:T(1,128)S(1)} %get-tuple-element.22.s0), channel_id=1, source_target_pairs={{0,4},{4,8},{8,12},{12,16},{16,20},{20,24},{24,28},{28,32},{32,36}... | collective-permute-start | bytes 3080 | tf_op jit(solution)/shard_map/ppermute | solution.py:41
  69.5 8.2 %collective-permute-start.18 = (f32[1,256]{1,0:T(1,128)S(1)}, f32[1,256]{1,0:T(1,128)S(1)}, u32[]{:S(2)}, u32[]{:S(2)}) collective-permute-start(f32[1,256]{1,0:T(1,128)S(1)} %get-tuple-element.22.s0), channel_id=1, source_target_pairs={{0,8},{4,12},{8,16},{12,20},{16,24},{20,28},{24,32},{28,36},{32,40... | collective-permute-start | bytes 3080 | tf_op jit(solution)/shard_map/ppermute | solution.py:41
  74.7 27.3 %collective-permute-start.10 = (bf16[256,1024]{1,0:T(8,128)(2,1)}, bf16[256,1024]{1,0:T(8,128)(2,1)}, u32[]{:S(2)}, u32[]{:S(2)}) collective-permute-start(bf16[256,1024]{1,0:T(8,128)(2,1)} %collective-permute-done.9.v1), channel_id=1, source_target_pairs={{0,4},{4,8},{8,12},{12,16},{16,20},{20,24},{24,28},{28,32},{32,36}... | collective-permute-start | bytes 1572872 | tf_op jit(solution)/shard_map/ppermute | solution.py:41
  93.1 4.3 %collective-permute-start.21 = (f32[128,128]{1,0:T(8,128)S(1)}, f32[128,128]{1,0:T(8,128)S(1)}, u32[]{:S(2)}, u32[]{:S(2)}) collective-permute-start(f32[128,128]{1,0:T(8,128)S(1)} %get-tuple-element.29), channel_id=1, source_target_pairs={{0,12},{4,0},{8,4},{12,8},{16,28},{20,16},{24,20},{28,24},{32,44},... | collective-permute-start | bytes 196616 | tf_op jit(solution)/shard_map/ppermute | solution.py:51
  93.1 6.0 %collective-permute-start.22 = (f32[128,128]{1,0:T(8,128)S(1)}, f32[128,128]{1,0:T(8,128)S(1)}, u32[]{:S(2)}, u32[]{:S(2)}) collective-permute-start(f32[128,128]{1,0:T(8,128)S(1)} %get-tuple-element.29), channel_id=1, source_target_pairs={{0,8},{4,12},{8,0},{12,4},{16,24},{20,28},{24,16},{28,20},{32,40},... | collective-permute-start | bytes 196616 | tf_op jit(solution)/shard_map/ppermute | solution.py:51
  95.9 5.5 %collective-permute-start.23 = (f32[128,128]{1,0:T(8,128)S(1)}, f32[128,128]{1,0:T(8,128)S(1)}, u32[]{:S(2)}, u32[]{:S(2)}) collective-permute-start(f32[128,128]{1,0:T(8,128)S(1)} %get-tuple-element.29), channel_id=1, source_target_pairs={{0,4},{4,8},{8,12},{12,0},{16,20},{20,24},{24,28},{28,16},{32,36},... | collective-permute-start | bytes 196616 | tf_op jit(solution)/shard_map/ppermute | solution.py:51
  101.5 14.4 %collective-permute-start.24 = (f32[128,128]{1,0:T(8,128)S(1)}, f32[128,128]{1,0:T(8,128)S(1)}, u32[]{:S(2)}, u32[]{:S(2)}) collective-permute-start(f32[128,128]{1,0:T(8,128)S(1)} %multiply_add_fusion.1), channel_id=1, source_target_pairs={{0,16},{4,20},{8,24},{12,28},{16,0},{20,4},{24,8},{28,12},{32,48},... | collective-permute-start | bytes 196616 | tf_op jit(solution)/shard_map/ppermute | solution.py:51
  111.8 6.4 %collective-permute-start.19 = (f32[8,256]{1,0:T(8,128)}, f32[8,256]{1,0:T(8,128)S(1)}, u32[]{:S(2)}, u32[]{:S(2)}) collective-permute-start(f32[8,256]{1,0:T(8,128)} %get-tuple-element.26.e0), channel_id=1, source_target_pairs={{0,124},{4,0},{8,4},{12,8},{16,12},{20,16},{24,20},{28,24},{32,28}... | collective-permute-start | bytes 24584 | tf_op jit(solution)/shard_map/ppermute | solution.py:41
  114.4 5.4 %collective-permute-start.20 = (f32[8,256]{1,0:T(8,128)}, f32[8,256]{1,0:T(8,128)S(1)}, u32[]{:S(2)}, u32[]{:S(2)}) collective-permute-start(f32[8,256]{1,0:T(8,128)} %get-tuple-element.26.e0), channel_id=1, source_target_pairs={{0,120},{4,124},{8,0},{12,4},{16,8},{20,12},{24,16},{28,20},{32,24... | collective-permute-start | bytes 24584 | tf_op jit(solution)/shard_map/ppermute | solution.py:41
  115.9 10.8 %collective-permute-start.25 = (f32[128,128]{1,0:T(8,128)S(1)}, f32[128,128]{1,0:T(8,128)S(1)}, u32[]{:S(2)}, u32[]{:S(2)}) collective-permute-start(f32[128,128]{1,0:T(8,128)S(1)} %get-tuple-element.30), channel_id=1, source_target_pairs={{0,96},{4,100},{8,104},{12,108},{16,112},{20,116},{24,120},{28,124... | collective-permute-start | bytes 196616 | tf_op jit(solution)/shard_map/ppermute | solution.py:51
  116.7 10.0 %collective-permute-start.26 = (f32[128,128]{1,0:T(8,128)S(1)}, f32[128,128]{1,0:T(8,128)S(1)}, u32[]{:S(2)}, u32[]{:S(2)}) collective-permute-start(f32[128,128]{1,0:T(8,128)S(1)} %get-tuple-element.30), channel_id=1, source_target_pairs={{0,64},{4,68},{8,72},{12,76},{16,80},{20,84},{24,88},{28,92},{32,9... | collective-permute-start | bytes 196616 | tf_op jit(solution)/shard_map/ppermute | solution.py:51
  118.2 8.5 %collective-permute-start.27 = (f32[128,128]{1,0:T(8,128)S(1)}, f32[128,128]{1,0:T(8,128)S(1)}, u32[]{:S(2)}, u32[]{:S(2)}) collective-permute-start(f32[128,128]{1,0:T(8,128)S(1)} %get-tuple-element.30), channel_id=1, source_target_pairs={{0,32},{4,36},{8,40},{12,44},{16,48},{20,52},{24,56},{28,60},{32,6... | collective-permute-start | bytes 196616 | tf_op jit(solution)/shard_map/ppermute | solution.py:51
  (25 other events, 249.7 us)

commit v5 on v4

--- a/solution.py
+++ b/solution.py
@@ -15,9 +15,8 @@
 MASKED = -1e30
 LANES = 128
 SUBLANES = 8
-ROWS_PER_STEP = 8
-HEADS_PER_STEP = 4
-GROUP = HEADS_PER_STEP * HEAD_DIM
+ROWS_PER_STEP = 16
+GROUP = 4 * HEAD_DIM
 f32 = jnp.float32
 bf16 = jnp.bfloat16
 
@@ -323,14 +322,15 @@
 SCALE = 1.0 / math.sqrt(HEAD_DIM)
 
 
-def step_heads():
-    first = pl.program_id(0) * HEADS_PER_STEP
-    return [(first + j, head_slice(j)) for j in range(HEADS_PER_STEP)]
+def step_heads(block):
+    count = block.shape[1] // HEAD_DIM
+    first = pl.program_id(0) * count
+    return [(first + j, head_slice(j)) for j in range(count)]
 
 
 def totals_kernel(place, queries, keys, keys_1, keys_2, totals):
     position = place[0]
-    for head, cut in step_heads():
+    for head, cut in step_heads(keys):
         scores = [
             masked(
                 rows_by_rows(block[:, cut], queries[:, cut]) * (SCALE * LOG2E), offset, position >= offset, True
@@ -342,22 +342,22 @@
         totals[pl.ds(head, 1), :] = top + jnp.log(total) * LOG2E
 
 
-def head_block(rows):
-    return pl.BlockSpec((rows, GROUP), lambda step, *_: (0, step))
+def head_block(rows, group=GROUP):
+    return pl.BlockSpec((rows, group), lambda step, *_: (0, step))
 
 
 def whole(shape):
     return pl.BlockSpec(shape, lambda head, *_: (0,) * len(shape))
 
 
-def per_head(kernel, place, operands, specs, out_shape, out_specs, scratch=(), name=None, time=5, vmem=48):
-    heads = operands[0].shape[1] // GROUP
+def per_head(kernel, place, operands, specs, out_shape, out_specs, scratch=(), name=None, time=5, vmem=48, group=GROUP):
+    steps = operands[0].shape[1] // group
     return pl.pallas_call(
         kernel,
         out_shape=out_shape,
         grid_spec=pltpu.PrefetchScalarGridSpec(
             num_scalar_prefetch=1,
-            grid=(heads,),
+            grid=(steps,),
             in_specs=specs,
             out_specs=out_specs,
             scratch_shapes=scratch,
@@ -371,7 +371,7 @@
 def row_totals(place, queries, keys, keys_1, keys_2):
     rows, width = queries.shape
     shape = (width // HEAD_DIM, rows)
-    block = head_block(rows)
+    block = head_block(rows, width)
     return per_head(
         totals_kernel,
         place,
@@ -380,6 +380,7 @@
         jax.ShapeDtypeStruct(shape, f32),
         whole(shape),
         name="row_totals",
+        group=width,
         time=4,
     )
 
@@ -394,7 +395,7 @@
     def _():
         acc[...] = jnp.zeros_like(acc)
 
-    for head, cut in step_heads():
+    for head, cut in step_heads(keys):
         grad = None
         for offset, (query, cotangent, total) in enumerate(((q0, d0, t0), (q1, d1, t1), (q2, d2, t2))):
             scores = rows_by_rows(keys[:, cut], query[:, cut]) * (SCALE * LOG2E)
@@ -416,17 +417,18 @@
 def value_grads(blocks, place, keys, queries, cotangents, totals, gain, mixed, squares):
     rows, width = keys.shape
     heads = width // HEAD_DIM
-    block = head_block(rows)
+    block = head_block(rows, width)
     stat = whole((heads, rows))
     return per_head(
         functools.partial(value_grads_kernel, blocks),
         place,
         (keys, *queries, *cotangents, *totals, gain, mixed, *squares),
-        [block] * 7 + [stat] * 3 + [head_block(1), block] + [whole((1, rows))] * 3,
+        [block] * 7 + [stat] * 3 + [head_block(1, width), block] + [whole((1, rows))] * 3,
         (jax.ShapeDtypeStruct((rows, width), f32), jax.ShapeDtypeStruct((SPAN + 2, rows), f32)),
         (block, whole((SPAN + 2, rows))),
         scratch=[pltpu.VMEM((rows, LANES), f32)],
         name="value_grads",
+        group=width,
         time=7,
     )
 
@@ -442,7 +444,7 @@
 
     lane = lax.broadcasted_iota(jnp.int32, columns.shape, 1)
     inverses = [inverse_of(stats[i : i + 1, :], full_width) for i in range(SPAN + 1)]
-    for head, cut in step_heads():
+    for head, cut in step_heads(queries):
         log_total = jnp.sum(jnp.where(lane == head, columns[...], 0.0), axis=1, keepdims=True)
         probs = []
         output = None
@@ -493,7 +495,7 @@
     position = place[0]
     inverse = inverse_of(column(squares[0:1, :]), full_width)
     groups = ((q0, d0, t0, e0), (q1, d1, t1, e1), (q2, d2, t2, e2))
-    for head, cut in step_heads():
+    for head, cut in step_heads(keys):
         total = None
         for offset, (query, cotangent, log_total, delta) in enumerate(groups):
             scores = rows_by_rows(keys[:, cut], query[:, cut]) * (SCALE * LOG2E)
@@ -509,7 +511,7 @@
 def key_grads(full_width, blocks, place, keys, values, queries, cotangents, totals, deltas, squares):
     rows, width = keys.shape
     heads = width // HEAD_DIM
-    block = head_block(rows)
+    block = head_block(rows, width)
     stat = whole((heads, rows))
     return per_head(
         functools.partial(key_grads_kernel, full_width, blocks),
@@ -519,6 +521,7 @@
         jax.ShapeDtypeStruct((rows, width), bf16),
         block,
         name="key_grads",
+        group=width,
         time=8,
     )
 

time: 131 us -> 131 us (level)
  no operation moved by 1% of the time
where the time goes in v5:
time: 131 us; the launch traced here: 130 us
  waiting for transfers between devices  44.1 us (34%)
  starting transfers between devices  37.5 us (29%)
  Pallas kernels  33.7 us (26%)
  blocking collectives  7.57 us (6%)
  local copies, waits for them, and re-layouts  5.77 us (4%)
    ppermute x14, waiting for transfers between devices, along(): return lax.ppermute(value, 'ctx', [(i, target(i)) for i in range(32)])  30.9 us
    pallas_call x4, Pallas kernels, per_head(): pl.pallas_call(kernel, out_shape=out_shape, grid_spec=pltpu.PrefetchScala...  24.2 us
    ppermute x14, starting transfers between devices, shifted(): lax.ppermute(value, 'ctx', [(i, (i + by) % devices) for i in range(device...  20 us
    ppermute x14, starting transfers between devices, along(): return lax.ppermute(value, 'ctx', [(i, target(i)) for i in range(32)])  17.5 us
    ppermute x14, waiting for transfers between devices, shifted(): lax.ppermute(value, 'ctx', [(i, (i + by) % devices) for i in range(device...  13.2 us
    psum x1, blocking collectives, shards(): stats = lax.psum(stats, 'tp')  7.57 us
    unnamed x58, local copies, waits for them, and re-layouts  5.77 us
    pallas_call x1, Pallas kernels, backward_mix(): pl.pallas_call(backward_mix_kernel, out_shape=jax.ShapeDtypeStruct((rows,...  3.37 us
  transfers between devices with their start and end apart: 28, of which 15 were waited for; matrix products, arithmetic and copies ran while one was open for 0% of the time, Pallas kernels for 22%

profile of v5, /device:TPU:0, one launch (start us, length us, event | category | flops | bytes accessed | tf_op | source)
XLA Modules:
  0.0 129.9 jit_solution(2159209303047131396)
XLA Ops:
  3.6 1.5 %forward_state.1 = (f32[128,128]{1,0:T(8,128)S(1)}, f32[128,128]{1,0:T(8,128)S(1)}) custom-call(bf16[256,1024]{1,0:T(8,128)(2,1)S(1)} %copy-done.5, bf16[256,1024]{1,0:T(8,128)(2,1)S(1)} %copy-done.13, f32[16,1024]{1,0:T(8,128)S(1)} %bitcast.4), custom_call_target="tpu_custom_call" | custom-call | flops 600000000 | bytes 1200000 | tf_op jit(solution)/shard_map/forward_state/pallas_call | solution.py:158
  5.1 2.1 %collective-permute-start.2 = (f32[128,128]{1,0:T(8,128)S(1)}, f32[128,128]{1,0:T(8,128)S(1)}, u32[]{:S(2)}, u32[]{:S(2)}) collective-permute-start(f32[128,128]{1,0:T(8,128)S(1)} %get-tuple-element.18), channel_id=1, source_target_pairs={{0,4},{4,8},{8,12},{12,0},{16,20},{20,24},{24,28},{28,16},{32,36},... | collective-permute-start | bytes 196616 | tf_op jit(solution)/shard_map/ppermute | solution.py:50
  7.2 3.6 %collective-permute-start.3 = (f32[128,128]{1,0:T(8,128)S(1)}, f32[128,128]{1,0:T(8,128)S(1)}, u32[]{:S(2)}, u32[]{:S(2)}) collective-permute-start(f32[128,128]{1,0:T(8,128)S(1)} %get-tuple-element.18), channel_id=1, source_target_pairs={{0,8},{4,12},{8,0},{12,4},{16,24},{20,28},{24,16},{28,20},{32,40},... | collective-permute-start | bytes 196616 | tf_op jit(solution)/shard_map/ppermute | solution.py:50
  12.8 2.1 %collective-permute-done.3 = f32[128,128]{1,0:T(8,128)S(1)} collective-permute-done((f32[128,128]{1,0:T(8,128)S(1)}, f32[128,128]{1,0:T(8,128)S(1)}, u32[]{:S(2)}, u32[]{:S(2)}) %collective-permute-start.3) | collective-permute-done | bytes 65568 | tf_op jit(solution)/shard_map/ppermute | solution.py:50
  15.1 1.7 %collective-permute-start.5 = (f32[128,128]{1,0:T(8,128)S(1)}, f32[128,128]{1,0:T(8,128)S(1)}, u32[]{:S(2)}, u32[]{:S(2)}) collective-permute-start(f32[128,128]{1,0:T(8,128)S(1)} %multiply_add_fusion.3), channel_id=1, source_target_pairs={{0,16},{4,20},{8,24},{12,28},{16,0},{20,4},{24,8},{28,12},{32,48},... | collective-permute-start | bytes 196616 | tf_op jit(solution)/shard_map/ppermute | solution.py:50
  16.7 4.3 %collective-permute-start.11 = (bf16[256,1024]{1,0:T(8,128)(2,1)S(1)}, bf16[256,1024]{1,0:T(8,128)(2,1)}, u32[]{:S(2)}, u32[]{:S(2)}) collective-permute-start(bf16[256,1024]{1,0:T(8,128)(2,1)S(1)} %copy-done.7), channel_id=1, source_target_pairs={{0,124},{4,0},{8,4},{12,8},{16,12},{20,16},{24,20},{28,24},{32,28}... | collective-permute-start | bytes 1572872 | tf_op jit(solution)/shard_map/ppermute | solution.py:40
  21.5 16.9 %collective-permute-done.5 = f32[128,128]{1,0:T(8,128)S(1)} collective-permute-done((f32[128,128]{1,0:T(8,128)S(1)}, f32[128,128]{1,0:T(8,128)S(1)}, u32[]{:S(2)}, u32[]{:S(2)}) %collective-permute-start.5) | collective-permute-done | bytes 65568 | tf_op jit(solution)/shard_map/ppermute | solution.py:50
  38.5 1.6 %collective-permute-start.6 = (f32[128,128]{1,0:T(8,128)S(1)}, f32[128,128]{1,0:T(8,128)S(1)}, u32[]{:S(2)}, u32[]{:S(2)}) collective-permute-start(f32[128,128]{1,0:T(8,128)S(1)} %get-tuple-element.32), channel_id=1, source_target_pairs={{0,32},{4,36},{8,40},{12,44},{16,48},{20,52},{24,56},{28,60},{32,6... | collective-permute-start | bytes 196616 | tf_op jit(solution)/shard_map/ppermute | solution.py:50
  40.1 1.6 %collective-permute-start.7 = (f32[128,128]{1,0:T(8,128)S(1)}, f32[128,128]{1,0:T(8,128)S(1)}, u32[]{:S(2)}, u32[]{:S(2)}) collective-permute-start(f32[128,128]{1,0:T(8,128)S(1)} %get-tuple-element.32), channel_id=1, source_target_pairs={{0,64},{4,68},{8,72},{12,76},{16,80},{20,84},{24,88},{28,92},{32,9... | collective-permute-start | bytes 196616 | tf_op jit(solution)/shard_map/ppermute | solution.py:50
  41.7 2.4 %collective-permute-done.6.p1 = f32[128,128]{1,0:T(8,128)S(1)} collective-permute-done((f32[128,128]{1,0:T(8,128)S(1)}, f32[128,128]{1,0:T(8,128)S(1)}, u32[]{:S(2)}, u32[]{:S(2)}) %collective-permute-start.6) | collective-permute-done | bytes 65568 | tf_op jit(solution)/shard_map/ppermute | solution.py:50
  45.9 2.5 %collective-permute-done.8.p3 = f32[128,128]{1,0:T(8,128)S(1)} collective-permute-done((f32[128,128]{1,0:T(8,128)S(1)}, f32[128,128]{1,0:T(8,128)S(1)}, u32[]{:S(2)}, u32[]{:S(2)}) %collective-permute-start.8) | collective-permute-done | bytes 65568 | tf_op jit(solution)/shard_map/ppermute | solution.py:50
  49.4 3.0 %forward_mix.1 = (f32[256,1024]{1,0:T(8,128)S(1)}, bf16[256,1024]{1,0:T(8,128)(2,1)S(1)}, f32[1,256]{1,0:T(1,128)S(1)}) custom-call(s32[1]{0:T(128)} %bitcast.place, bf16[256,1024]{1,0:T(8,128)(2,1)S(1)} %copy-done.6, bf16[256,1024]{1,0:T(8,128)(2,1)S(1)} %copy-done.14, f32[128,128]{1,0:T(8,128)S(1)} %get-tuple-element.17.rates, f32[16,1024]{1,0:T(8,128)S(1)} %bitcast.5, ...), custom_call_target="tpu_custom_call" | custom-call | flops 1200000000 | bytes 2400000 | tf_op jit(solution)/shard_map/forward_mix/pallas_call | solution.py:217
  52.5 6.2 %collective-permute-start.12 = (bf16[256,1024]{1,0:T(8,128)(2,1)}, bf16[256,1024]{1,0:T(8,128)(2,1)S(1)}, u32[]{:S(2)}, u32[]{:S(2)}) collective-permute-start(bf16[256,1024]{1,0:T(8,128)(2,1)} %collective-permute-done.11.q1), channel_id=1, source_target_pairs={{0,124},{4,0},{8,4},{12,8},{16,12},{20,16},{24,20},{28,24},{32,28}... | collective-permute-start | bytes 1572872 | tf_op jit(solution)/shard_map/ppermute | solution.py:40
  58.8 4.8 %collective-permute-done.1.keys_2.k2 = bf16[256,1024]{1,0:T(8,128)(2,1)S(1)} collective-permute-done((bf16[256,1024]{1,0:T(8,128)(2,1)}, bf16[256,1024]{1,0:T(8,128)(2,1)S(1)}, u32[]{:S(2)}, u32[]{:S(2)}) %collective-permute-start.1) | collective-permute-done | bytes 524320 | tf_op jit(solution)/shard_map/ppermute | solution.py:40
  63.6 3.1 %row_totals.1.t0.totals = f32[8,256]{1,0:T(8,128)S(1)} custom-call(s32[1]{0:T(128)} %bitcast.place, bf16[256,1024]{1,0:T(8,128)(2,1)S(1)} %copy-done.7, bf16[256,1024]{1,0:T(8,128)(2,1)S(1)} %copy-done.11, bf16[256,1024]{1,0:T(8,128)(2,1)} %collective-permute-done.keys_1.k1, bf16[256,1024]{1,0:T(8,128)(2,1)S(1)} %collective-permute-done.1.keys_2.k2), custom_call_target="tpu_custom_call" | custom-call | flops 1200000000 | bytes 2400000 | tf_op jit(solution)/shard_map/row_totals/pallas_call | solution.py:355
  67.0 2.4 %collective-permute-done.9.v1 = bf16[256,1024]{1,0:T(8,128)(2,1)} collective-permute-done((bf16[256,1024]{1,0:T(8,128)(2,1)S(1)}, bf16[256,1024]{1,0:T(8,128)(2,1)}, u32[]{:S(2)}, u32[]{:S(2)}) %collective-permute-start.9) | collective-permute-done | bytes 524320 | tf_op jit(solution)/shard_map/ppermute | solution.py:40
  69.3 3.6 %collective-permute-start.18 = (f32[1,256]{1,0:T(1,128)S(1)}, f32[1,256]{1,0:T(1,128)S(1)}, u32[]{:S(2)}, u32[]{:S(2)}) collective-permute-start(f32[1,256]{1,0:T(1,128)S(1)} %get-tuple-element.22.s0), channel_id=1, source_target_pairs={{0,8},{4,12},{8,16},{12,20},{16,24},{20,28},{24,32},{28,36},{32,40... | collective-permute-start | bytes 3080 | tf_op jit(solution)/shard_map/ppermute | solution.py:40
  73.0 1.6 %collective-permute-done.14.d2 = bf16[256,1024]{1,0:T(8,128)(2,1)S(1)} collective-permute-done((bf16[256,1024]{1,0:T(8,128)(2,1)}, bf16[256,1024]{1,0:T(8,128)(2,1)S(1)}, u32[]{:S(2)}, u32[]{:S(2)}) %collective-permute-start.14) | collective-permute-done | bytes 524320 | tf_op jit(solution)/shard_map/ppermute | solution.py:40
  74.5 2.7 %collective-permute-done.17.s1 = f32[1,256]{1,0:T(1,128)S(1)} collective-permute-done((f32[1,256]{1,0:T(1,128)S(1)}, f32[1,256]{1,0:T(1,128)S(1)}, u32[]{:S(2)}, u32[]{:S(2)}) %collective-permute-start.17) | collective-permute-done | bytes 1056 | tf_op jit(solution)/shard_map/ppermute | solution.py:40
  77.5 5.1 %value_grads.1 = (f32[256,1024]{1,0:T(8,128)S(1)}, f32[4,256]{1,0:T(4,128)S(1)}) custom-call(s32[1]{0:T(128)} %bitcast.place, bf16[256,1024]{1,0:T(8,128)(2,1)S(1)} %copy-done.11, bf16[256,1024]{1,0:T(8,128)(2,1)S(1)} %copy-done.8, bf16[256,1024]{1,0:T(8,128)(2,1)} %collective-permute-done.11.q1, bf16[256,1024]{1,0:T(8,128)(2,1)S(1)} %collective-permute-done.12.q2, ...), custom_call_target="tpu_custom_call" | custom-call | flops 2100000000 | bytes 4200000 | tf_op jit(solution)/shard_map/value_grads/pallas_call | solution.py:355
  82.7 7.6 %psum.7.stats.squares = f32[4,256]{1,0:T(4,128)S(1)} all-reduce(f32[4,256]{1,0:T(4,128)S(1)} %get-tuple-element.23), channel_id=1, replica_groups=mesh['ctx'=32,'tp'=4] {'tp'}, use_global_device_ids=true, to_apply=%region_0.1 | all-reduce | flops 1024 | bytes 8192 | tf_op jit(solution)/shard_map/psum | solution.py:565
  90.2 1.6 %backward_state.1 = (f32[128,128]{1,0:T(8,128)S(1)}, f32[2048,128]{1,0:T(8,128)S(1)}) custom-call(f32[256,1024]{1,0:T(8,128)S(1)} %get-tuple-element.27.scaled, f32[256,1024]{1,0:T(8,128)S(1)} %get-tuple-element.20.mixed, bf16[256,1024]{1,0:T(8,128)(2,1)S(1)} %copy-done, f32[4,256]{1,0:T(4,128)S(1)} %psum.7.stats.squares, f32[128,128]{1,0:T(8,128)S(1)} %get-tuple-element.17.rates), custom_call_target="tpu_custom_call" | custom-call | flops 600000000 | bytes 1200000 | tf_op jit(solution)/shard_map/backward_state/pallas_call | solution.py:262
  92.9 2.7 %collective-permute-start.22 = (f32[128,128]{1,0:T(8,128)S(1)}, f32[128,128]{1,0:T(8,128)S(1)}, u32[]{:S(2)}, u32[]{:S(2)}) collective-permute-start(f32[128,128]{1,0:T(8,128)S(1)} %get-tuple-element.29), channel_id=1, source_target_pairs={{0,8},{4,12},{8,0},{12,4},{16,24},{20,28},{24,16},{28,20},{32,40},... | collective-permute-start | bytes 196616 | tf_op jit(solution)/shard_map/ppermute | solution.py:50
  95.6 1.6 %collective-permute-done.21 = f32[128,128]{1,0:T(8,128)S(1)} collective-permute-done((f32[128,128]{1,0:T(8,128)S(1)}, f32[128,128]{1,0:T(8,128)S(1)}, u32[]{:S(2)}, u32[]{:S(2)}) %collective-permute-start.21) | collective-permute-done | bytes 65568 | tf_op jit(solution)/shard_map/ppermute | solution.py:50
  97.2 1.7 %collective-permute-done.22 = f32[128,128]{1,0:T(8,128)S(1)} collective-permute-done((f32[128,128]{1,0:T(8,128)S(1)}, f32[128,128]{1,0:T(8,128)S(1)}, u32[]{:S(2)}, u32[]{:S(2)}) %collective-permute-start.22) | collective-permute-done | bytes 65568 | tf_op jit(solution)/shard_map/ppermute | solution.py:50
  98.9 2.2 %collective-permute-done.23 = f32[128,128]{1,0:T(8,128)S(1)} collective-permute-done((f32[128,128]{1,0:T(8,128)S(1)}, f32[128,128]{1,0:T(8,128)S(1)}, u32[]{:S(2)}, u32[]{:S(2)}) %collective-permute-start.23) | collective-permute-done | bytes 65568 | tf_op jit(solution)/shard_map/ppermute | solution.py:50
  101.8 9.8 %attend.1 = (bf16[256,1024]{1,0:T(8,128)(2,1)}, bf16[256,1024]{1,0:T(8,128)(2,1)}, f32[8,256]{1,0:T(8,128)}) custom-call(s32[1]{0:T(128)} %bitcast.place, bf16[256,1024]{1,0:T(8,128)(2,1)} %q0.3, bf16[256,1024]{1,0:T(8,128)(2,1)} %d0.3, bf16[256,1024]{1,0:T(8,128)(2,1)} %keys.5, bf16[256,1024]{1,0:T(8,128)(2,1)} %collective-permute-done.keys_1.k1, ...), custom_call_target="tpu_custom_call" | custom-call | flops 3000000000 | bytes 6000000 | tf_op jit(solution)/shard_map/attend/pallas_call | solution.py:355
  111.6 2.5 %collective-permute-start.19 = (f32[8,256]{1,0:T(8,128)}, f32[8,256]{1,0:T(8,128)S(1)}, u32[]{:S(2)}, u32[]{:S(2)}) collective-permute-start(f32[8,256]{1,0:T(8,128)} %get-tuple-element.26.e0), channel_id=1, source_target_pairs={{0,124},{4,0},{8,4},{12,8},{16,12},{20,16},{24,20},{28,24},{32,28}... | collective-permute-start | bytes 24584 | tf_op jit(solution)/shard_map/ppermute | solution.py:40
  116.5 1.5 %collective-permute-start.26 = (f32[128,128]{1,0:T(8,128)S(1)}, f32[128,128]{1,0:T(8,128)S(1)}, u32[]{:S(2)}, u32[]{:S(2)}) collective-permute-start(f32[128,128]{1,0:T(8,128)S(1)} %get-tuple-element.30), channel_id=1, source_target_pairs={{0,64},{4,68},{8,72},{12,76},{16,80},{20,84},{24,88},{28,92},{32,9... | collective-permute-start | bytes 196616 | tf_op jit(solution)/shard_map/ppermute | solution.py:50
  118.0 1.5 %collective-permute-done.20.e2 = f32[8,256]{1,0:T(8,128)S(1)} collective-permute-done((f32[8,256]{1,0:T(8,128)}, f32[8,256]{1,0:T(8,128)S(1)}, u32[]{:S(2)}, u32[]{:S(2)}) %collective-permute-start.20) | collective-permute-done | bytes 8224 | tf_op jit(solution)/shard_map/ppermute | solution.py:40
  120.3 6.2 %key_grads.1 = bf16[256,1024]{1,0:T(8,128)(2,1)} custom-call(s32[1]{0:T(128)} %bitcast.place, bf16[256,1024]{1,0:T(8,128)(2,1)S(1)} %copy-done.12, bf16[256,1024]{1,0:T(8,128)(2,1)S(1)} %copy-done.17, bf16[256,1024]{1,0:T(8,128)(2,1)S(1)} %copy-done.9, bf16[256,1024]{1,0:T(8,128)(2,1)} %collective-permute-done.11.q1, bf16[256,1024]{1,0:T(8,128)(2,1)S(1)} %copy-done.19, ...), custom_call_target="tpu_custom_call" | custom-call | flops 2400000000 | bytes 4800000 | tf_op jit(solution)/shard_map/key_grads/pallas_call | solution.py:355
  126.5 3.4 %backward_mix.1 = bf16[256,1024]{1,0:T(8,128)(2,1)} custom-call(s32[1]{0:T(128)} %bitcast.place, f32[2048,128]{1,0:T(8,128)S(1)} %copy-done.4, f32[128,128]{1,0:T(8,128)S(1)} %get-tuple-element.17.rates, f32[16,1024]{1,0:T(8,128)S(1)} %bitcast.6, f32[128,128]{1,0:T(8,128)S(1)} %get-tuple-element.31.start, f32[128,128]{1,0:T(8,128)S(1)} %collective-permute-done.25.p1, ...), custom_call_target="tpu_custom_call" | custom-call | flops 1200000000 | bytes 2400000 | tf_op jit(solution)/shard_map/backward_mix/pallas_call | solution.py:290
  (95 shorter events, 14.1 us)
Async XLA Ops:
  3.6 44.8 %copy-start.24 = (f32[1024,16]{0,1:T(8,128)S(1)}, f32[1024,16]{0,1:T(8,128)}, u32[]{:S(2)}) copy-start(f32[1024,16]{0,1:T(8,128)} %param.12) | copy-start | bytes 196612
  5.1 7.7 %collective-permute-start.2 = (f32[128,128]{1,0:T(8,128)S(1)}, f32[128,128]{1,0:T(8,128)S(1)}, u32[]{:S(2)}, u32[]{:S(2)}) collective-permute-start(f32[128,128]{1,0:T(8,128)S(1)} %get-tuple-element.18), channel_id=1, source_target_pairs={{0,4},{4,8},{8,12},{12,0},{16,20},{20,24},{24,28},{28,16},{32,36},... | collective-permute-start | bytes 196616 | tf_op jit(solution)/shard_map/ppermute | solution.py:50
  7.2 7.7 %collective-permute-start.3 = (f32[128,128]{1,0:T(8,128)S(1)}, f32[128,128]{1,0:T(8,128)S(1)}, u32[]{:S(2)}, u32[]{:S(2)}) collective-permute-start(f32[128,128]{1,0:T(8,128)S(1)} %get-tuple-element.18), channel_id=1, source_target_pairs={{0,8},{4,12},{8,0},{12,4},{16,24},{20,28},{24,16},{28,20},{32,40},... | collective-permute-start | bytes 196616 | tf_op jit(solution)/shard_map/ppermute | solution.py:50
  10.7 4.3 %collective-permute-start.4 = (f32[128,128]{1,0:T(8,128)S(1)}, f32[128,128]{1,0:T(8,128)S(1)}, u32[]{:S(2)}, u32[]{:S(2)}) collective-permute-start(f32[128,128]{1,0:T(8,128)S(1)} %get-tuple-element.18), channel_id=1, source_target_pairs={{0,12},{4,0},{8,4},{12,8},{16,28},{20,16},{24,20},{28,24},{32,44},... | collective-permute-start | bytes 196616 | tf_op jit(solution)/shard_map/ppermute | solution.py:50
  11.7 32.7 %collective-permute-start = (bf16[256,1024]{1,0:T(8,128)(2,1)S(1)}, bf16[256,1024]{1,0:T(8,128)(2,1)}, u32[]{:S(2)}, u32[]{:S(2)}) collective-permute-start(bf16[256,1024]{1,0:T(8,128)(2,1)S(1)} %copy-done.10), channel_id=1, source_target_pairs={{0,4},{4,8},{8,12},{12,16},{16,20},{20,24},{24,28},{28,32},{32,36}... | collective-permute-start | bytes 1572872 | tf_op jit(solution)/shard_map/ppermute | solution.py:40
  12.8 35.6 %copy-start.28 = (f32[1024]{0:T(1024)S(1)}, f32[1024]{0:T(1024)}, u32[]{:S(2)}) copy-start(f32[1024]{0:T(1024)} %param.14) | copy-start | bytes 12292
  12.8 35.6 %copy-start = (bf16[256,1024]{1,0:T(8,128)(2,1)S(1)}, bf16[256,1024]{1,0:T(8,128)(2,1)}, u32[]{:S(2)}) copy-start(bf16[256,1024]{1,0:T(8,128)(2,1)} %gate_out.3) | copy-start | bytes 1572868
  12.8 35.6 %copy-start.6 = (bf16[256,1024]{1,0:T(8,128)(2,1)S(1)}, bf16[256,1024]{1,0:T(8,128)(2,1)}, u32[]{:S(2)}) copy-start(bf16[256,1024]{1,0:T(8,128)(2,1)} %mixer.3) | copy-start | bytes 1572868
  15.1 23.4 %collective-permute-start.5 = (f32[128,128]{1,0:T(8,128)S(1)}, f32[128,128]{1,0:T(8,128)S(1)}, u32[]{:S(2)}, u32[]{:S(2)}) collective-permute-start(f32[128,128]{1,0:T(8,128)S(1)} %multiply_add_fusion.3), channel_id=1, source_target_pairs={{0,16},{4,20},{8,24},{12,28},{16,0},{20,4},{24,8},{28,12},{32,48},... | collective-permute-start | bytes 196616 | tf_op jit(solution)/shard_map/ppermute | solution.py:50
  16.7 35.8 %collective-permute-start.11 = (bf16[256,1024]{1,0:T(8,128)(2,1)S(1)}, bf16[256,1024]{1,0:T(8,128)(2,1)}, u32[]{:S(2)}, u32[]{:S(2)}) collective-permute-start(bf16[256,1024]{1,0:T(8,128)(2,1)S(1)} %copy-done.7), channel_id=1, source_target_pairs={{0,124},{4,0},{8,4},{12,8},{16,12},{20,16},{24,20},{28,24},{32,28}... | collective-permute-start | bytes 1572872 | tf_op jit(solution)/shard_map/ppermute | solution.py:40
  21.0 37.7 %collective-permute-start.13 = (bf16[256,1024]{1,0:T(8,128)(2,1)}, bf16[256,1024]{1,0:T(8,128)(2,1)}, u32[]{:S(2)}, u32[]{:S(2)}) collective-permute-start(bf16[256,1024]{1,0:T(8,128)(2,1)} %d0.3), channel_id=1, source_target_pairs={{0,124},{4,0},{8,4},{12,8},{16,12},{20,16},{24,20},{28,24},{32,28}... | collective-permute-start | bytes 1572872 | tf_op jit(solution)/shard_map/ppermute | solution.py:40
  38.5 5.5 %collective-permute-start.6 = (f32[128,128]{1,0:T(8,128)S(1)}, f32[128,128]{1,0:T(8,128)S(1)}, u32[]{:S(2)}, u32[]{:S(2)}) collective-permute-start(f32[128,128]{1,0:T(8,128)S(1)} %get-tuple-element.32), channel_id=1, source_target_pairs={{0,32},{4,36},{8,40},{12,44},{16,48},{20,52},{24,56},{28,60},{32,6... | collective-permute-start | bytes 196616 | tf_op jit(solution)/shard_map/ppermute | solution.py:50
  40.1 5.8 %collective-permute-start.7 = (f32[128,128]{1,0:T(8,128)S(1)}, f32[128,128]{1,0:T(8,128)S(1)}, u32[]{:S(2)}, u32[]{:S(2)}) collective-permute-start(f32[128,128]{1,0:T(8,128)S(1)} %get-tuple-element.32), channel_id=1, source_target_pairs={{0,64},{4,68},{8,72},{12,76},{16,80},{20,84},{24,88},{28,92},{32,9... | collective-permute-start | bytes 196616 | tf_op jit(solution)/shard_map/ppermute | solution.py:50
  44.1 4.3 %collective-permute-start.8 = (f32[128,128]{1,0:T(8,128)S(1)}, f32[128,128]{1,0:T(8,128)S(1)}, u32[]{:S(2)}, u32[]{:S(2)}) collective-permute-start(f32[128,128]{1,0:T(8,128)S(1)} %get-tuple-element.32), channel_id=1, source_target_pairs={{0,96},{4,100},{8,104},{12,108},{16,112},{20,116},{24,120},{28,124... | collective-permute-start | bytes 196616 | tf_op jit(solution)/shard_map/ppermute | solution.py:50
  44.4 19.2 %collective-permute-start.1 = (bf16[256,1024]{1,0:T(8,128)(2,1)}, bf16[256,1024]{1,0:T(8,128)(2,1)S(1)}, u32[]{:S(2)}, u32[]{:S(2)}) collective-permute-start(bf16[256,1024]{1,0:T(8,128)(2,1)} %collective-permute-done.keys_1.k1), channel_id=1, source_target_pairs={{0,4},{4,8},{8,12},{12,16},{16,20},{20,24},{24,28},{28,32},{32,36}... | collective-permute-start | bytes 1572872 | tf_op jit(solution)/shard_map/ppermute | solution.py:40
  52.5 16.9 %collective-permute-start.9 = (bf16[256,1024]{1,0:T(8,128)(2,1)S(1)}, bf16[256,1024]{1,0:T(8,128)(2,1)}, u32[]{:S(2)}, u32[]{:S(2)}) collective-permute-start(bf16[256,1024]{1,0:T(8,128)(2,1)S(1)} %get-tuple-element.19.v0.values), channel_id=1, source_target_pairs={{0,4},{4,8},{8,12},{12,16},{16,20},{20,24},{24,28},{28,32},{32,36}... | collective-permute-start | bytes 1572872 | tf_op jit(solution)/shard_map/ppermute | solution.py:40
  52.5 16.8 %collective-permute-start.12 = (bf16[256,1024]{1,0:T(8,128)(2,1)}, bf16[256,1024]{1,0:T(8,128)(2,1)S(1)}, u32[]{:S(2)}, u32[]{:S(2)}) collective-permute-start(bf16[256,1024]{1,0:T(8,128)(2,1)} %collective-permute-done.11.q1), channel_id=1, source_target_pairs={{0,124},{4,0},{8,4},{12,8},{16,12},{20,16},{24,20},{28,24},{32,28}... | collective-permute-start | bytes 1572872 | tf_op jit(solution)/shard_map/ppermute | solution.py:40
  58.7 15.8 %collective-permute-start.14 = (bf16[256,1024]{1,0:T(8,128)(2,1)}, bf16[256,1024]{1,0:T(8,128)(2,1)S(1)}, u32[]{:S(2)}, u32[]{:S(2)}) collective-permute-start(bf16[256,1024]{1,0:T(8,128)(2,1)} %collective-permute-done.13.d1), channel_id=1, source_target_pairs={{0,124},{4,0},{8,4},{12,8},{16,12},{20,16},{24,20},{28,24},{32,28}... | collective-permute-start | bytes 1572872 | tf_op jit(solution)/shard_map/ppermute | solution.py:40
  66.7 10.8 %collective-permute-start.15 = (f32[8,256]{1,0:T(8,128)S(1)}, f32[8,256]{1,0:T(8,128)S(1)}, u32[]{:S(2)}, u32[]{:S(2)}) collective-permute-start(f32[8,256]{1,0:T(8,128)S(1)} %row_totals.1.t0.totals), channel_id=1, source_target_pairs={{0,124},{4,0},{8,4},{12,8},{16,12},{20,16},{24,20},{28,24},{32,28}... | collective-permute-start | bytes 24584 | tf_op jit(solution)/shard_map/ppermute | solution.py:40
  66.8 10.7 %collective-permute-start.16 = (f32[8,256]{1,0:T(8,128)S(1)}, f32[8,256]{1,0:T(8,128)S(1)}, u32[]{:S(2)}, u32[]{:S(2)}) collective-permute-start(f32[8,256]{1,0:T(8,128)S(1)} %row_totals.1.t0.totals), channel_id=1, source_target_pairs={{0,120},{4,124},{8,0},{12,4},{16,8},{20,12},{24,16},{28,20},{32,24... | collective-permute-start | bytes 24584 | tf_op jit(solution)/shard_map/ppermute | solution.py:40
  69.3 7.9 %collective-permute-start.17 = (f32[1,256]{1,0:T(1,128)S(1)}, f32[1,256]{1,0:T(1,128)S(1)}, u32[]{:S(2)}, u32[]{:S(2)}) collective-permute-start(f32[1,256]{1,0:T(1,128)S(1)} %get-tuple-element.22.s0), channel_id=1, source_target_pairs={{0,4},{4,8},{8,12},{12,16},{16,20},{20,24},{24,28},{28,32},{32,36}... | collective-permute-start | bytes 3080 | tf_op jit(solution)/shard_map/ppermute | solution.py:40
  69.3 8.2 %collective-permute-start.18 = (f32[1,256]{1,0:T(1,128)S(1)}, f32[1,256]{1,0:T(1,128)S(1)}, u32[]{:S(2)}, u32[]{:S(2)}) collective-permute-start(f32[1,256]{1,0:T(1,128)S(1)} %get-tuple-element.22.s0), channel_id=1, source_target_pairs={{0,8},{4,12},{8,16},{12,20},{16,24},{20,28},{24,32},{28,36},{32,40... | collective-permute-start | bytes 3080 | tf_op jit(solution)/shard_map/ppermute | solution.py:40
  74.5 27.2 %collective-permute-start.10 = (bf16[256,1024]{1,0:T(8,128)(2,1)}, bf16[256,1024]{1,0:T(8,128)(2,1)}, u32[]{:S(2)}, u32[]{:S(2)}) collective-permute-start(bf16[256,1024]{1,0:T(8,128)(2,1)} %collective-permute-done.9.v1), channel_id=1, source_target_pairs={{0,4},{4,8},{8,12},{12,16},{16,20},{20,24},{24,28},{28,32},{32,36}... | collective-permute-start | bytes 1572872 | tf_op jit(solution)/shard_map/ppermute | solution.py:40
  92.9 4.3 %collective-permute-start.21 = (f32[128,128]{1,0:T(8,128)S(1)}, f32[128,128]{1,0:T(8,128)S(1)}, u32[]{:S(2)}, u32[]{:S(2)}) collective-permute-start(f32[128,128]{1,0:T(8,128)S(1)} %get-tuple-element.29), channel_id=1, source_target_pairs={{0,12},{4,0},{8,4},{12,8},{16,28},{20,16},{24,20},{28,24},{32,44},... | collective-permute-start | bytes 196616 | tf_op jit(solution)/shard_map/ppermute | solution.py:50
  92.9 6.0 %collective-permute-start.22 = (f32[128,128]{1,0:T(8,128)S(1)}, f32[128,128]{1,0:T(8,128)S(1)}, u32[]{:S(2)}, u32[]{:S(2)}) collective-permute-start(f32[128,128]{1,0:T(8,128)S(1)} %get-tuple-element.29), channel_id=1, source_target_pairs={{0,8},{4,12},{8,0},{12,4},{16,24},{20,28},{24,16},{28,20},{32,40},... | collective-permute-start | bytes 196616 | tf_op jit(solution)/shard_map/ppermute | solution.py:50
  95.6 5.5 %collective-permute-start.23 = (f32[128,128]{1,0:T(8,128)S(1)}, f32[128,128]{1,0:T(8,128)S(1)}, u32[]{:S(2)}, u32[]{:S(2)}) collective-permute-start(f32[128,128]{1,0:T(8,128)S(1)} %get-tuple-element.29), channel_id=1, source_target_pairs={{0,4},{4,8},{8,12},{12,0},{16,20},{20,24},{24,28},{28,16},{32,36},... | collective-permute-start | bytes 196616 | tf_op jit(solution)/shard_map/ppermute | solution.py:50
  101.1 14.5 %collective-permute-start.24 = (f32[128,128]{1,0:T(8,128)S(1)}, f32[128,128]{1,0:T(8,128)S(1)}, u32[]{:S(2)}, u32[]{:S(2)}) collective-permute-start(f32[128,128]{1,0:T(8,128)S(1)} %multiply_add_fusion.1), channel_id=1, source_target_pairs={{0,16},{4,20},{8,24},{12,28},{16,0},{20,4},{24,8},{28,12},{32,48},... | collective-permute-start | bytes 196616 | tf_op jit(solution)/shard_map/ppermute | solution.py:50
  111.6 6.4 %collective-permute-start.19 = (f32[8,256]{1,0:T(8,128)}, f32[8,256]{1,0:T(8,128)S(1)}, u32[]{:S(2)}, u32[]{:S(2)}) collective-permute-start(f32[8,256]{1,0:T(8,128)} %get-tuple-element.26.e0), channel_id=1, source_target_pairs={{0,124},{4,0},{8,4},{12,8},{16,12},{20,16},{24,20},{28,24},{32,28}... | collective-permute-start | bytes 24584 | tf_op jit(solution)/shard_map/ppermute | solution.py:40
  114.2 5.4 %collective-permute-start.20 = (f32[8,256]{1,0:T(8,128)}, f32[8,256]{1,0:T(8,128)S(1)}, u32[]{:S(2)}, u32[]{:S(2)}) collective-permute-start(f32[8,256]{1,0:T(8,128)} %get-tuple-element.26.e0), channel_id=1, source_target_pairs={{0,120},{4,124},{8,0},{12,4},{16,8},{20,12},{24,16},{28,20},{32,24... | collective-permute-start | bytes 24584 | tf_op jit(solution)/shard_map/ppermute | solution.py:40
  115.7 10.8 %collective-permute-start.25 = (f32[128,128]{1,0:T(8,128)S(1)}, f32[128,128]{1,0:T(8,128)S(1)}, u32[]{:S(2)}, u32[]{:S(2)}) collective-permute-start(f32[128,128]{1,0:T(8,128)S(1)} %get-tuple-element.30), channel_id=1, source_target_pairs={{0,96},{4,100},{8,104},{12,108},{16,112},{20,116},{24,120},{28,124... | collective-permute-start | bytes 196616 | tf_op jit(solution)/shard_map/ppermute | solution.py:50
  116.5 10.0 %collective-permute-start.26 = (f32[128,128]{1,0:T(8,128)S(1)}, f32[128,128]{1,0:T(8,128)S(1)}, u32[]{:S(2)}, u32[]{:S(2)}) collective-permute-start(f32[128,128]{1,0:T(8,128)S(1)} %get-tuple-element.30), channel_id=1, source_target_pairs={{0,64},{4,68},{8,72},{12,76},{16,80},{20,84},{24,88},{28,92},{32,9... | collective-permute-start | bytes 196616 | tf_op jit(solution)/shard_map/ppermute | solution.py:50
  118.0 8.5 %collective-permute-start.27 = (f32[128,128]{1,0:T(8,128)S(1)}, f32[128,128]{1,0:T(8,128)S(1)}, u32[]{:S(2)}, u32[]{:S(2)}) collective-permute-start(f32[128,128]{1,0:T(8,128)S(1)} %get-tuple-element.30), channel_id=1, source_target_pairs={{0,32},{4,36},{8,40},{12,44},{16,48},{20,52},{24,56},{28,60},{32,6... | collective-permute-start | bytes 196616 | tf_op jit(solution)/shard_map/ppermute | solution.py:50
  (25 other events, 248.8 us)
